TPU v7x, 32 devices: a whole 2x2x4 slice. The times are simulated.
32 devices in a mesh: groups: 2 (over y), seq: 8 (over z, x), chan: 1, section: 2 (over core).
Axes of the slice: x: 2, y: 2, z: 4, core: 2. Of those that a mesh axis runs over, the one named last changes fastest.
Arguments:
- queries: bfloat16 [8192, 8192], P(('groups', 'seq', 'section'), 'chan'), parts along dimension 0, may hold values from -6 to 6
- key_proj: bfloat16 [8192, 8192], P(('groups', 'seq', 'section'), 'chan'), parts along dimension 0, may hold values from -6 to 6
- value_proj: bfloat16 [8192, 8192], P(('groups', 'seq', 'section'), 'chan'), parts along dimension 0, may hold values from -6 to 6
- filter_taps: bfloat16 [512, 128], P('chan'), may hold values from -0.5 to 0.5
- skip_gain: float32 [8192], P('chan'), may hold values from -3 to 3
- out_weight: bfloat16 [8192, 4096], P('chan', ('seq', 'section')), may hold values from -0.09375 to 0.09375
- residual: bfloat16 [8192, 4096], P(('groups', 'seq', 'section'), 'chan'), parts along dimension 0, may hold values from -6 to 6
Outputs:
- layer_out: bfloat16 [8192, 4096], P(('groups', 'seq', 'section'), 'chan'), parts along dimension 0
There are 2 independent parts, one for each index of `groups`. A program takes and returns all parts, laid end to end along the dimension named above; an argument that names none is the same for every part. Nothing has to cross between parts.
All inputs are finite; a program needn't handle non-finite values.
Results may differ from a plain program's by a relative error of at most 0.0053.
Values may be sent and summed in bfloat16 or wider, within the bound.
No kernel may reach another device: no remote copies, remote signals or barrier semaphores. Data moves between devices by JAX's collectives and lax.ppermute only.
A program may use at most 256 MiB of HBM per device.

v0:
```python
import jax
import jax.numpy as jnp
from jax import lax
from jax.sharding import PartitionSpec as P


def shifted(value, axis, steps):
    count = lax.axis_size(axis)
    initial, last = (max(0, -steps), min(count, count - steps))
    return lax.ppermute(value, axis, [(source, source + steps) for source in range(initial, last)])


def filter_matrices(filter_taps):
    groups_here, block_len = filter_taps.shape
    pattern = jnp.concatenate(
        [
            jnp.zeros((groups_here, 1), filter_taps.dtype),
            filter_taps[:, ::-1],
            jnp.zeros((groups_here, block_len), filter_taps.dtype),
        ],
        axis=1,
    )
    tiled = jnp.tile(pattern, (1, block_len))[:, : block_len * 2 * block_len]
    both = tiled.reshape(groups_here, block_len, 2 * block_len)
    return (both[:, :, block_len:], both[:, :, :block_len])


def apply_blocks(matrix, blocks):
    return jnp.einsum("gij,bjgc->bigc", matrix, blocks, preferred_element_type=jnp.float32)


def body(queries, key_proj, value_proj, filter_taps, skip_gain, out_weight, residual):
    seq_len, channels = queries.shape
    groups_here, block_len = filter_taps.shape
    per_group = channels // groups_here
    block_count = seq_len // block_len
    product = (key_proj.astype(jnp.float32) * value_proj.astype(jnp.float32)).astype(jnp.bfloat16)
    blocks = product.reshape(block_count, block_len, groups_here, per_group)
    now_matrix, prev_matrix = filter_matrices(filter_taps)
    convolved = apply_blocks(now_matrix, blocks)
    carried = apply_blocks(prev_matrix, blocks)
    outgoing = carried[block_count - 1, : block_len - 1].reshape(block_len - 1, channels)
    incoming = shifted(outgoing, ("seq", "section"), 1)
    first = jnp.concatenate([incoming, jnp.zeros((1, channels), jnp.float32)], axis=0)
    first = first.reshape(1, block_len, groups_here, per_group)
    carried = jnp.concatenate([first, carried[: block_count - 1]], axis=0)
    convolved = (convolved + carried).reshape(seq_len, channels)
    gated = (
        queries.astype(jnp.float32) * (convolved + skip_gain[None, :] * product.astype(jnp.float32))
    ).astype(jnp.bfloat16)
    partial_out = jnp.dot(
        gated,
        lax.all_gather(out_weight, ("seq", "section"), axis=1, tiled=True),
        preferred_element_type=jnp.float32,
    )
    out_share = lax.psum_scatter(partial_out, "chan", scatter_dimension=1, tiled=True)
    return (residual.astype(jnp.float32) + out_share).astype(jnp.bfloat16)


def solution(mesh):
    return jax.shard_map(
        body,
        mesh=mesh,
        in_specs=(
            P(("groups", "seq", "section"), "chan"),
            P(("groups", "seq", "section"), "chan"),
            P(("groups", "seq", "section"), "chan"),
            P("chan", None),
            P("chan"),
            P("chan", ("seq", "section")),
            P(("groups", "seq", "section"), "chan"),
        ),
        out_specs=P(("groups", "seq", "section"), "chan"),
        check_vma=False,
    )
```

profile of v0, /device:TPU:0, one launch (start us, length us, event | category | flops | bytes accessed | tf_op | source)
XLA Modules:
  0.0 429.6 jit_solution(3508828686068066326)
XLA Ops:
  6.5 0.7 all-gather.2.cloned.1.call-update
  7.3 6.4 %copy.11 = bf16[256,8192]{0,1:T(8,128)(2,1)} copy(bf16[256,8192]{1,0:T(8,128)(2,1)} %param.8) | data formatting | bytes 8388608 | tf_op args[1]
  13.6 6.6 %copy.12 = bf16[256,8192]{0,1:T(8,128)(2,1)} copy(bf16[256,8192]{1,0:T(8,128)(2,1)} %param.9) | data formatting | bytes 8388608 | tf_op args[2]
  20.2 6.8 %multiply_convert_fusion = bf16[256,8192]{0,1:T(8,128)(2,1)} fusion(bf16[256,8192]{0,1:T(8,128)(2,1)} %copy.12, bf16[256,8192]{0,1:T(8,128)(2,1)} %copy.11), kind=kLoop, calls=%fused_computation.8 | loop fusion | flops 8388608 | bytes 12582912 | tf_op jit(solution)/shard_map/convert_element_type | solution.py:37
  27.0 7.0 %reshape.17 = bf16[2,128,512,16]{1,0,3,2:T(2,128)(2,1)} reshape(bf16[256,8192]{0,1:T(8,128)(2,1)} %multiply_convert_fusion) | data formatting | bytes 8388608 | tf_op jit(solution)/shard_map/reshape | solution.py:38
  34.0 0.4 rev.3
  34.4 0.1 maximum_maximum_fusion
  34.6 0.2 copy.13
  34.8 11.6 %tile.4 = bf16[512,128,257]{0,2,1:T(8,128)(2,1)} broadcast(bf16[512,257]{0,1:T(8,128)(2,1)S(1)} %copy.13), dimensions={0,2} | broadcast | bytes 33948672 | tf_op jit(solution)/shard_map/tile | solution.py:23
  46.4 30.7 %tile.10 = bf16[512,32896]{0,1:T(8,128)(2,1)} reshape(bf16[512,128,257]{0,2,1:T(8,128)(2,1)} %tile.4) | data formatting | bytes 67371008 | tf_op jit(solution)/shard_map/tile | solution.py:23
  77.0 23.3 %slice.20 = bf16[512,32768]{0,1:T(8,128)(2,1)} slice(bf16[512,32896]{0,1:T(8,128)(2,1)} %tile.10), slice={[0:512], [0:32768]} | slice | bytes 67108864 | tf_op jit(solution)/shard_map/slice | solution.py:23
  100.4 24.4 %fusion.20 = (bf16[512,128,128]{0,2,1:T(8,128)(2,1)}, bf16[512,128,128]{0,2,1:T(8,128)(2,1)}) fusion(bf16[512,128,256]{0,2,1:T(8,128)(2,1)} %bitcast.38), kind=kLoop, calls=%fused_computation.16 | loop fusion | bytes 67108864 | tf_op jit(solution)/shard_map/slice | solution.py:25
  124.8 23.7 %copy.22 = bf16[512,128,128]{2,1,0:T(8,128)(2,1)} copy(bf16[512,128,128]{0,2,1:T(8,128)(2,1)} %get-tuple-element.6) | data formatting | bytes 33554432
  148.5 15.3 %fusion.11 = f32[2,128,512,16]{1,3,0,2:T(8,128)} fusion(bf16[512,128,128]{2,1,0:T(8,128)(2,1)} %copy.22, bf16[2,128,512,16]{1,0,3,2:T(2,128)(2,1)} %reshape.17), kind=kOutput, calls=%fused_computation.14 | convolution fusion | flops 536870912 | bytes 29360128 | tf_op jit(solution)/shard_map/gij,bjgc->bigc/dot_general | solution.py:29
  163.8 4.9 %slice.23 = f32[1,127,512,16]{1,3,0,2:T(8,128)} slice(f32[2,128,512,16]{1,3,0,2:T(8,128)} %fusion.11), slice={[1:2], [0:127], [0:512], [0:16]} | slice | bytes 8323072 | tf_op jit(solution)/shard_map/slice | solution.py:42
  168.7 4.8 %collective-permute-start = (f32[127,8192]{0,1:T(8,128)}, f32[127,8192]{0,1:T(8,128)}, u32[]{:S(2)}, u32[]{:S(2)}) collective-permute-start(f32[127,8192]{0,1:T(8,128)} %bitcast.7), channel_id=1, source_target_pairs={{0,1},{1,2},{2,3},{3,4},{4,5},{5,6},{6,7},{7,8},{8,9},{9,10},{10,1... | collective-permute-start | bytes 12484616 | tf_op jit(solution)/shard_map/ppermute | solution.py:10
  173.5 2.5 slice.24
  175.9 23.7 %copy.21 = bf16[512,128,128]{2,1,0:T(8,128)(2,1)} copy(bf16[512,128,128]{0,2,1:T(8,128)(2,1)} %get-tuple-element.5) | data formatting | bytes 33554432
  199.6 6.4 %copy.10 = bf16[256,8192]{0,1:T(8,128)(2,1)} copy(bf16[256,8192]{1,0:T(8,128)(2,1)} %param.7) | data formatting | bytes 8388608 | tf_op args[0]
  206.0 5.0 %concatenate.10 = f32[128,8192]{0,1:T(8,128)} pad(f32[127,8192]{0,1:T(8,128)} %collective-permute-done, f32[]{:T(128)} %constant.0.clone.1), padding=0_1x0_0 | pad | bytes 8355844 | tf_op jit(solution)/shard_map/concatenate | solution.py:44
  211.1 16.4 %maximum_add_fusion = f32[2,128,512,16]{1,3,0,2:T(8,128)} fusion(f32[1,128,512,16]{1,3,0,2:T(8,128)} %slice.24, f32[1,128,512,16]{1,3,0,2:T(8,128)} %bitcast.40, bf16[512,128,128]{2,1,0:T(8,128)(2,1)} %copy.21, bf16[2,128,512,16]{1,0,3,2:T(2,128)(2,1)} %reshape.17), kind=kOutput, calls=%fused_computation.7 | convolution fusion | flops 541065216 | bytes 37748736 | tf_op jit(solution)/shard_map/gij,bjgc->bigc/dot_general | solution.py:29
  227.5 13.4 %copy.17 = f32[2,128,512,16]{1,0,3,2:T(2,128)} copy(f32[2,128,512,16]{1,3,0,2:T(8,128)} %maximum_add_fusion) | data formatting | bytes 16777216 | tf_op jit(solution)/shard_map/add | solution.py:47
  240.9 150.1 %all-gather.2.cloned.1.call-done = bf16[8192,4096]{1,0:T(8,128)(2,1)} async-done(((bf16[8192,256]{1,0:T(8,128)(2,1)}), bf16[8192,4096]{1,0:T(8,128)(2,1)}) %all-gather.2.cloned.1.call-update) | async-done | bytes 67108880 | tf_op jit(solution)/shard_map/all_gather | solution.py:53
  390.9 31.8 %fusion.6 = bf16[256,4096]{1,0:T(8,128)(2,1)} fusion(bf16[8192,4096]{1,0:T(8,128)(2,1)} %all-gather.2.cloned.1.call-done, f32[1024,8,2,128]{3,2,1,0:T(2,128)} %bitcast.39, bf16[256,8192]{0,1:T(8,128)(2,1)} %multiply_convert_fusion, bf16[256,8192]{0,1:T(8,128)(2,1)} %copy.10, f32[8192]{0:T(1024)S(1)} %copy-done.3, bf16[256,4096]{1,0:T(8,128)(2,1)S(1)} %copy-done.1), kind=kOutput, calls=%fused_computation.10 | convolution fusion | flops 17195597824 | bytes 88113152 | tf_op jit(solution)/shard_map/dot_general | solution.py:51
  (13 shorter events, 0.1 us)
Async XLA Ops:
  6.5 384.4 %all-gather.2.cloned.1.call-start = ((), (), s32[]{:S(2)}) async-start(), calls=%async_computation | async-start | bytes 71303168 | tf_op jit(solution)/shard_map/all_gather | solution.py:53
  20.2 13.8 %copy-start.2 = (bf16[512,128]{1,0:T(8,128)(2,1)S(1)}, bf16[512,128]{1,0:T(8,128)(2,1)}, u32[]{:S(2)}) copy-start(bf16[512,128]{1,0:T(8,128)(2,1)} %param.10) | copy-start | bytes 393220
  163.8 9.7 %copy-start = (f32[2,128,512,16]{1,3,0,2:T(8,128)S(1)}, f32[2,128,512,16]{1,3,0,2:T(8,128)}, u32[]{:S(2)}) copy-start(f32[2,128,512,16]{1,3,0,2:T(8,128)} %fusion.11) | copy-start | bytes 25165828
  168.7 37.4 %collective-permute-start = (f32[127,8192]{0,1:T(8,128)}, f32[127,8192]{0,1:T(8,128)}, u32[]{:S(2)}, u32[]{:S(2)}) collective-permute-start(f32[127,8192]{0,1:T(8,128)} %bitcast.7), channel_id=1, source_target_pairs={{0,1},{1,2},{2,3},{3,4},{4,5},{5,6},{6,7},{7,8},{8,9},{9,10},{10,1... | collective-permute-start | bytes 12484616 | tf_op jit(solution)/shard_map/ppermute | solution.py:10
  227.5 163.4 %copy-start.1 = (bf16[256,4096]{1,0:T(8,128)(2,1)S(1)}, bf16[256,4096]{1,0:T(8,128)(2,1)}, u32[]{:S(2)}) copy-start(bf16[256,4096]{1,0:T(8,128)(2,1)} %param.13) | copy-start | bytes 6291460
  227.5 163.4 %copy-start.3 = (f32[8192]{0:T(1024)S(1)}, f32[8192]{0:T(1024)}, u32[]{:S(2)}) copy-start(f32[8192]{0:T(1024)} %param.11) | copy-start | bytes 98308
Sparse Core Ops, SparseCore 0:
  8.9 382.0 all-gather.1
where the time goes:
time: 432 us; the launch traced here: 430 us
  local copies, waits for them, and re-layouts  190 us (44%)
  waiting for transfers between devices  151 us (35%)
  matrix products  63.5 us (15%)
  between operations  13.4 us (3%)
  other arithmetic  6.9 us (2%)
  starting transfers between devices  4.79 us (1%)
    all_gather x1, waiting for transfers between devices, body(): lax.all_gather(out_weight, ('seq', 'section'), axis=1, tiled=True)  150 us
    unnamed x13, local copies, waits for them, and re-layouts  66.8 us
    another operation x2, local copies, waits for them, and re-layouts, filter_matrices(): tiled = jnp.tile(pattern, (1, block_len))[:, :block_len * 2 * block_len]  42.3 us
    dot_general x1, matrix products, body(): jnp.dot(gated, lax.all_gather(out_weight, ('seq', 'section'), axis=1, til...  31.8 us
    dot_general x2, matrix products, apply_blocks(): jnp.einsum('gij,bjgc->bigc', matrix, blocks, preferred_element_type=jnp.f...  31.7 us
    slice x1, local copies, waits for them, and re-layouts, filter_matrices(): return (both[:, :, block_len:], both[:, :, :block_len])  24.4 us
    slice x1, local copies, waits for them, and re-layouts, filter_matrices(): tiled = jnp.tile(pattern, (1, block_len))[:, :block_len * 2 * block_len]  23.3 us
    add x1, local copies, waits for them, and re-layouts, body(): convolved = (convolved + carried).reshape(seq_len, channels)  13.4 us
  transfers between devices with their start and end apart: 2, of which 1 were waited for; matrix products, arithmetic and copies ran while one was open for 53% of the time, Pallas kernels for 0%

commit v1 on v0

v1 whole, which is shorter than its diff:
```python
import functools

import jax
import jax.numpy as jnp
from jax import lax
from jax.experimental import pallas as pl
from jax.experimental.pallas import tpu as pltpu
from jax.sharding import PartitionSpec as P

LANES = 128
SEQ = ("seq", "section")
EVERY = ("groups", "seq", "section")
F32, BF16 = jnp.float32, jnp.bfloat16


def cost(us):
    return pl.CostEstimate(flops=int(us * 1.1e9), bytes_accessed=1, transcendentals=0)


def pass_kernel(*refs):
    pass


def after(values, *waits, weight=0):
    return pl.pallas_call(
        pass_kernel,
        in_specs=[pl.BlockSpec(memory_space=pl.ANY)] * (len(values) + len(waits)),
        out_specs=[pl.BlockSpec(memory_space=pl.ANY)] * len(values),
        out_shape=[jax.ShapeDtypeStruct(v.shape, v.dtype) for v in values],
        input_output_aliases={i: i for i in range(len(values))},
        cost_estimate=cost(weight),
    )(*values, *waits)


def product_of(key, value):
    return (key.astype(F32) * value.astype(F32)).astype(BF16)


def gate_kernel(per_group, blocks, start_ref, ring_ref, skip_ref, q_ref, k_ref, v_ref, before_ref, *rest):
    out_refs = rest[-blocks:]
    rows, width = out_refs[0].shape
    groups = LANES // per_group
    row = lax.broadcasted_iota(jnp.int32, (rows, rows), 0)
    col = lax.broadcasted_iota(jnp.int32, (rows, rows), 1)
    keep = (row >= col).astype(F32).astype(BF16)
    lane_group = lax.broadcasted_iota(jnp.int32, (2 * rows, blocks * LANES), 1) % LANES // per_group

    def step(t, carry):
        lanes = pl.ds(pl.multiple_of(t * LANES, LANES), LANES)
        spans = [slice(b * rows, (b + 1) * rows) for b in range(blocks)]
        products = [product_of(k_ref[span, lanes], v_ref[span, lanes]) for span in spans]
        before = [before_ref[:, lanes]] + products[:-1]
        data = jnp.concatenate([jnp.concatenate(products, axis=1), jnp.concatenate(before, axis=1)], axis=0)
        rings = ring_ref[pl.ds(pl.multiple_of(t * groups, groups), groups), :]
        left, right = [], []
        for g in range(groups):
            ring = jnp.broadcast_to(rings[g : g + 1, :], (rows, rows))
            ring = pltpu.roll(ring, 0, 1, stride=1, stride_axis=0).astype(BF16)
            lower = ring * keep
            left += [lower, ring - lower]
            right.append(jnp.where(lane_group == g, data, jnp.zeros_like(data)))
        convolved = jnp.dot(
            jnp.concatenate(left, axis=1), jnp.concatenate(right, axis=0), preferred_element_type=F32
        )
        skip = skip_ref[:, lanes]
        for b, span in enumerate(spans):
            here = convolved[:, b * LANES : (b + 1) * LANES] + skip * products[b].astype(F32)
            out_refs[b][:, lanes] = (q_ref[span, lanes].astype(F32) * here).astype(BF16)
        return carry

    lax.fori_loop(0, width // LANES, step, 0)


def gate(rings, skip, queries, key_proj, value_proj, before, start, count, waits=()):
    rows = rings.shape[1]
    seq_len, channels = queries.shape
    blocks = seq_len // rows
    per_group = channels // rings.shape[0]
    tile = min(512, count)
    steps = count // tile

    def at(height):
        return pl.BlockSpec((height, tile), lambda i, s: (0, s[0] * steps + i))

    return pl.pallas_call(
        functools.partial(gate_kernel, per_group, blocks),
        grid_spec=pltpu.PrefetchScalarGridSpec(
            num_scalar_prefetch=1,
            grid=(steps,),
            in_specs=[
                pl.BlockSpec((tile // per_group, rows), lambda i, s: (s[0] * steps + i, 0)),
                at(1),
                at(seq_len),
                at(seq_len),
                at(seq_len),
                pl.BlockSpec((rows, tile), lambda i, s: (0, i)),
            ]
            + [pl.BlockSpec(memory_space=pl.ANY)] * len(waits),
            out_specs=[pl.BlockSpec((rows, tile), lambda i, s: (0, i))] * blocks,
        ),
        out_shape=[jax.ShapeDtypeStruct((rows, count), BF16)] * blocks,
        compiler_params=pltpu.CompilerParams(vmem_limit_bytes=56 << 20),
        cost_estimate=cost(0),
    )(jnp.reshape(start, (1,)).astype(jnp.int32), rings, skip, queries, key_proj, value_proj, before, *waits)


def rings_of(filter_taps):
    return jnp.roll(filter_taps[:, ::-1], 1, axis=1).astype(F32)


def project_kernel(count, weight_count, *refs):
    rows, weights = refs[:count], refs[count : count + weight_count]
    keep_ref, send_ref, total = refs[-3:]
    step = pl.program_id(0)

    @pl.when(step == 0)
    def _():
        total[...] = jnp.zeros_like(total)

    left = jnp.concatenate([r[...] for r in rows], axis=0)
    right = jnp.concatenate([w[...] for w in weights], axis=1)
    total[...] += jnp.dot(left, right, preferred_element_type=F32)

    @pl.when(step == pl.num_programs(0) - 1)
    def _():
        half = total.shape[0] // 2
        keep_ref[...] = total[:half, :]
        send_ref[...] = total[half:, :].astype(BF16)


def project(rows, weights, weight, waits=()):
    depth = rows[0].shape[1]
    height = sum(r.shape[0] for r in rows)
    width = sum(w.shape[1] for w in weights)
    tile = min(1024, depth)
    return pl.pallas_call(
        functools.partial(project_kernel, len(rows), len(weights)),
        grid=(depth // tile,),
        in_specs=[pl.BlockSpec((r.shape[0], tile), lambda k: (0, k)) for r in rows]
        + [pl.BlockSpec((tile, w.shape[1]), lambda k: (k, 0)) for w in weights]
        + [pl.BlockSpec(memory_space=pl.ANY)] * len(waits),
        out_specs=[pl.BlockSpec((height // 2, width), lambda k: (0, 0))] * 2,
        out_shape=[
            jax.ShapeDtypeStruct((height // 2, width), F32),
            jax.ShapeDtypeStruct((height // 2, width), BF16),
        ],
        scratch_shapes=[pltpu.VMEM((height, width), F32)],
        compiler_params=pltpu.CompilerParams(vmem_limit_bytes=40 << 20),
        cost_estimate=cost(weight),
    )(*rows, *weights, *waits)


def settle_kernel(keep_ref, arrived_ref, *refs):
    near_ref, far_ref = refs[-2:]
    rows = near_ref.shape[0]
    near_ref[...] = (keep_ref[:rows, :] + arrived_ref[:rows, :].astype(F32)).astype(BF16)
    far_ref[...] = (keep_ref[rows:, :] + arrived_ref[rows:, :].astype(F32)).astype(BF16)


def settle(keep, arrived, waits):
    rows, width = keep.shape
    tile = min(512, width)
    whole = pl.BlockSpec((rows, tile), lambda i: (0, i))
    return pl.pallas_call(
        settle_kernel,
        grid=(width // tile,),
        in_specs=[whole, whole] + [pl.BlockSpec(memory_space=pl.ANY)] * len(waits),
        out_specs=[pl.BlockSpec((rows // 2, tile), lambda i: (0, i))] * 2,
        out_shape=[jax.ShapeDtypeStruct((rows // 2, width), BF16)] * 2,
        compiler_params=pltpu.CompilerParams(vmem_limit_bytes=16 << 20),
        cost_estimate=cost(0),
    )(keep, arrived, *waits)


def add_kernel(widths, place_ref, *refs):
    total_ref, out_ref = refs[0], refs[-1]
    span = sum(widths)
    for h, width in enumerate(widths):
        for j in range(4):
            start = place_ref[1 + j] * span + sum(widths[:h])
            lanes = pl.ds(pl.multiple_of(start, LANES), width)
            mine = refs[1 + 2 * h + j // 2][:, (j % 2) * width : (j % 2 + 1) * width]
            out_ref[:, lanes] = (total_ref[:, lanes].astype(F32) + mine.astype(F32)).astype(BF16)


def add_slots(residual, total, parts, block, places, slots, order):
    widths = [cut[0].shape[1] // slots // 2 for cut in parts]
    rows = parts[0][0].shape[0]
    span = 4 * sum(widths)
    flat = [(piece, 2 * width) for cut, width in zip(parts, widths) for piece in cut]
    whole = pl.BlockSpec((rows, span), lambda i, s: (block, s[5 + i]))
    so_far = [] if total is None else [total]
    return pl.pallas_call(
        functools.partial(add_kernel, widths),
        grid_spec=pltpu.PrefetchScalarGridSpec(
            num_scalar_prefetch=1,
            grid=(slots,),
            in_specs=[whole]
            + [pl.BlockSpec((rows, w), lambda i, s: (0, i)) for _, w in flat]
            + [pl.BlockSpec(memory_space=pl.ANY)] * len(so_far),
            out_specs=whole,
        ),
        out_shape=jax.ShapeDtypeStruct(residual.shape, residual.dtype),
        input_output_aliases={2 + len(flat): 0} if so_far else {},
        compiler_params=pltpu.CompilerParams(vmem_limit_bytes=16 << 20),
        cost_estimate=cost(1),
    )(jnp.concatenate([jnp.zeros((1,), jnp.int32), order, places]), residual, *[p for p, _ in flat], *so_far)


def swapped(value, bit, devices):
    return lax.ppermute(value, EVERY, [(d, d ^ bit) for d in range(devices)])


def along(value, planes, sources, steps, stride):
    per_window = planes * stride
    pairs = [
        (w * per_window + z * stride + i, w * per_window + (z + steps) * stride + i)
        for w in range(2)
        for z in sources
        for i in range(stride)
    ]
    return lax.ppermute(value, EVERY, pairs)


def arrivals(planes):
    return [
        [(way, s) for s in range(1, planes) for way in (1, -1) if 0 <= z + way * s < planes]
        for z in range(planes)
    ]


def paired(queries, key_proj, value_proj, filter_taps, skip_gain, out_weight, residual):
    seq_len, channels = queries.shape
    rows = filter_taps.shape[1]
    blocks = seq_len // rows
    half = channels // 2
    devices = 2 * lax.axis_size("seq") * 2
    window, section = lax.axis_index("groups"), lax.axis_index("section")
    planes = lax.axis_size("seq") // 2
    plane, side = lax.axis_index("seq") // 2, lax.axis_index("seq") % 2

    last = seq_len - rows
    shards = planes * 4
    edge = [w * shards + i for w in range(2) for i in range(shards - 1)]
    turn = [i for i in edge if i % 4 == 3]

    def outgoing(start):
        return product_of(
            lax.dynamic_slice(key_proj, (last, start), (rows, half)),
            lax.dynamic_slice(value_proj, (last, start), (rows, half)),
        )

    before_own = lax.ppermute(outgoing(window * half), EVERY, [(i, i + 1) for i in edge])
    leaving = outgoing((1 - window) * half)
    before_theirs = lax.ppermute(leaving, EVERY, [(i, i + 1) for i in edge if i not in turn])
    passing = lax.ppermute(leaving, EVERY, [(i, i - 2) for i in turn])
    passing = lax.ppermute(passing, EVERY, [(i - 2, i + 1) for i in turn])
    before_theirs = jnp.where(side + section == 0, passing, before_theirs)

    mine = lax.dynamic_slice_in_dim(out_weight, window * half, half, 0)
    cuts = [mine[:, : mine.shape[1] // 2], mine[:, mine.shape[1] // 2 :]]
    got = [{}, {}]
    ends = [[c, c] for c in cuts]

    def hold(cuts_held, s, *waits):
        held = after([v for cut in cuts_held for v in ends[cut]], *waits)
        for n, cut in enumerate(cuts_held):
            ends[cut] = held[2 * n : 2 * n + 2]
            got[cut][-1, s], got[cut][1, s] = ends[cut]

    def forward(cut, s):
        up, down = ends[cut]
        up = along(up, planes, range(s - 1, planes - 1), 1, 4)
        down = along(down, planes, range(1, planes - s + 1), -1, 4)
        got[cut][1, s], got[cut][-1, s] = down, up
        ends[cut] = [up, down]

    forward(0, 1)
    forward(1, 1)
    order = arrivals(planes)

    def slot(cut, j):
        value = got[cut][order[0][j]]
        for z in range(1, planes):
            value = jnp.where(plane == z, got[cut][order[z][j]], value)
        return value

    def slot_place(j):
        return sum(jnp.where(plane == z, z + order[z][j][0] * order[z][j][1], 0) for z in range(planes))

    rings, skip = rings_of(filter_taps), skip_gain[None, :]
    args = (rings, skip, queries, key_proj, value_proj)
    firsts = gate(*args, before_own, window, half)[::-1]
    crossed = [swapped(f, 2, devices) for f in firsts]
    theirs = gate(*args, before_theirs, 1 - window, half, firsts)[::-1]
    seconds = [swapped(t, devices // 2, devices) for t in theirs]
    hold([0, 1], 1, *theirs)
    forward(0, 2)
    forward(1, 2)
    marker = after([jnp.zeros((8, LANES), F32)], crossed[0], weight=1)
    for s in range(3, planes):
        hold([0], s - 1, *marker)
        forward(0, s)
        hold([1], s - 1, crossed[-1], seconds[0])
        forward(1, s)
    far = [swapped(o, 2, devices) for o in seconds]
    gathered = list(zip(firsts, crossed, seconds, far))

    def sent_back(send):
        return swapped(send, devices // 2, devices)

    def shared(keep, arrived, *waits):
        near, far_rows = settle(keep, arrived, waits)
        return [near, swapped(far_rows, 2, devices)]

    def both(value):
        return [value, swapped(value, 1, devices)]

    place = jnp.stack([side * 2 + section, side * 2 + 1 - section, 2 - side * 2 + section, 3 - side * 2 - section])
    place = place.astype(jnp.int32)
    early = both(mine)
    for j in range(planes - 2):
        pairs = [both(slot(cut, j)) for cut in range(2)]
        early += [pairs[0][0], pairs[1][0], pairs[0][1], pairs[1][1]]
    early_places = jnp.stack([plane] + [slot_place(j) for j in range(planes - 2)]).astype(jnp.int32)
    total, sends, arrivals_back = None, [], []
    last_slots = []
    for i, block in enumerate(reversed(range(blocks))):
        keep, send = project(gathered[i], early, 1 if i else 2, sends[-1:])
        sends.append(send)
        arrivals_back.append(sent_back(send))
        total = add_slots(residual, total, [shared(keep, arrivals_back[-1])], block, early_places, planes - 1, place)
        if i < 2:
            hold([i], planes - 1, far[i], send)
            last_slots.append(both(slot(i, planes - 2)))
    everyone = [gathered[blocks - 1 - b][p] for p in range(4) for b in range(blocks)]
    late = []
    for cut in range(2):
        keep, send = project(everyone, last_slots[cut], 4, [sends[-1], arrivals_back[cut]])
        sends.append(send)
        late.append(shared(keep, sent_back(send), *([total] if cut else [])))
    return add_slots(residual, total, late, 0, slot_place(planes - 2)[None].astype(jnp.int32), 1, place)


def general(queries, key_proj, value_proj, filter_taps, skip_gain, out_weight, residual):
    seq_len, channels = queries.shape
    rows = filter_taps.shape[1]
    outgoing = product_of(key_proj[seq_len - rows :], value_proj[seq_len - rows :])
    count = lax.axis_size(SEQ)
    before = lax.ppermute(outgoing, SEQ, [(i, i + 1) for i in range(count - 1)])
    rings, skip = rings_of(filter_taps), skip_gain[None, :]
    gated = gate(rings, skip, queries, key_proj, value_proj, before, jnp.int32(0), channels)
    gated = jnp.concatenate(gated, axis=0)
    weight = lax.all_gather(out_weight, SEQ, axis=1, tiled=True)
    projected = jnp.dot(gated, weight, preferred_element_type=F32)
    share = lax.psum_scatter(projected, "chan", scatter_dimension=1, tiled=True)
    return (residual.astype(F32) + share).astype(BF16)


def solution(mesh):
    sizes = mesh.shape
    fits = sizes["groups"] == 2 and sizes["chan"] == 1 and sizes["section"] == 2 and sizes["seq"] % 2 == 0
    return jax.shard_map(
        paired if fits and sizes["seq"] >= 6 else general,
        mesh=mesh,
        in_specs=(
            P(("groups", "seq", "section"), "chan"),
            P(("groups", "seq", "section"), "chan"),
            P(("groups", "seq", "section"), "chan"),
            P("chan", None),
            P("chan"),
            P("chan", ("seq", "section")),
            P(("groups", "seq", "section"), "chan"),
        ),
        out_specs=P(("groups", "seq", "section"), "chan"),
        check_vma=False,
    )
```

time: 432 us -> 257 us (0.59)
  local copies, waits for them, and re-layouts: 190 us -> 15.5 us
  waiting for transfers between devices: 151 us -> 74 us
  Pallas kernels: 0 us -> 74.6 us
  starting transfers between devices: 4.79 us -> 77.6 us
  matrix products: 63.5 us -> 0 us
  between operations: 13.4 us -> 0.45 us
  other arithmetic: 6.9 us -> 13.6 us
    all_gather x1 -> x0, waiting for transfers between devices: 150 us -> none  [body(): lax.all_gather(out_weight, ('seq', 'section'), axis=1, tiled=True)]
    pallas_call x0 -> x19, Pallas kernels: none -> 74.6 us  [the longest x4 32.5 us: project(): pl.pallas_call(functools.partial(project_kernel, len(rows), len(weights))...]
    ppermute x1 -> x37, waiting for transfers between devices: 0.01 us -> 74 us  [the longest x21 54.5 us: swapped(): return lax.ppermute(value, EVERY, [(d, d ^ bit) for d in range(devices)])]
    ppermute x1 -> x37, starting transfers between devices: 4.78 us -> 77.6 us  [the longest x21 45.2 us: swapped(): return lax.ppermute(value, EVERY, [(d, d ^ bit) for d in range(devices)])]
    dot_general x3 -> x0, matrix products: 63.5 us -> none  [the longest x1 31.8 us: body(): jnp.dot(gated, lax.all_gather(out_weight, ('seq', 'section'), axis=1, til...]
    unnamed x13 -> x56, local copies, waits for them, and re-layouts: 66.8 us -> 8.19 us
    slice x4 -> x3, local copies, waits for them, and re-layouts: 55.1 us -> 3.51 us  [the longest x1 3.02 us: paired(): cuts = [mine[:, :mine.shape[1] // 2], mine[:, mine.shape[1] // 2:]]]
    another operation x2 -> x0, local copies, waits for them, and re-layouts: 42.3 us -> none  [filter_matrices(): tiled = jnp.tile(pattern, (1, block_len))[:, :block_len * 2 * block_len]]
  transfers between devices with their start and end apart: 2 -> 37, of which waited for: 1 -> 10; matrix products, arithmetic and copies ran while one was open for 53% -> 6% of each run, Pallas kernels for 0% -> 29%
where the time goes in v1:
time: 257 us; the launch traced here: 256 us
  starting transfers between devices  77.6 us (30%)
  Pallas kernels  74.6 us (29%)
  waiting for transfers between devices  74 us (29%)
  local copies, waits for them, and re-layouts  15.5 us (6%)
  other arithmetic  13.6 us (5%)
    ppermute x21, waiting for transfers between devices, swapped(): return lax.ppermute(value, EVERY, [(d, d ^ bit) for d in range(devices)])  54.5 us
    ppermute x21, starting transfers between devices, swapped(): return lax.ppermute(value, EVERY, [(d, d ^ bit) for d in range(devices)])  45.2 us
    pallas_call x4, Pallas kernels, project(): pl.pallas_call(functools.partial(project_kernel, len(rows), len(weights))...  32.5 us
    pallas_call x2, Pallas kernels, gate(): pl.pallas_call(functools.partial(gate_kernel, per_group, blocks), grid_sp...  28.6 us
    ppermute x12, starting transfers between devices, along(): return lax.ppermute(value, EVERY, pairs)  22.2 us
    ppermute x12, waiting for transfers between devices, along(): return lax.ppermute(value, EVERY, pairs)  19.4 us
    pallas_call x3, Pallas kernels, add_slots(): pl.pallas_call(functools.partial(add_kernel, widths), grid_spec=pltpu.Pre...  8.51 us
    unnamed x56, local copies, waits for them, and re-layouts  8.19 us
  transfers between devices with their start and end apart: 37, of which 10 were waited for; matrix products, arithmetic and copies ran while one was open for 6% of the time, Pallas kernels for 29%

profile of v1, /device:TPU:0, one launch (start us, length us, event | category | flops | bytes accessed | tf_op | source)
XLA Modules:
  0.0 255.7 jit_solution(10605001569043147203)
XLA Ops:
  0.0 4.3 %multiply_convert_fusion = (bf16[128,4096]{1,0:T(8,128)(2,1)}, bf16[128,4096]{1,0:T(8,128)(2,1)}) fusion(bf16[256,8192]{1,0:T(8,128)(2,1)} %v_ref.3, s32[]{:T(128)S(6)} %select_n.137, bf16[256,8192]{1,0:T(8,128)(2,1)} %k_ref.3, s32[]{:T(128)S(6)} %select_n.135), kind=kLoop, calls=%fused_computation | loop fusion | flops 4194304 | bytes 6291464 | tf_op jit(solution)/shard_map/convert_element_type | solution.py:36
  8.0 5.8 %collective-permute-start = (bf16[128,4096]{1,0:T(8,128)(2,1)}, bf16[128,4096]{1,0:T(8,128)(2,1)}, u32[]{:S(2)}, u32[]{:S(2)}) collective-permute-start(bf16[128,4096]{1,0:T(8,128)(2,1)} %get-tuple-element.70), channel_id=1, source_target_pairs={{0,1},{1,2},{2,3},{3,4},{4,5},{5,6},{6,7},{7,8},{8,9},{9,10},{10,1... | collective-permute-start | bytes 3145736 | tf_op jit(solution)/shard_map/ppermute | solution.py:253
  17.5 3.1 %collective-permute-start.10 = (bf16[4096,128]{1,0:T(8,128)(2,1)}, bf16[4096,128]{1,0:T(8,128)(2,1)S(1)}, u32[]{:S(2)}, u32[]{:S(2)}) collective-permute-start(bf16[4096,128]{1,0:T(8,128)(2,1)} %get-tuple-element.72), channel_id=1, source_target_pairs={{0,4},{1,5},{2,6},{3,7},{4,8},{5,9},{6,10},{7,11},{8,12},{9,13},{1... | collective-permute-start | bytes 3145736 | tf_op jit(solution)/shard_map/ppermute | solution.py:222
  22.5 5.6 %collective-permute-start.12 = (bf16[4096,128]{1,0:T(8,128)(2,1)}, bf16[4096,128]{1,0:T(8,128)(2,1)}, u32[]{:S(2)}, u32[]{:S(2)}) collective-permute-start(bf16[4096,128]{1,0:T(8,128)(2,1)} %get-tuple-element.71), channel_id=1, source_target_pairs={{0,4},{1,5},{2,6},{3,7},{4,8},{5,9},{6,10},{7,11},{8,12},{9,13},{1... | collective-permute-start | bytes 3145736 | tf_op jit(solution)/shard_map/ppermute | solution.py:222
  30.2 14.3 %shard_map.73 = (bf16[128,4096]{1,0:T(8,128)(2,1)}, bf16[128,4096]{1,0:T(8,128)(2,1)}) custom-call(s32[1]{0:T(128)} %bitcast.5.start_ref, f32[512,128]{1,0:T(8,128)} %maximum_convert_fusion.ring_ref, f32[1,8192]{1,0:T(1,128)} %bitcast.13, bf16[256,8192]{1,0:T(8,128)(2,1)} %q_ref.3, bf16[256,8192]{1,0:T(8,128)(2,1)} %k_ref.3, bf16[256,8192]{1,0:T(8,128)(2,1)} %v_ref.3, ...), custom_call_target="tpu_custom_call" | custom-call | bytes 1 | tf_op jit(solution)/shard_map/pallas_call | solution.py:85
  44.5 8.4 %collective-permute-start.2 = (bf16[128,4096]{1,0:T(8,128)(2,1)}, bf16[128,4096]{1,0:T(8,128)(2,1)}, u32[]{:S(2)}, u32[]{:S(2)}) collective-permute-start(bf16[128,4096]{1,0:T(8,128)(2,1)} %get-tuple-element.38.rest_0_.refs_0_.refs_1_), channel_id=1, source_target_pairs={{0,2},{1,3},{2,0},{3,1},{4,6},{5,7},{6,4},{7,5},{8,10},{9,11},{10,... | collective-permute-start | bytes 3145736 | tf_op jit(solution)/shard_map/ppermute | solution.py:211
  54.0 14.4 %shard_map.74 = (bf16[128,4096]{1,0:T(8,128)(2,1)}, bf16[128,4096]{1,0:T(8,128)(2,1)}) custom-call(s32[1]{0:T(128)} %bitcast.7.start_ref, f32[512,128]{1,0:T(8,128)} %maximum_convert_fusion.ring_ref, f32[1,8192]{1,0:T(1,128)} %bitcast.14, bf16[256,8192]{1,0:T(8,128)(2,1)} %q_ref.3, bf16[256,8192]{1,0:T(8,128)(2,1)} %k_ref.3, bf16[256,8192]{1,0:T(8,128)(2,1)} %v_ref.3, ...), custom_call_target="tpu_custom_call" | custom-call | bytes 1 | tf_op jit(solution)/shard_map/pallas_call | solution.py:85
  73.9 3.0 %constant_dynamic-slice_fusion.1.refs_4_ = bf16[4096,256]{1,0:T(8,128)(2,1)} fusion(bf16[8192,256]{1,0:T(8,128)(2,1)} %param.12, s32[]{:T(128)S(6)} %select_n.135), kind=kLoop, calls=%fused_computation.13 | loop fusion | bytes 4194308 | tf_op jit(solution)/shard_map/dynamic_slice | solution.py:260
  77.0 11.1 %collective-permute-start.18 = (bf16[4096,256]{1,0:T(8,128)(2,1)}, bf16[4096,256]{1,0:T(8,128)(2,1)}, u32[]{:S(2)}, u32[]{:S(2)}) collective-permute-start(bf16[4096,256]{1,0:T(8,128)(2,1)} %constant_dynamic-slice_fusion.1.refs_4_), channel_id=1, source_target_pairs={{0,1},{1,0},{2,3},{3,2},{4,5},{5,4},{6,7},{7,6},{8,9},{9,8},{10,11... | collective-permute-start | bytes 6291464 | tf_op jit(solution)/shard_map/ppermute | solution.py:211
  88.7 5.9 %collective-permute-done.1.refs_2_.refs_1_ = bf16[128,4096]{1,0:T(8,128)(2,1)S(1)} collective-permute-done((bf16[128,4096]{1,0:T(8,128)(2,1)S(1)}, bf16[128,4096]{1,0:T(8,128)(2,1)S(1)}, u32[]{:S(2)}, u32[]{:S(2)}) %collective-permute-start.1) | collective-permute-done | bytes 1048608 | tf_op jit(solution)/shard_map/ppermute | solution.py:211
  105.1 5.9 %collective-permute-start.20 = (bf16[4096,128]{1,0:T(8,128)(2,1)S(1)}, bf16[4096,128]{1,0:T(8,128)(2,1)}, u32[]{:S(2)}, u32[]{:S(2)}) collective-permute-start(bf16[4096,128]{1,0:T(8,128)(2,1)S(1)} %get-tuple-element.74.refs_7_), channel_id=1, source_target_pairs={{0,1},{1,0},{2,3},{3,2},{4,5},{5,4},{6,7},{7,6},{8,9},{9,8},{10,11... | collective-permute-start | bytes 3145736 | tf_op jit(solution)/shard_map/ppermute | solution.py:211
  111.1 16.4 %collective-permute-done.15.refs_1_ = bf16[4096,128]{1,0:T(8,128)(2,1)} collective-permute-done((bf16[4096,128]{1,0:T(8,128)(2,1)}, bf16[4096,128]{1,0:T(8,128)(2,1)}, u32[]{:S(2)}, u32[]{:S(2)}) %collective-permute-start.15) | collective-permute-done | bytes 1048608 | tf_op jit(solution)/shard_map/ppermute | solution.py:222
  129.7 5.2 %collective-permute-start.19 = (bf16[4096,128]{1,0:T(8,128)(2,1)S(1)}, bf16[4096,128]{1,0:T(8,128)(2,1)S(1)}, u32[]{:S(2)}, u32[]{:S(2)}) collective-permute-start(bf16[4096,128]{1,0:T(8,128)(2,1)S(1)} %get-tuple-element.76.refs_6_), channel_id=1, source_target_pairs={{0,1},{1,0},{2,3},{3,2},{4,5},{5,4},{6,7},{7,6},{8,9},{9,8},{10,11... | collective-permute-start | bytes 3145736 | tf_op jit(solution)/shard_map/ppermute | solution.py:211
  140.7 20.2 %collective-permute-done.9.refs_3_.refs_2_.refs_7_ = bf16[128,4096]{1,0:T(8,128)(2,1)S(1)} collective-permute-done((bf16[128,4096]{1,0:T(8,128)(2,1)S(1)}, bf16[128,4096]{1,0:T(8,128)(2,1)S(1)}, u32[]{:S(2)}, u32[]{:S(2)}) %collective-permute-start.9) | collective-permute-done | bytes 1048608 | tf_op jit(solution)/shard_map/ppermute | solution.py:211
  162.4 10.8 %shard_map.79 = (f32[256,1536]{1,0:T(8,128)}, bf16[256,1536]{1,0:T(8,128)(2,1)}) custom-call(bf16[128,4096]{1,0:T(8,128)(2,1)S(1)} %copy-done.3, bf16[128,4096]{1,0:T(8,128)(2,1)} %collective-permute-done.2.refs_1_.refs_3_, bf16[128,4096]{1,0:T(8,128)(2,1)S(1)} %copy-done.9, bf16[128,4096]{1,0:T(8,128)(2,1)S(1)} %collective-permute-done.9.refs_3_.refs_2_.refs_7_, ...), custom_call_target="tpu_custom_call" | custom-call | flops 2200000000 | bytes 1 | tf_op jit(solution)/shard_map/pallas_call | solution.py:136
  173.3 9.7 %collective-permute-done.8.refs_3_.refs_6_.refs_2_ = bf16[128,4096]{1,0:T(8,128)(2,1)S(1)} collective-permute-done((bf16[128,4096]{1,0:T(8,128)(2,1)}, bf16[128,4096]{1,0:T(8,128)(2,1)S(1)}, u32[]{:S(2)}, u32[]{:S(2)}) %collective-permute-start.8) | collective-permute-done | bytes 1048608 | tf_op jit(solution)/shard_map/ppermute | solution.py:211
  183.5 10.7 %shard_map.81 = (f32[256,1536]{1,0:T(8,128)}, bf16[256,1536]{1,0:T(8,128)(2,1)}) custom-call(bf16[128,4096]{1,0:T(8,128)(2,1)S(1)} %copy-done.2, bf16[128,4096]{1,0:T(8,128)(2,1)S(1)} %copy-done.6, bf16[128,4096]{1,0:T(8,128)(2,1)} %collective-permute-done.6.refs_2_.refs_4_, bf16[128,4096]{1,0:T(8,128)(2,1)S(1)} %collective-permute-done.8.refs_3_.refs_6_.refs_2_, ...), custom_call_target="tpu_custom_call" | custom-call | flops 1100000000 | bytes 1 | tf_op jit(solution)/shard_map/pallas_call | solution.py:136
  200.3 3.4 %collective-permute-done.26.refs_11_.arrived_ref = bf16[256,1536]{1,0:T(8,128)(2,1)} collective-permute-done((bf16[256,1536]{1,0:T(8,128)(2,1)}, bf16[256,1536]{1,0:T(8,128)(2,1)}, u32[]{:S(2)}, u32[]{:S(2)}) %collective-permute-start.26) | collective-permute-done | bytes 786464 | tf_op jit(solution)/shard_map/ppermute | solution.py:211
  203.7 3.2 %shard_map.87 = (bf16[128,1536]{1,0:T(8,128)(2,1)S(1)}, bf16[128,1536]{1,0:T(8,128)(2,1)}) custom-call(f32[256,1536]{1,0:T(8,128)S(1)} %copy-done.16, bf16[256,1536]{1,0:T(8,128)(2,1)} %collective-permute-done.26.refs_11_.arrived_ref), custom_call_target="tpu_custom_call" | custom-call | bytes 1 | tf_op jit(solution)/shard_map/pallas_call | solution.py:164
  208.2 11.0 %collective-permute-done.32.refs_11_.arrived_ref = bf16[256,1536]{1,0:T(8,128)(2,1)S(1)} collective-permute-done((bf16[256,1536]{1,0:T(8,128)(2,1)}, bf16[256,1536]{1,0:T(8,128)(2,1)S(1)}, u32[]{:S(2)}, u32[]{:S(2)}) %collective-permute-start.32) | collective-permute-done | bytes 786464 | tf_op jit(solution)/shard_map/ppermute | solution.py:211
  222.2 5.5 %shard_map.82 = (f32[512,256]{1,0:T(8,128)S(1)}, bf16[512,256]{1,0:T(8,128)(2,1)}) custom-call(bf16[128,4096]{1,0:T(8,128)(2,1)S(1)} %copy-done.2, bf16[128,4096]{1,0:T(8,128)(2,1)S(1)} %copy-done.4, bf16[128,4096]{1,0:T(8,128)(2,1)S(1)} %copy-done.7, bf16[128,4096]{1,0:T(8,128)(2,1)} %collective-permute-done.2.refs_1_.refs_3_, ...), custom_call_target="tpu_custom_call" | custom-call | flops 4400000000 | bytes 1 | tf_op jit(solution)/shard_map/pallas_call | solution.py:136
  229.7 5.5 %shard_map.85 = (f32[512,256]{1,0:T(8,128)S(1)}, bf16[512,256]{1,0:T(8,128)(2,1)}) custom-call(bf16[128,4096]{1,0:T(8,128)(2,1)S(1)} %copy-done.2, bf16[128,4096]{1,0:T(8,128)(2,1)S(1)} %copy-done.4, bf16[128,4096]{1,0:T(8,128)(2,1)S(1)} %copy-done.7, bf16[128,4096]{1,0:T(8,128)(2,1)} %collective-permute-done.2.refs_1_.refs_3_, ...), custom_call_target="tpu_custom_call" | custom-call | flops 4400000000 | bytes 1 | tf_op jit(solution)/shard_map/pallas_call | solution.py:136
  239.1 3.4 %shard_map.88.refs_3_ = bf16[256,4096]{1,0:T(8,128)(2,1)} custom-call(s32[8]{0:T(128)S(1)} %concatenate.16.place_ref, bf16[256,4096]{1,0:T(8,128)(2,1)S(1)} %copy-done.1, bf16[128,1536]{1,0:T(8,128)(2,1)S(1)} %copy-done.24, bf16[128,1536]{1,0:T(8,128)(2,1)} %collective-permute-done.35.refs_2_), custom_call_target="tpu_custom_call" | custom-call | flops 1100000000 | bytes 1 | tf_op jit(solution)/shard_map/pallas_call | solution.py:193
  242.5 3.4 %shard_map.89.refs_0_.refs_5_ = bf16[256,4096]{1,0:T(8,128)(2,1)} custom-call(s32[8]{0:T(128)S(1)} %concatenate.16.place_ref, bf16[256,4096]{1,0:T(8,128)(2,1)S(1)} %copy-done.1, bf16[128,1536]{1,0:T(8,128)(2,1)S(1)} %get-tuple-element.62.refs_1_, bf16[128,1536]{1,0:T(8,128)(2,1)} %collective-permute-done.34.refs_2_, ...), custom_call_target="tpu_custom_call", output_to_operand_aliasing={{}: (4, {})} | custom-call | flops 1100000000 | bytes 1 | tf_op jit(solution)/shard_map/pallas_call | solution.py:193
  (139 shorter events, 65.1 us)
Async XLA Ops:
  13.8 30.7 %collective-permute-start.4 = (bf16[128,4096]{1,0:T(8,128)(2,1)}, bf16[128,4096]{1,0:T(8,128)(2,1)S(1)}, u32[]{:S(2)}, u32[]{:S(2)}) collective-permute-start(bf16[128,4096]{1,0:T(8,128)(2,1)} %collective-permute-done.3), channel_id=1, source_target_pairs={{1,4},{5,8},{9,12},{17,20},{21,24},{25,28}} | collective-permute-start | bytes 3145736 | tf_op jit(solution)/shard_map/ppermute | solution.py:257
  17.5 50.9 %collective-permute-start.10 = (bf16[4096,128]{1,0:T(8,128)(2,1)}, bf16[4096,128]{1,0:T(8,128)(2,1)S(1)}, u32[]{:S(2)}, u32[]{:S(2)}) collective-permute-start(bf16[4096,128]{1,0:T(8,128)(2,1)} %get-tuple-element.72), channel_id=1, source_target_pairs={{0,4},{1,5},{2,6},{3,7},{4,8},{5,9},{6,10},{7,11},{8,12},{9,13},{1... | collective-permute-start | bytes 3145736 | tf_op jit(solution)/shard_map/ppermute | solution.py:222
  20.7 47.8 %collective-permute-start.11 = (bf16[4096,128]{1,0:T(8,128)(2,1)}, bf16[4096,128]{1,0:T(8,128)(2,1)}, u32[]{:S(2)}, u32[]{:S(2)}) collective-permute-start(bf16[4096,128]{1,0:T(8,128)(2,1)} %get-tuple-element.72), channel_id=1, source_target_pairs={{4,0},{5,1},{6,2},{7,3},{8,4},{9,5},{10,6},{11,7},{12,8},{13,9},{1... | collective-permute-start | bytes 3145736 | tf_op jit(solution)/shard_map/ppermute | solution.py:222
  22.5 46.0 %collective-permute-start.12 = (bf16[4096,128]{1,0:T(8,128)(2,1)}, bf16[4096,128]{1,0:T(8,128)(2,1)}, u32[]{:S(2)}, u32[]{:S(2)}) collective-permute-start(bf16[4096,128]{1,0:T(8,128)(2,1)} %get-tuple-element.71), channel_id=1, source_target_pairs={{0,4},{1,5},{2,6},{3,7},{4,8},{5,9},{6,10},{7,11},{8,12},{9,13},{1... | collective-permute-start | bytes 3145736 | tf_op jit(solution)/shard_map/ppermute | solution.py:222
  28.1 40.4 %collective-permute-start.13 = (bf16[4096,128]{1,0:T(8,128)(2,1)}, bf16[4096,128]{1,0:T(8,128)(2,1)}, u32[]{:S(2)}, u32[]{:S(2)}) collective-permute-start(bf16[4096,128]{1,0:T(8,128)(2,1)} %get-tuple-element.71), channel_id=1, source_target_pairs={{4,0},{5,1},{6,2},{7,3},{8,4},{9,5},{10,6},{11,7},{12,8},{13,9},{1... | collective-permute-start | bytes 3145736 | tf_op jit(solution)/shard_map/ppermute | solution.py:222
  44.5 32.5 %collective-permute-start.2 = (bf16[128,4096]{1,0:T(8,128)(2,1)}, bf16[128,4096]{1,0:T(8,128)(2,1)}, u32[]{:S(2)}, u32[]{:S(2)}) collective-permute-start(bf16[128,4096]{1,0:T(8,128)(2,1)} %get-tuple-element.38.rest_0_.refs_0_.refs_1_), channel_id=1, source_target_pairs={{0,2},{1,3},{2,0},{3,1},{4,6},{5,7},{6,4},{7,5},{8,10},{9,11},{10,... | collective-permute-start | bytes 3145736 | tf_op jit(solution)/shard_map/ppermute | solution.py:211
  68.4 26.2 %collective-permute-start.1 = (bf16[128,4096]{1,0:T(8,128)(2,1)S(1)}, bf16[128,4096]{1,0:T(8,128)(2,1)S(1)}, u32[]{:S(2)}, u32[]{:S(2)}) collective-permute-start(bf16[128,4096]{1,0:T(8,128)(2,1)S(1)} %copy-done.2), channel_id=1, source_target_pairs={{0,2},{1,3},{2,0},{3,1},{4,6},{5,7},{6,4},{7,5},{8,10},{9,11},{10,... | collective-permute-start | bytes 3145736 | tf_op jit(solution)/shard_map/ppermute | solution.py:211
  69.4 26.7 %collective-permute-start.21 = (bf16[4096,128]{1,0:T(8,128)(2,1)}, bf16[4096,128]{1,0:T(8,128)(2,1)}, u32[]{:S(2)}, u32[]{:S(2)}) collective-permute-start(bf16[4096,128]{1,0:T(8,128)(2,1)} %get-tuple-element.45), channel_id=1, source_target_pairs={{4,8},{5,9},{6,10},{7,11},{8,12},{9,13},{10,14},{11,15},{20,24},{2... | collective-permute-start | bytes 3145736 | tf_op jit(solution)/shard_map/ppermute | solution.py:222
  71.0 29.7 %collective-permute-start.22 = (bf16[4096,128]{1,0:T(8,128)(2,1)}, bf16[4096,128]{1,0:T(8,128)(2,1)}, u32[]{:S(2)}, u32[]{:S(2)}) collective-permute-start(bf16[4096,128]{1,0:T(8,128)(2,1)} %get-tuple-element.46), channel_id=1, source_target_pairs={{4,0},{5,1},{6,2},{7,3},{8,4},{9,5},{10,6},{11,7},{20,16},{21,17},... | collective-permute-start | bytes 3145736 | tf_op jit(solution)/shard_map/ppermute | solution.py:222
  72.3 29.7 %collective-permute-start.7 = (bf16[128,4096]{1,0:T(8,128)(2,1)}, bf16[128,4096]{1,0:T(8,128)(2,1)S(1)}, u32[]{:S(2)}, u32[]{:S(2)}) collective-permute-start(bf16[128,4096]{1,0:T(8,128)(2,1)} %get-tuple-element.40.refs_4_), channel_id=1, source_target_pairs={{0,16},{1,17},{2,18},{3,19},{4,20},{5,21},{6,22},{7,23},{8,24},{9,... | collective-permute-start | bytes 3145736 | tf_op jit(solution)/shard_map/ppermute | solution.py:211
  77.0 57.9 %collective-permute-start.18 = (bf16[4096,256]{1,0:T(8,128)(2,1)}, bf16[4096,256]{1,0:T(8,128)(2,1)}, u32[]{:S(2)}, u32[]{:S(2)}) collective-permute-start(bf16[4096,256]{1,0:T(8,128)(2,1)} %constant_dynamic-slice_fusion.1.refs_4_), channel_id=1, source_target_pairs={{0,1},{1,0},{2,3},{3,2},{4,5},{5,4},{6,7},{7,6},{8,9},{9,8},{10,11... | collective-permute-start | bytes 6291464 | tf_op jit(solution)/shard_map/ppermute | solution.py:211
  94.6 40.4 %collective-permute-start.6 = (bf16[128,4096]{1,0:T(8,128)(2,1)}, bf16[128,4096]{1,0:T(8,128)(2,1)}, u32[]{:S(2)}, u32[]{:S(2)}) collective-permute-start(bf16[128,4096]{1,0:T(8,128)(2,1)} %get-tuple-element.39.refs_5_), channel_id=1, source_target_pairs={{0,16},{1,17},{2,18},{3,19},{4,20},{5,21},{6,22},{7,23},{8,24},{9,... | collective-permute-start | bytes 3145736 | tf_op jit(solution)/shard_map/ppermute | solution.py:211
  100.8 26.7 %collective-permute-start.15 = (bf16[4096,128]{1,0:T(8,128)(2,1)}, bf16[4096,128]{1,0:T(8,128)(2,1)}, u32[]{:S(2)}, u32[]{:S(2)}) collective-permute-start(bf16[4096,128]{1,0:T(8,128)(2,1)} %get-tuple-element.42), channel_id=1, source_target_pairs={{4,0},{5,1},{6,2},{7,3},{8,4},{9,5},{10,6},{11,7},{20,16},{21,17},... | collective-permute-start | bytes 3145736 | tf_op jit(solution)/shard_map/ppermute | solution.py:222
  105.1 31.1 %collective-permute-start.20 = (bf16[4096,128]{1,0:T(8,128)(2,1)S(1)}, bf16[4096,128]{1,0:T(8,128)(2,1)}, u32[]{:S(2)}, u32[]{:S(2)}) collective-permute-start(bf16[4096,128]{1,0:T(8,128)(2,1)S(1)} %get-tuple-element.74.refs_7_), channel_id=1, source_target_pairs={{0,1},{1,0},{2,3},{3,2},{4,5},{5,4},{6,7},{7,6},{8,9},{9,8},{10,11... | collective-permute-start | bytes 3145736 | tf_op jit(solution)/shard_map/ppermute | solution.py:211
  111.0 26.0 %collective-permute-start.24 = (bf16[4096,128]{1,0:T(8,128)(2,1)S(1)}, bf16[4096,128]{1,0:T(8,128)(2,1)}, u32[]{:S(2)}, u32[]{:S(2)}) collective-permute-start(bf16[4096,128]{1,0:T(8,128)(2,1)S(1)} %get-tuple-element.73.refs_11_), channel_id=1, source_target_pairs={{0,1},{1,0},{2,3},{3,2},{4,5},{5,4},{6,7},{7,6},{8,9},{9,8},{10,11... | collective-permute-start | bytes 3145736 | tf_op jit(solution)/shard_map/ppermute | solution.py:211
  135.0 26.0 %collective-permute-start.9 = (bf16[128,4096]{1,0:T(8,128)(2,1)S(1)}, bf16[128,4096]{1,0:T(8,128)(2,1)S(1)}, u32[]{:S(2)}, u32[]{:S(2)}) collective-permute-start(bf16[128,4096]{1,0:T(8,128)(2,1)S(1)} %copy-done.9), channel_id=1, source_target_pairs={{0,2},{1,3},{2,0},{3,1},{4,6},{5,7},{6,4},{7,5},{8,10},{9,11},{10,... | collective-permute-start | bytes 3145736 | tf_op jit(solution)/shard_map/ppermute | solution.py:211
  136.3 46.7 %collective-permute-start.8 = (bf16[128,4096]{1,0:T(8,128)(2,1)}, bf16[128,4096]{1,0:T(8,128)(2,1)S(1)}, u32[]{:S(2)}, u32[]{:S(2)}) collective-permute-start(bf16[128,4096]{1,0:T(8,128)(2,1)} %collective-permute-done.6.refs_2_.refs_4_), channel_id=1, source_target_pairs={{0,2},{1,3},{2,0},{3,1},{4,6},{5,7},{6,4},{7,5},{8,10},{9,11},{10,... | collective-permute-start | bytes 3145736 | tf_op jit(solution)/shard_map/ppermute | solution.py:211
  137.0 57.2 %collective-permute-start.16 = (bf16[4096,128]{1,0:T(8,128)(2,1)}, bf16[4096,128]{1,0:T(8,128)(2,1)S(1)}, u32[]{:S(2)}, u32[]{:S(2)}) collective-permute-start(bf16[4096,128]{1,0:T(8,128)(2,1)} %get-tuple-element.43), channel_id=1, source_target_pairs={{8,12},{9,13},{10,14},{11,15},{24,28},{25,29},{26,30},{27,31}} | collective-permute-start | bytes 3145736 | tf_op jit(solution)/shard_map/ppermute | solution.py:222
  137.8 58.9 %collective-permute-start.17 = (bf16[4096,128]{1,0:T(8,128)(2,1)}, bf16[4096,128]{1,0:T(8,128)(2,1)}, u32[]{:S(2)}, u32[]{:S(2)}) collective-permute-start(bf16[4096,128]{1,0:T(8,128)(2,1)} %get-tuple-element.44), channel_id=1, source_target_pairs={{4,0},{5,1},{6,2},{7,3},{20,16},{21,17},{22,18},{23,19}} | collective-permute-start | bytes 3145736 | tf_op jit(solution)/shard_map/ppermute | solution.py:222
  139.1 59.1 %collective-permute-start.29 = (bf16[4096,128]{1,0:T(8,128)(2,1)}, bf16[4096,128]{1,0:T(8,128)(2,1)}, u32[]{:S(2)}, u32[]{:S(2)}) collective-permute-start(bf16[4096,128]{1,0:T(8,128)(2,1)} %get-tuple-element.47), channel_id=1, source_target_pairs={{8,12},{9,13},{10,14},{11,15},{24,28},{25,29},{26,30},{27,31}} | collective-permute-start | bytes 3145736 | tf_op jit(solution)/shard_map/ppermute | solution.py:222
  161.0 37.2 %collective-permute-start.30 = (bf16[4096,128]{1,0:T(8,128)(2,1)}, bf16[4096,128]{1,0:T(8,128)(2,1)}, u32[]{:S(2)}, u32[]{:S(2)}) collective-permute-start(bf16[4096,128]{1,0:T(8,128)(2,1)} %get-tuple-element.48), channel_id=1, source_target_pairs={{4,0},{5,1},{6,2},{7,3},{20,16},{21,17},{22,18},{23,19}} | collective-permute-start | bytes 3145736 | tf_op jit(solution)/shard_map/ppermute | solution.py:222
  198.1 24.1 %collective-permute-start.25 = (bf16[4096,128]{1,0:T(8,128)(2,1)S(1)}, bf16[4096,128]{1,0:T(8,128)(2,1)}, u32[]{:S(2)}, u32[]{:S(2)}) collective-permute-start(bf16[4096,128]{1,0:T(8,128)(2,1)S(1)} %select_select_fusion.3.refs_8_), channel_id=1, source_target_pairs={{0,1},{1,0},{2,3},{3,2},{4,5},{5,4},{6,7},{7,6},{8,9},{9,8},{10,11... | collective-permute-start | bytes 3145736 | tf_op jit(solution)/shard_map/ppermute | solution.py:211
  199.8 28.7 %collective-permute-start.31 = (bf16[4096,128]{1,0:T(8,128)(2,1)S(1)}, bf16[4096,128]{1,0:T(8,128)(2,1)S(1)}, u32[]{:S(2)}, u32[]{:S(2)}) collective-permute-start(bf16[4096,128]{1,0:T(8,128)(2,1)S(1)} %select_select_fusion.2.refs_8_), channel_id=1, source_target_pairs={{0,1},{1,0},{2,3},{3,2},{4,5},{5,4},{6,7},{7,6},{8,9},{9,8},{10,11... | collective-permute-start | bytes 3145736 | tf_op jit(solution)/shard_map/ppermute | solution.py:211
  206.9 31.2 %collective-permute-start.35 = (bf16[128,1536]{1,0:T(8,128)(2,1)}, bf16[128,1536]{1,0:T(8,128)(2,1)}, u32[]{:S(2)}, u32[]{:S(2)}) collective-permute-start(bf16[128,1536]{1,0:T(8,128)(2,1)} %get-tuple-element.66), channel_id=1, source_target_pairs={{0,2},{1,3},{2,0},{3,1},{4,6},{5,7},{6,4},{7,5},{8,10},{9,11},{10,... | collective-permute-start | bytes 1179656 | tf_op jit(solution)/shard_map/ppermute | solution.py:211
  (41 other events, 490.5 us)

commit v2 on v1

--- a/solution.py
+++ b/solution.py
@@ -30,6 +30,39 @@
         input_output_aliases={i: i for i in range(len(values))},
         cost_estimate=cost(weight),
     )(*values, *waits)
+
+
+def pick_kernel(count, which_ref, *refs):
+    outs = refs[count:]
+    part = outs[0].shape[1]
+    for n, ref in enumerate(refs[:count]):
+
+        @pl.when(which_ref[0] == n)
+        def _():
+            for i, out in enumerate(outs):
+                out[...] = ref[:, i * part : (i + 1) * part]
+
+
+def pick(choices, which, rows, parts=1):
+    width = choices[0].shape[1]
+    part = width // parts
+    tile = min(1024, rows)
+
+    def block_of(n):
+        return pl.BlockSpec((tile, width), lambda i, s: (jnp.where(s[0] == n, i, 0), 0))
+
+    return pl.pallas_call(
+        functools.partial(pick_kernel, len(choices)),
+        grid_spec=pltpu.PrefetchScalarGridSpec(
+            num_scalar_prefetch=1,
+            grid=(rows // tile,),
+            in_specs=[block_of(n) for n in range(len(choices))],
+            out_specs=[pl.BlockSpec((tile, part), lambda i, s: (i, 0))] * parts,
+        ),
+        out_shape=[jax.ShapeDtypeStruct((rows, part), choices[0].dtype)] * parts,
+        compiler_params=pltpu.CompilerParams(vmem_limit_bytes=16 << 20),
+        cost_estimate=cost(0.1),
+    )(jnp.reshape(which, (1,)).astype(jnp.int32), *choices)
 
 
 def product_of(key, value):
@@ -99,8 +132,8 @@
             out_specs=[pl.BlockSpec((rows, tile), lambda i, s: (0, i))] * blocks,
         ),
         out_shape=[jax.ShapeDtypeStruct((rows, count), BF16)] * blocks,
-        compiler_params=pltpu.CompilerParams(vmem_limit_bytes=56 << 20),
-        cost_estimate=cost(0),
+        compiler_params=pltpu.CompilerParams(vmem_limit_bytes=60 << 20),
+        cost_estimate=cost(0.1),
     )(jnp.reshape(start, (1,)).astype(jnp.int32), rings, skip, queries, key_proj, value_proj, before, *waits)
 
 
@@ -108,9 +141,9 @@
     return jnp.roll(filter_taps[:, ::-1], 1, axis=1).astype(F32)
 
 
-def project_kernel(count, weight_count, *refs):
-    rows, weights = refs[:count], refs[count : count + weight_count]
-    keep_ref, send_ref, total = refs[-3:]
+def project_kernel(row_count, choices, weight_count, outs, which_ref, *refs):
+    rows, weights = refs[:row_count], refs[row_count : row_count + choices * weight_count]
+    out_refs, total = refs[-1 - outs : -1], refs[-1]
     step = pl.program_id(0)
 
     @pl.when(step == 0)
@@ -118,36 +151,48 @@
         total[...] = jnp.zeros_like(total)
 
     left = jnp.concatenate([r[...] for r in rows], axis=0)
-    right = jnp.concatenate([w[...] for w in weights], axis=1)
-    total[...] += jnp.dot(left, right, preferred_element_type=F32)
+    for n in range(choices):
+
+        @pl.when(which_ref[0] == n)
+        def _():
+            right = jnp.concatenate([w[...] for w in weights[n::choices]], axis=1)
+            total[...] += jnp.dot(left, right, preferred_element_type=F32)
 
     @pl.when(step == pl.num_programs(0) - 1)
     def _():
-        half = total.shape[0] // 2
-        keep_ref[...] = total[:half, :]
-        send_ref[...] = total[half:, :].astype(BF16)
-
-
-def project(rows, weights, weight, waits=()):
+        part = out_refs[0].shape[0]
+        for i, out_ref in enumerate(out_refs):
+            out_ref[...] = total[i * part : (i + 1) * part, :].astype(out_ref.dtype)
+
+
+def project(rows, weights, dtypes, waits=(), which=0):
     depth = rows[0].shape[1]
     height = sum(r.shape[0] for r in rows)
-    width = sum(w.shape[1] for w in weights)
+    widths = [w[0].shape[1] for w in weights]
     tile = min(1024, depth)
-    return pl.pallas_call(
-        functools.partial(project_kernel, len(rows), len(weights)),
-        grid=(depth // tile,),
-        in_specs=[pl.BlockSpec((r.shape[0], tile), lambda k: (0, k)) for r in rows]
-        + [pl.BlockSpec((tile, w.shape[1]), lambda k: (k, 0)) for w in weights]
-        + [pl.BlockSpec(memory_space=pl.ANY)] * len(waits),
-        out_specs=[pl.BlockSpec((height // 2, width), lambda k: (0, 0))] * 2,
-        out_shape=[
-            jax.ShapeDtypeStruct((height // 2, width), F32),
-            jax.ShapeDtypeStruct((height // 2, width), BF16),
-        ],
-        scratch_shapes=[pltpu.VMEM((height, width), F32)],
-        compiler_params=pltpu.CompilerParams(vmem_limit_bytes=40 << 20),
-        cost_estimate=cost(weight),
-    )(*rows, *weights, *waits)
+    choices = len(weights[0])
+
+    def weight_spec(width, n):
+        if choices == 1:
+            return pl.BlockSpec((tile, width), lambda k, s: (k, 0))
+        return pl.BlockSpec((tile, width), lambda k, s: (jnp.where(s[0] == n, k, 0), 0))
+
+    part = (height // len(dtypes), sum(widths))
+    return pl.pallas_call(
+        functools.partial(project_kernel, len(rows), choices, len(weights), len(dtypes)),
+        grid_spec=pltpu.PrefetchScalarGridSpec(
+            num_scalar_prefetch=1,
+            grid=(depth // tile,),
+            in_specs=[pl.BlockSpec((r.shape[0], tile), lambda k, s: (0, k)) for r in rows]
+            + [weight_spec(width, n) for width in widths for n in range(choices)]
+            + [pl.BlockSpec(memory_space=pl.ANY)] * len(waits),
+            out_specs=[pl.BlockSpec(part, lambda k, s: (0, 0))] * len(dtypes),
+            scratch_shapes=[pltpu.VMEM((height, sum(widths)), F32)],
+        ),
+        out_shape=[jax.ShapeDtypeStruct(part, dtype) for dtype in dtypes],
+        compiler_params=pltpu.CompilerParams(vmem_limit_bytes=60 << 20),
+        cost_estimate=cost(1),
+    )(jnp.full((1,), which, jnp.int32), *rows, *[w for group in weights for w in group], *waits)
 
 
 def settle_kernel(keep_ref, arrived_ref, *refs):
@@ -241,70 +286,66 @@
 
     last = seq_len - rows
     shards = planes * 4
-    edge = [w * shards + i for w in range(2) for i in range(shards - 1)]
-    turn = [i for i in edge if i % 4 == 3]
-
-    def outgoing(start):
-        return product_of(
+    edge = [(w * shards + i, w * shards + i + 1) for w in range(2) for i in range(shards - 1)]
+
+    def outgoing(start, spare):
+        product = product_of(
             lax.dynamic_slice(key_proj, (last, start), (rows, half)),
             lax.dynamic_slice(value_proj, (last, start), (rows, half)),
         )
-
-    before_own = lax.ppermute(outgoing(window * half), EVERY, [(i, i + 1) for i in edge])
-    leaving = outgoing((1 - window) * half)
-    before_theirs = lax.ppermute(leaving, EVERY, [(i, i + 1) for i in edge if i not in turn])
-    passing = lax.ppermute(leaving, EVERY, [(i, i - 2) for i in turn])
-    passing = lax.ppermute(passing, EVERY, [(i - 2, i + 1) for i in turn])
-    before_theirs = jnp.where(side + section == 0, passing, before_theirs)
+        return jnp.pad(product, ((0, spare), (0, 0)))
+
+    before_own = lax.ppermute(outgoing(window * half, 32), EVERY, edge)
+    before_theirs = lax.ppermute(outgoing((1 - window) * half, 16), EVERY, edge)
 
     mine = lax.dynamic_slice_in_dim(out_weight, window * half, half, 0)
-    cuts = [mine[:, : mine.shape[1] // 2], mine[:, mine.shape[1] // 2 :]]
-    got = [{}, {}]
-    ends = [[c, c] for c in cuts]
-
-    def hold(cuts_held, s, *waits):
-        held = after([v for cut in cuts_held for v in ends[cut]], *waits)
-        for n, cut in enumerate(cuts_held):
-            ends[cut] = held[2 * n : 2 * n + 2]
-            got[cut][-1, s], got[cut][1, s] = ends[cut]
-
-    def forward(cut, s):
-        up, down = ends[cut]
-        up = along(up, planes, range(s - 1, planes - 1), 1, 4)
-        down = along(down, planes, range(1, planes - s + 1), -1, 4)
-        got[cut][1, s], got[cut][-1, s] = down, up
-        ends[cut] = [up, down]
-
-    forward(0, 1)
-    forward(1, 1)
-    order = arrivals(planes)
-
-    def slot(cut, j):
-        value = got[cut][order[0][j]]
-        for z in range(1, planes):
-            value = jnp.where(plane == z, got[cut][order[z][j]], value)
-        return value
+    (mine,) = after([mine], before_own)
+    got = {}
+
+    def forward(s, up, down):
+        got[-1, s] = along(up, planes, range(s - 1, planes - 1), 1, 4)
+        got[1, s] = along(down, planes, range(1, planes - s + 1), -1, 4)
+
+    def hold(s, *waits):
+        got[-1, s], got[1, s] = after([got[-1, s], got[1, s]], *waits)
+
+    def chosen(j, among, parts=1):
+        names = sorted({order[z][j] for z in among})
+        which = sum(jnp.where(plane == z, names.index(order[z][j]), 0) for z in among)
+        return pick([got[name] for name in names], which, half, parts)
 
     def slot_place(j):
         return sum(jnp.where(plane == z, z + order[z][j][0] * order[z][j][1], 0) for z in range(planes))
+
+    def both(value):
+        return [value, swapped(value, 1, devices)]
+
+    order = arrivals(planes)
+    everywhere, inner = list(range(planes)), list(range(1, planes - 1))
+    forward(1, mine, mine)
+    early = both(mine)
 
     rings, skip = rings_of(filter_taps), skip_gain[None, :]
     args = (rings, skip, queries, key_proj, value_proj)
     firsts = gate(*args, before_own, window, half)[::-1]
     crossed = [swapped(f, 2, devices) for f in firsts]
-    theirs = gate(*args, before_theirs, 1 - window, half, firsts)[::-1]
-    seconds = [swapped(t, devices // 2, devices) for t in theirs]
-    hold([0, 1], 1, *theirs)
-    forward(0, 2)
-    forward(1, 2)
-    marker = after([jnp.zeros((8, LANES), F32)], crossed[0], weight=1)
-    for s in range(3, planes):
-        hold([0], s - 1, *marker)
-        forward(0, s)
-        hold([1], s - 1, crossed[-1], seconds[0])
-        forward(1, s)
+    theirs = gate(*args, before_theirs, 1 - window, half, [*firsts, early[1]])[::-1]
+    hold(1, *theirs)
+    seconds = [swapped(theirs[0], devices // 2, devices)]
+    for t in theirs[1:]:
+        seconds += [swapped(*after([t], crossed[0]), devices // 2, devices)]
     far = [swapped(o, 2, devices) for o in seconds]
+    for s in range(2, planes - 1):
+        forward(s, got[-1, s - 1], got[1, s - 1])
+        early += both(*after(chosen(s - 2, everywhere), seconds[0], crossed[-1]))
+        hold(s, far[0], seconds[-1])
     gathered = list(zip(firsts, crossed, seconds, far))
+
+    (middle,) = after(chosen(planes - 2, inner), early[-1])
+    to_ends = [(w * shards + p * 4 + i, w * shards + q * 4 + i) for w in range(2) for i in range(4)
+               for p, q in ((1, 0), (planes - 2, planes - 1))]
+    last_arrived = lax.ppermute(middle, EVERY, to_ends)
+    at_end = jnp.where((plane == 0) | (plane == planes - 1), 0, 1)
 
     def sent_back(send):
         return swapped(send, devices // 2, devices)
@@ -313,33 +354,37 @@
         near, far_rows = settle(keep, arrived, waits)
         return [near, swapped(far_rows, 2, devices)]
 
-    def both(value):
-        return [value, swapped(value, 1, devices)]
-
     place = jnp.stack([side * 2 + section, side * 2 + 1 - section, 2 - side * 2 + section, 3 - side * 2 - section])
     place = place.astype(jnp.int32)
-    early = both(mine)
-    for j in range(planes - 2):
-        pairs = [both(slot(cut, j)) for cut in range(2)]
-        early += [pairs[0][0], pairs[1][0], pairs[0][1], pairs[1][1]]
-    early_places = jnp.stack([plane] + [slot_place(j) for j in range(planes - 2)]).astype(jnp.int32)
-    total, sends, arrivals_back = None, [], []
-    last_slots = []
+    def places(slots):
+        return jnp.stack([slot_place(j) if j >= 0 else plane for j in slots]).astype(jnp.int32)
+
+    sums = []
+
+    def summed(rows, weights):
+        keep, send = project(rows, weights, [F32, BF16], [v for _, v, _ in sums[-1:]])
+        sums.append((keep, send, sent_back(send)))
+
+    single = [[w] for w in early]
+    for pieces in gathered:
+        summed(pieces, single)
+    halves = [both(cut) for cut in chosen(planes - 3, everywhere, 2)]
+    everyone = [gathered[blocks - 1 - b][p] for p in range(4) for b in range(blocks)]
+    summed(everyone, [[pair[c]] for c in range(2) for pair in halves])
+    parts = [shared(keep, arrived) for keep, _, arrived in sums]
+
+    middle = both(middle)
+    last_arrived = both(*after([last_arrived], parts[0][1], sums[blocks - 1][2], sums[blocks][1], middle[1]))
+    ends = list(zip(last_arrived, middle))
+    (send,) = project(everyone[2 * blocks :], ends, [BF16], [], at_end)
+    (keep,) = project(everyone[: 2 * blocks], ends, [F32], [send], at_end)
+
+    total = None
     for i, block in enumerate(reversed(range(blocks))):
-        keep, send = project(gathered[i], early, 1 if i else 2, sends[-1:])
-        sends.append(send)
-        arrivals_back.append(sent_back(send))
-        total = add_slots(residual, total, [shared(keep, arrivals_back[-1])], block, early_places, planes - 1, place)
-        if i < 2:
-            hold([i], planes - 1, far[i], send)
-            last_slots.append(both(slot(i, planes - 2)))
-    everyone = [gathered[blocks - 1 - b][p] for p in range(4) for b in range(blocks)]
-    late = []
-    for cut in range(2):
-        keep, send = project(everyone, last_slots[cut], 4, [sends[-1], arrivals_back[cut]])
-        sends.append(send)
-        late.append(shared(keep, sent_back(send), *([total] if cut else [])))
-    return add_slots(residual, total, late, 0, slot_place(planes - 2)[None].astype(jnp.int32), 1, place)
+        total = add_slots(residual, total, [parts[i]], block, places(range(-1, planes - 3)), planes - 2, place)
+    total = add_slots(residual, total, [parts[blocks]], 0, places([planes - 3]), 1, place)
+    last_part = shared(keep, sent_back(send), total)
+    return add_slots(residual, total, [last_part], 0, places([planes - 2]), 1, place)
 
 
 def general(queries, key_proj, value_proj, filter_taps, skip_gain, out_weight, residual):
@@ -361,7 +406,7 @@
     sizes = mesh.shape
     fits = sizes["groups"] == 2 and sizes["chan"] == 1 and sizes["section"] == 2 and sizes["seq"] % 2 == 0
     return jax.shard_map(
-        paired if fits and sizes["seq"] >= 6 else general,
+        paired if fits and sizes["seq"] >= 8 else general,
         mesh=mesh,
         in_specs=(
             P(("groups", "seq", "section"), "chan"),

time: 257 us -> 237 us (0.922)
  starting transfers between devices: 77.6 us -> 54.6 us
  Pallas kernels: 74.6 us -> 89.6 us
  waiting for transfers between devices: 74 us -> 63.5 us
  other arithmetic: 13.6 us -> 4.86 us
  local copies, waits for them, and re-layouts: 15.5 us -> 22.7 us
    pallas_call x4 -> x8, Pallas kernels: 32.5 us -> 49.7 us  [the longest x5 42.2 us: project(): pl.pallas_call(functools.partial(project_kernel, len(rows), choices, len(...]
    ppermute x12 -> x4, starting transfers between devices: 22.2 us -> 10.1 us  [along(): return lax.ppermute(value, EVERY, pairs)]
    ppermute x21 -> x20, waiting for transfers between devices: 54.5 us -> 42.8 us  [swapped(): return lax.ppermute(value, EVERY, [(d, d ^ bit) for d in range(devices)])]
    unnamed x56 -> x64, local copies, waits for them, and re-layouts: 8.19 us -> 19.2 us
    select_n x5 -> x0, other arithmetic: 8.49 us -> none  [the longest x4 7.32 us: slot(): value = jnp.where(plane == z, got[cut][order[z][j]], value)]
    ppermute x21 -> x20, starting transfers between devices: 45.2 us -> 37.6 us  [swapped(): return lax.ppermute(value, EVERY, [(d, d ^ bit) for d in range(devices)])]
    ppermute x4 -> x3, waiting for transfers between devices: 0.01 us -> 6.5 us  [the longest x1 5.41 us: paired(): last_arrived = lax.ppermute(middle, EVERY, to_ends)]
    ppermute x12 -> x4, waiting for transfers between devices: 19.4 us -> 14.2 us  [along(): return lax.ppermute(value, EVERY, pairs)]
  transfers between devices with their start and end apart: 37 -> 27, of which waited for: 10 -> 11; matrix products, arithmetic and copies ran while one was open for 6% -> 2% of each run, Pallas kernels for 29% -> 37%
where the time goes in v2:
time: 237 us; the launch traced here: 236 us
  Pallas kernels  89.6 us (38%)
  waiting for transfers between devices  63.5 us (27%)
  starting transfers between devices  54.6 us (23%)
  local copies, waits for them, and re-layouts  22.7 us (10%)
  other arithmetic  4.86 us (2%)
    ppermute x20, waiting for transfers between devices, swapped(): return lax.ppermute(value, EVERY, [(d, d ^ bit) for d in range(devices)])  42.8 us
    pallas_call x5, Pallas kernels, project(): pl.pallas_call(functools.partial(project_kernel, len(rows), choices, len(...  42.2 us
    ppermute x20, starting transfers between devices, swapped(): return lax.ppermute(value, EVERY, [(d, d ^ bit) for d in range(devices)])  37.6 us
    pallas_call x2, Pallas kernels, gate(): pl.pallas_call(functools.partial(gate_kernel, per_group, blocks), grid_sp...  28.6 us
    unnamed x64, local copies, waits for them, and re-layouts  19.2 us
    ppermute x4, waiting for transfers between devices, along(): return lax.ppermute(value, EVERY, pairs)  14.2 us
    ppermute x4, starting transfers between devices, along(): return lax.ppermute(value, EVERY, pairs)  10.1 us
    pallas_call x3, Pallas kernels, pick(): pl.pallas_call(functools.partial(pick_kernel, len(choices)), grid_spec=pl...  7.52 us
  transfers between devices with their start and end apart: 27, of which 11 were waited for; matrix products, arithmetic and copies ran while one was open for 2% of the time, Pallas kernels for 37%

profile of v2, /device:TPU:0, one launch (start us, length us, event | category | flops | bytes accessed | tf_op | source)
XLA Modules:
  0.0 235.6 jit_solution(5675959289050039235)
XLA Ops:
  0.0 3.1 %multiply_convert_fusion = (bf16[128,4096]{1,0:T(8,128)(2,1)S(1)}, bf16[128,4096]{1,0:T(8,128)(2,1)S(1)}) fusion(bf16[256,8192]{1,0:T(8,128)(2,1)} %v_ref.3, s32[]{:T(128)S(6)} %select_n.77, bf16[256,8192]{1,0:T(8,128)(2,1)} %k_ref.3, s32[]{:T(128)S(6)} %select_n.75), kind=kLoop, calls=%fused_computation | loop fusion | flops 4194304 | bytes 6291464 | tf_op jit(solution)/shard_map/convert_element_type | solution.py:69
  3.3 2.4 %collective-permute-start = (bf16[160,4096]{1,0:T(8,128)(2,1)S(1)}, bf16[160,4096]{1,0:T(8,128)(2,1)S(1)}, u32[]{:S(2)}, u32[]{:S(2)}) collective-permute-start(bf16[160,4096]{1,0:T(8,128)(2,1)S(1)} %pad.8), channel_id=1, source_target_pairs={{0,1},{1,2},{2,3},{3,4},{4,5},{5,6},{6,7},{7,8},{8,9},{9,10},{10,1... | collective-permute-start | bytes 3932168 | tf_op jit(solution)/shard_map/ppermute | solution.py:298
  9.4 14.5 %collective-permute-start.6 = (bf16[4096,256]{1,0:T(8,128)(2,1)}, bf16[4096,256]{1,0:T(8,128)(2,1)}, u32[]{:S(2)}, u32[]{:S(2)}) collective-permute-start(bf16[4096,256]{1,0:T(8,128)(2,1)} %shard_map.74.refs_4_), channel_id=1, source_target_pairs={{0,1},{1,0},{2,3},{3,2},{4,5},{5,4},{6,7},{7,6},{8,9},{9,8},{10,11... | collective-permute-start | bytes 6291464 | tf_op jit(solution)/shard_map/ppermute | solution.py:256
  24.0 2.9 %collective-permute-start.5 = (bf16[144,4096]{1,0:T(8,128)(2,1)S(1)}, bf16[144,4096]{1,0:T(8,128)(2,1)}, u32[]{:S(2)}, u32[]{:S(2)}) collective-permute-start(bf16[144,4096]{1,0:T(8,128)(2,1)S(1)} %pad.9), channel_id=1, source_target_pairs={{0,1},{1,2},{2,3},{3,4},{4,5},{5,6},{6,7},{7,8},{8,9},{9,10},{10,1... | collective-permute-start | bytes 3538952 | tf_op jit(solution)/shard_map/ppermute | solution.py:299
  28.2 5.5 %collective-permute-start.3 = (bf16[4096,256]{1,0:T(8,128)(2,1)}, bf16[4096,256]{1,0:T(8,128)(2,1)S(1)}, u32[]{:S(2)}, u32[]{:S(2)}) collective-permute-start(bf16[4096,256]{1,0:T(8,128)(2,1)} %shard_map.74.refs_4_), channel_id=1, source_target_pairs={{0,4},{1,5},{2,6},{3,7},{4,8},{5,9},{6,10},{7,11},{8,12},{9,13},{1... | collective-permute-start | bytes 6291464 | tf_op jit(solution)/shard_map/ppermute | solution.py:267
  37.1 14.3 %shard_map.73 = (bf16[128,4096]{1,0:T(8,128)(2,1)}, bf16[128,4096]{1,0:T(8,128)(2,1)}) custom-call(s32[1]{0:T(128)} %bitcast.6.start_ref, f32[512,128]{1,0:T(8,128)} %maximum_convert_fusion.ring_ref, f32[1,8192]{1,0:T(1,128)} %bitcast.17, bf16[256,8192]{1,0:T(8,128)(2,1)} %q_ref.3, bf16[256,8192]{1,0:T(8,128)(2,1)} %k_ref.3, bf16[256,8192]{1,0:T(8,128)(2,1)} %v_ref.3, ...), custom_call_target="tpu_custom_call" | custom-call | flops 110000000 | bytes 1 | tf_op jit(solution)/shard_map/pallas_call | solution.py:118
  52.4 14.3 %shard_map.75 = (bf16[128,4096]{1,0:T(8,128)(2,1)}, bf16[128,4096]{1,0:T(8,128)(2,1)}) custom-call(s32[1]{0:T(128)} %bitcast.9.start_ref, f32[512,128]{1,0:T(8,128)} %maximum_convert_fusion.ring_ref, f32[1,8192]{1,0:T(1,128)} %bitcast.18, bf16[256,8192]{1,0:T(8,128)(2,1)} %q_ref.3, bf16[256,8192]{1,0:T(8,128)(2,1)} %k_ref.3, bf16[256,8192]{1,0:T(8,128)(2,1)} %v_ref.3, ...), custom_call_target="tpu_custom_call" | custom-call | flops 110000000 | bytes 1 | tf_op jit(solution)/shard_map/pallas_call | solution.py:118
  69.2 8.9 %collective-permute-done.4.refs_1_ = bf16[4096,256]{1,0:T(8,128)(2,1)} collective-permute-done((bf16[4096,256]{1,0:T(8,128)(2,1)}, bf16[4096,256]{1,0:T(8,128)(2,1)}, u32[]{:S(2)}, u32[]{:S(2)}) %collective-permute-start.4) | collective-permute-done | bytes 2097184 | tf_op jit(solution)/shard_map/ppermute | solution.py:267
  89.3 3.5 %collective-permute-done.9.refs_1_.refs_2_.refs_5_ = bf16[128,4096]{1,0:T(8,128)(2,1)S(1)} collective-permute-done((bf16[128,4096]{1,0:T(8,128)(2,1)}, bf16[128,4096]{1,0:T(8,128)(2,1)S(1)}, u32[]{:S(2)}, u32[]{:S(2)}) %collective-permute-start.9) | collective-permute-done | bytes 1048608 | tf_op jit(solution)/shard_map/ppermute | solution.py:256
  94.2 5.8 %collective-permute-done.2.refs_1_.refs_3_ = bf16[128,4096]{1,0:T(8,128)(2,1)} collective-permute-done((bf16[128,4096]{1,0:T(8,128)(2,1)}, bf16[128,4096]{1,0:T(8,128)(2,1)}, u32[]{:S(2)}, u32[]{:S(2)}) %collective-permute-start.2) | collective-permute-done | bytes 1048608 | tf_op jit(solution)/shard_map/ppermute | solution.py:256
  102.2 23.1 %collective-permute-done.11.refs_3_.refs_2_.refs_4_.refs_0_ = bf16[128,4096]{1,0:T(8,128)(2,1)} collective-permute-done((bf16[128,4096]{1,0:T(8,128)(2,1)}, bf16[128,4096]{1,0:T(8,128)(2,1)}, u32[]{:S(2)}, u32[]{:S(2)}) %collective-permute-start.11) | collective-permute-done | bytes 1048608 | tf_op jit(solution)/shard_map/ppermute | solution.py:256
  126.6 4.0 %collective-permute-done.8.refs_1_ = bf16[4096,256]{1,0:T(8,128)(2,1)S(1)} collective-permute-done((bf16[4096,256]{1,0:T(8,128)(2,1)}, bf16[4096,256]{1,0:T(8,128)(2,1)S(1)}, u32[]{:S(2)}, u32[]{:S(2)}) %collective-permute-start.8) | collective-permute-done | bytes 2097184 | tf_op jit(solution)/shard_map/ppermute | solution.py:267
  140.5 2.8 %shard_map.86 = (bf16[4096,128]{1,0:T(8,128)(2,1)S(1)}, bf16[4096,128]{1,0:T(8,128)(2,1)}) custom-call(s32[1]{0:T(128)} %bitcast.11.which_ref, bf16[4096,256]{1,0:T(8,128)(2,1)S(1)} %copy-done.7, bf16[4096,256]{1,0:T(8,128)(2,1)} %get-tuple-element.35.refs_0_.refs_1_, bf16[4096,256]{1,0:T(8,128)(2,1)S(1)} %copy-done.10), custom_call_target="tpu_custom_call" | custom-call | flops 110000000 | bytes 1 | tf_op jit(solution)/shard_map/pallas_call | solution.py:54
  143.8 9.2 %shard_map.83 = (f32[256,1024]{1,0:T(8,128)}, bf16[256,1024]{1,0:T(8,128)(2,1)}) custom-call(s32[1]{0:T(128)} %constant.37.clone.1.which_ref, bf16[128,4096]{1,0:T(8,128)(2,1)} %get-tuple-element.30.rest_0_.refs_0_.refs_1_, bf16[128,4096]{1,0:T(8,128)(2,1)} %collective-permute-done.2.refs_1_.refs_3_, bf16[128,4096]{1,0:T(8,128)(2,1)} %copy-done.26, ...), custom_call_target="tpu_custom_call" | custom-call | flops 1100000000 | bytes 1 | tf_op jit(solution)/shard_map/pallas_call | solution.py:181
  154.6 9.2 %shard_map.85 = (f32[256,1024]{1,0:T(8,128)}, bf16[256,1024]{1,0:T(8,128)(2,1)}) custom-call(s32[1]{0:T(128)} %constant.37.clone.1.which_ref, bf16[128,4096]{1,0:T(8,128)(2,1)} %get-tuple-element.29.rest_1_.refs_0_, bf16[128,4096]{1,0:T(8,128)(2,1)} %collective-permute-done.1.refs_2_.refs_1_, ...), custom_call_target="tpu_custom_call" | custom-call | flops 1100000000 | bytes 1 | tf_op jit(solution)/shard_map/pallas_call | solution.py:181
  163.8 3.6 %collective-permute-done.14.arrived_ref = bf16[256,1024]{1,0:T(8,128)(2,1)S(1)} collective-permute-done((bf16[256,1024]{1,0:T(8,128)(2,1)}, bf16[256,1024]{1,0:T(8,128)(2,1)S(1)}, u32[]{:S(2)}, u32[]{:S(2)}) %collective-permute-start.14) | collective-permute-done | bytes 524320 | tf_op jit(solution)/shard_map/ppermute | solution.py:256
  170.0 2.6 %collective-permute-start.15 = (bf16[128,1024]{1,0:T(8,128)(2,1)S(1)}, bf16[128,1024]{1,0:T(8,128)(2,1)S(1)}, u32[]{:S(2)}, u32[]{:S(2)}) collective-permute-start(bf16[128,1024]{1,0:T(8,128)(2,1)S(1)} %get-tuple-element.39), channel_id=1, source_target_pairs={{0,2},{1,3},{2,0},{3,1},{4,6},{5,7},{6,4},{7,5},{8,10},{9,11},{10,... | collective-permute-start | bytes 786440 | tf_op jit(solution)/shard_map/ppermute | solution.py:256
  172.6 9.4 %shard_map.87 = (f32[512,512]{1,0:T(8,128)}, bf16[512,512]{1,0:T(8,128)(2,1)}) custom-call(s32[1]{0:T(128)} %constant.37.clone.1.which_ref, bf16[128,4096]{1,0:T(8,128)(2,1)} %get-tuple-element.29.rest_1_.refs_0_, bf16[128,4096]{1,0:T(8,128)(2,1)} %get-tuple-element.30.rest_0_.refs_0_.refs_1_, bf16[128,4096]{1,0:T(8,128)(2,1)} %collective-permute-done.1.refs_2_.refs_1_, ...), custom_call_target="tpu_custom_call" | custom-call | flops 1100000000 | bytes 1 | tf_op jit(solution)/shard_map/pallas_call | solution.py:181
  182.1 5.4 %collective-permute-done.13.refs_0_ = bf16[4096,256]{1,0:T(8,128)(2,1)} collective-permute-done((bf16[4096,256]{1,0:T(8,128)(2,1)}, bf16[4096,256]{1,0:T(8,128)(2,1)}, u32[]{:S(2)}, u32[]{:S(2)}) %collective-permute-start.13) | collective-permute-done | bytes 2097184 | tf_op jit(solution)/shard_map/ppermute | solution.py:347
  191.9 2.6 %collective-permute-start.25 = (bf16[128,1024]{1,0:T(8,128)(2,1)}, bf16[128,1024]{1,0:T(8,128)(2,1)}, u32[]{:S(2)}, u32[]{:S(2)}) collective-permute-start(bf16[128,1024]{1,0:T(8,128)(2,1)} %get-tuple-element.49), channel_id=1, source_target_pairs={{0,2},{1,3},{2,0},{3,1},{4,6},{5,7},{6,4},{7,5},{8,10},{9,11},{10,... | collective-permute-start | bytes 786440 | tf_op jit(solution)/shard_map/ppermute | solution.py:256
  194.5 7.1 %shard_map.89.refs_8_ = bf16[512,512]{1,0:T(8,128)(2,1)} custom-call(s32[1]{0:T(128)} %bitcast.5.which_ref, bf16[128,4096]{1,0:T(8,128)(2,1)} %collective-permute-done.11.refs_3_.refs_2_.refs_4_.refs_0_, bf16[128,4096]{1,0:T(8,128)(2,1)} %copy-done.26, bf16[128,4096]{1,0:T(8,128)(2,1)} %collective-permute-done.16.refs_3_.refs_6_.refs_2_, ...), custom_call_target="tpu_custom_call" | custom-call | flops 1100000000 | bytes 1 | tf_op jit(solution)/shard_map/pallas_call | solution.py:181
  210.1 2.4 %shard_map.94.refs_3_ = bf16[256,4096]{1,0:T(8,128)(2,1)} custom-call(s32[7]{0:T(128)S(1)} %concatenate.21.place_ref, bf16[256,4096]{1,0:T(8,128)(2,1)S(1)} %copy-done.3, bf16[128,1024]{1,0:T(8,128)(2,1)S(1)} %copy-done.23, bf16[128,1024]{1,0:T(8,128)(2,1)} %collective-permute-done.25.refs_2_, ...), custom_call_target="tpu_custom_call", output_to_operand_aliasing={{}: (4, {})} | custom-call | flops 1100000000 | bytes 1 | tf_op jit(solution)/shard_map/pallas_call | solution.py:238
  215.3 7.3 %shard_map.90.keep_ref = f32[512,512]{1,0:T(8,128)} custom-call(s32[1]{0:T(128)} %bitcast.5.which_ref, bf16[128,4096]{1,0:T(8,128)(2,1)} %get-tuple-element.29.rest_1_.refs_0_, bf16[128,4096]{1,0:T(8,128)(2,1)} %get-tuple-element.30.rest_0_.refs_0_.refs_1_, bf16[128,4096]{1,0:T(8,128)(2,1)} %collective-permute-done.1.refs_2_.refs_1_, ...), custom_call_target="tpu_custom_call" | custom-call | flops 1100000000 | bytes 1 | tf_op jit(solution)/shard_map/pallas_call | solution.py:181
  226.8 5.6 %collective-permute-done.26.refs_2_ = bf16[256,512]{1,0:T(8,128)(2,1)S(1)} collective-permute-done((bf16[256,512]{1,0:T(8,128)(2,1)S(1)}, bf16[256,512]{1,0:T(8,128)(2,1)S(1)}, u32[]{:S(2)}, u32[]{:S(2)}) %collective-permute-start.26) | collective-permute-done | bytes 262176 | tf_op jit(solution)/shard_map/ppermute | solution.py:256
  (129 shorter events, 65.6 us)
Async XLA Ops:
  9.4 43.0 %collective-permute-start.6 = (bf16[4096,256]{1,0:T(8,128)(2,1)}, bf16[4096,256]{1,0:T(8,128)(2,1)}, u32[]{:S(2)}, u32[]{:S(2)}) collective-permute-start(bf16[4096,256]{1,0:T(8,128)(2,1)} %shard_map.74.refs_4_), channel_id=1, source_target_pairs={{0,1},{1,0},{2,3},{3,2},{4,5},{5,4},{6,7},{7,6},{8,9},{9,8},{10,11... | collective-permute-start | bytes 6291464 | tf_op jit(solution)/shard_map/ppermute | solution.py:256
  24.0 28.4 %collective-permute-start.5 = (bf16[144,4096]{1,0:T(8,128)(2,1)S(1)}, bf16[144,4096]{1,0:T(8,128)(2,1)}, u32[]{:S(2)}, u32[]{:S(2)}) collective-permute-start(bf16[144,4096]{1,0:T(8,128)(2,1)S(1)} %pad.9), channel_id=1, source_target_pairs={{0,1},{1,2},{2,3},{3,4},{4,5},{5,6},{6,7},{7,8},{8,9},{9,10},{10,1... | collective-permute-start | bytes 3538952 | tf_op jit(solution)/shard_map/ppermute | solution.py:299
  26.9 51.2 %collective-permute-start.4 = (bf16[4096,256]{1,0:T(8,128)(2,1)}, bf16[4096,256]{1,0:T(8,128)(2,1)}, u32[]{:S(2)}, u32[]{:S(2)}) collective-permute-start(bf16[4096,256]{1,0:T(8,128)(2,1)} %shard_map.74.refs_4_), channel_id=1, source_target_pairs={{4,0},{5,1},{6,2},{7,3},{8,4},{9,5},{10,6},{11,7},{12,8},{13,9},{1... | collective-permute-start | bytes 6291464 | tf_op jit(solution)/shard_map/ppermute | solution.py:267
  28.2 51.1 %collective-permute-start.3 = (bf16[4096,256]{1,0:T(8,128)(2,1)}, bf16[4096,256]{1,0:T(8,128)(2,1)S(1)}, u32[]{:S(2)}, u32[]{:S(2)}) collective-permute-start(bf16[4096,256]{1,0:T(8,128)(2,1)} %shard_map.74.refs_4_), channel_id=1, source_target_pairs={{0,4},{1,5},{2,6},{3,7},{4,8},{5,9},{6,10},{7,11},{8,12},{9,13},{1... | collective-permute-start | bytes 6291464 | tf_op jit(solution)/shard_map/ppermute | solution.py:267
  51.4 37.9 %collective-permute-start.1 = (bf16[128,4096]{1,0:T(8,128)(2,1)}, bf16[128,4096]{1,0:T(8,128)(2,1)}, u32[]{:S(2)}, u32[]{:S(2)}) collective-permute-start(bf16[128,4096]{1,0:T(8,128)(2,1)} %get-tuple-element.29.rest_1_.refs_0_), channel_id=1, source_target_pairs={{0,2},{1,3},{2,0},{3,1},{4,6},{5,7},{6,4},{7,5},{8,10},{9,11},{10,... | collective-permute-start | bytes 3145736 | tf_op jit(solution)/shard_map/ppermute | solution.py:256
  66.7 26.0 %collective-permute-start.9 = (bf16[128,4096]{1,0:T(8,128)(2,1)}, bf16[128,4096]{1,0:T(8,128)(2,1)S(1)}, u32[]{:S(2)}, u32[]{:S(2)}) collective-permute-start(bf16[128,4096]{1,0:T(8,128)(2,1)} %get-tuple-element.31.refs_2_), channel_id=1, source_target_pairs={{0,16},{1,17},{2,18},{3,19},{4,20},{5,21},{6,22},{7,23},{8,24},{9,... | collective-permute-start | bytes 3145736 | tf_op jit(solution)/shard_map/ppermute | solution.py:256
  68.1 31.8 %collective-permute-start.2 = (bf16[128,4096]{1,0:T(8,128)(2,1)}, bf16[128,4096]{1,0:T(8,128)(2,1)}, u32[]{:S(2)}, u32[]{:S(2)}) collective-permute-start(bf16[128,4096]{1,0:T(8,128)(2,1)} %get-tuple-element.30.rest_0_.refs_0_.refs_1_), channel_id=1, source_target_pairs={{0,2},{1,3},{2,0},{3,1},{4,6},{5,7},{6,4},{7,5},{8,10},{9,11},{10,... | collective-permute-start | bytes 3145736 | tf_op jit(solution)/shard_map/ppermute | solution.py:256
  80.7 49.9 %collective-permute-start.8 = (bf16[4096,256]{1,0:T(8,128)(2,1)}, bf16[4096,256]{1,0:T(8,128)(2,1)S(1)}, u32[]{:S(2)}, u32[]{:S(2)}) collective-permute-start(bf16[4096,256]{1,0:T(8,128)(2,1)} %get-tuple-element.34.refs_1_), channel_id=1, source_target_pairs={{4,0},{5,1},{6,2},{7,3},{8,4},{9,5},{10,6},{11,7},{20,16},{21,17},... | collective-permute-start | bytes 6291464 | tf_op jit(solution)/shard_map/ppermute | solution.py:267
  82.0 48.6 %collective-permute-start.7 = (bf16[4096,256]{1,0:T(8,128)(2,1)}, bf16[4096,256]{1,0:T(8,128)(2,1)}, u32[]{:S(2)}, u32[]{:S(2)}) collective-permute-start(bf16[4096,256]{1,0:T(8,128)(2,1)} %get-tuple-element.33.refs_0_), channel_id=1, source_target_pairs={{4,8},{5,9},{6,10},{7,11},{8,12},{9,13},{10,14},{11,15},{20,24},{2... | collective-permute-start | bytes 6291464 | tf_op jit(solution)/shard_map/ppermute | solution.py:267
  93.7 43.5 %collective-permute-start.12 = (bf16[4096,256]{1,0:T(8,128)(2,1)}, bf16[4096,256]{1,0:T(8,128)(2,1)}, u32[]{:S(2)}, u32[]{:S(2)}) collective-permute-start(bf16[4096,256]{1,0:T(8,128)(2,1)} %shard_map.81.refs_6_), channel_id=1, source_target_pairs={{0,1},{1,0},{2,3},{3,2},{4,5},{5,4},{6,7},{7,6},{8,9},{9,8},{10,11... | collective-permute-start | bytes 6291464 | tf_op jit(solution)/shard_map/ppermute | solution.py:256
  100.0 25.3 %collective-permute-start.11 = (bf16[128,4096]{1,0:T(8,128)(2,1)}, bf16[128,4096]{1,0:T(8,128)(2,1)}, u32[]{:S(2)}, u32[]{:S(2)}) collective-permute-start(bf16[128,4096]{1,0:T(8,128)(2,1)} %shard_map.77), channel_id=1, source_target_pairs={{0,16},{1,17},{2,18},{3,19},{4,20},{5,21},{6,22},{7,23},{8,24},{9,... | collective-permute-start | bytes 3145736 | tf_op jit(solution)/shard_map/ppermute | solution.py:256
  101.4 25.2 %collective-permute-start.10 = (bf16[128,4096]{1,0:T(8,128)(2,1)S(1)}, bf16[128,4096]{1,0:T(8,128)(2,1)S(1)}, u32[]{:S(2)}, u32[]{:S(2)}) collective-permute-start(bf16[128,4096]{1,0:T(8,128)(2,1)S(1)} %copy-done.27), channel_id=1, source_target_pairs={{0,2},{1,3},{2,0},{3,1},{4,6},{5,7},{6,4},{7,5},{8,10},{9,11},{10,... | collective-permute-start | bytes 3145736 | tf_op jit(solution)/shard_map/ppermute | solution.py:256
  125.3 27.7 %collective-permute-start.16 = (bf16[128,4096]{1,0:T(8,128)(2,1)}, bf16[128,4096]{1,0:T(8,128)(2,1)}, u32[]{:S(2)}, u32[]{:S(2)}) collective-permute-start(bf16[128,4096]{1,0:T(8,128)(2,1)} %collective-permute-done.11.refs_3_.refs_2_.refs_4_.refs_0_), channel_id=1, source_target_pairs={{0,2},{1,3},{2,0},{3,1},{4,6},{5,7},{6,4},{7,5},{8,10},{9,11},{10,... | collective-permute-start | bytes 3145736 | tf_op jit(solution)/shard_map/ppermute | solution.py:256
  137.3 44.8 %collective-permute-start.20 = (bf16[4096,256]{1,0:T(8,128)(2,1)}, bf16[4096,256]{1,0:T(8,128)(2,1)}, u32[]{:S(2)}, u32[]{:S(2)}) collective-permute-start(bf16[4096,256]{1,0:T(8,128)(2,1)} %shard_map.82.refs_5_), channel_id=1, source_target_pairs={{0,1},{1,0},{2,3},{3,2},{4,5},{5,4},{6,7},{7,6},{8,9},{9,8},{10,11... | collective-permute-start | bytes 6291464 | tf_op jit(solution)/shard_map/ppermute | solution.py:256
  137.3 50.2 %collective-permute-start.13 = (bf16[4096,256]{1,0:T(8,128)(2,1)}, bf16[4096,256]{1,0:T(8,128)(2,1)}, u32[]{:S(2)}, u32[]{:S(2)}) collective-permute-start(bf16[4096,256]{1,0:T(8,128)(2,1)} %shard_map.82.refs_5_), channel_id=1, source_target_pairs={{4,0},{8,12},{5,1},{9,13},{6,2},{10,14},{7,3},{11,15},{20,16},{24,... | collective-permute-start | bytes 6291464 | tf_op jit(solution)/shard_map/ppermute | solution.py:347
  143.3 26.8 %collective-permute-start.18 = (bf16[4096,128]{1,0:T(8,128)(2,1)S(1)}, bf16[4096,128]{1,0:T(8,128)(2,1)}, u32[]{:S(2)}, u32[]{:S(2)}) collective-permute-start(bf16[4096,128]{1,0:T(8,128)(2,1)S(1)} %get-tuple-element.41.refs_8_), channel_id=1, source_target_pairs={{0,1},{1,0},{2,3},{3,2},{4,5},{5,4},{6,7},{7,6},{8,9},{9,8},{10,11... | collective-permute-start | bytes 3145736 | tf_op jit(solution)/shard_map/ppermute | solution.py:256
  143.6 29.0 %collective-permute-start.19 = (bf16[4096,128]{1,0:T(8,128)(2,1)}, bf16[4096,128]{1,0:T(8,128)(2,1)}, u32[]{:S(2)}, u32[]{:S(2)}) collective-permute-start(bf16[4096,128]{1,0:T(8,128)(2,1)} %get-tuple-element.42.refs_9_), channel_id=1, source_target_pairs={{0,1},{1,0},{2,3},{3,2},{4,5},{5,4},{6,7},{7,6},{8,9},{9,8},{10,11... | collective-permute-start | bytes 3145736 | tf_op jit(solution)/shard_map/ppermute | solution.py:256
  153.0 14.5 %collective-permute-start.14 = (bf16[256,1024]{1,0:T(8,128)(2,1)}, bf16[256,1024]{1,0:T(8,128)(2,1)S(1)}, u32[]{:S(2)}, u32[]{:S(2)}) collective-permute-start(bf16[256,1024]{1,0:T(8,128)(2,1)} %get-tuple-element.38.refs_8_), channel_id=1, source_target_pairs={{0,16},{1,17},{2,18},{3,19},{4,20},{5,21},{6,22},{7,23},{8,24},{9,... | collective-permute-start | bytes 1572872 | tf_op jit(solution)/shard_map/ppermute | solution.py:256
  167.5 14.6 %collective-permute-start.17 = (bf16[256,1024]{1,0:T(8,128)(2,1)}, bf16[256,1024]{1,0:T(8,128)(2,1)S(1)}, u32[]{:S(2)}, u32[]{:S(2)}) collective-permute-start(bf16[256,1024]{1,0:T(8,128)(2,1)} %get-tuple-element.40.refs_12_), channel_id=1, source_target_pairs={{0,16},{1,17},{2,18},{3,19},{4,20},{5,21},{6,22},{7,23},{8,24},{9,... | collective-permute-start | bytes 1572872 | tf_op jit(solution)/shard_map/ppermute | solution.py:256
  170.0 12.0 %collective-permute-start.15 = (bf16[128,1024]{1,0:T(8,128)(2,1)S(1)}, bf16[128,1024]{1,0:T(8,128)(2,1)S(1)}, u32[]{:S(2)}, u32[]{:S(2)}) collective-permute-start(bf16[128,1024]{1,0:T(8,128)(2,1)S(1)} %get-tuple-element.39), channel_id=1, source_target_pairs={{0,2},{1,3},{2,0},{3,1},{4,6},{5,7},{6,4},{7,5},{8,10},{9,11},{10,... | collective-permute-start | bytes 786440 | tf_op jit(solution)/shard_map/ppermute | solution.py:256
  187.6 15.0 %collective-permute-start.23 = (bf16[512,512]{1,0:T(8,128)(2,1)}, bf16[512,512]{1,0:T(8,128)(2,1)}, u32[]{:S(2)}, u32[]{:S(2)}) collective-permute-start(bf16[512,512]{1,0:T(8,128)(2,1)} %get-tuple-element.43.refs_3_), channel_id=1, source_target_pairs={{0,16},{1,17},{2,18},{3,19},{4,20},{5,21},{6,22},{7,23},{8,24},{9,... | collective-permute-start | bytes 1572872 | tf_op jit(solution)/shard_map/ppermute | solution.py:256
  191.9 18.2 %collective-permute-start.25 = (bf16[128,1024]{1,0:T(8,128)(2,1)}, bf16[128,1024]{1,0:T(8,128)(2,1)}, u32[]{:S(2)}, u32[]{:S(2)}) collective-permute-start(bf16[128,1024]{1,0:T(8,128)(2,1)} %get-tuple-element.49), channel_id=1, source_target_pairs={{0,2},{1,3},{2,0},{3,1},{4,6},{5,7},{6,4},{7,5},{8,10},{9,11},{10,... | collective-permute-start | bytes 786440 | tf_op jit(solution)/shard_map/ppermute | solution.py:256
  201.5 21.0 %collective-permute-start.22 = (bf16[512,512]{1,0:T(8,128)(2,1)}, bf16[512,512]{1,0:T(8,128)(2,1)}, u32[]{:S(2)}, u32[]{:S(2)}) collective-permute-start(bf16[512,512]{1,0:T(8,128)(2,1)} %shard_map.89.refs_8_), channel_id=1, source_target_pairs={{0,16},{1,17},{2,18},{3,19},{4,20},{5,21},{6,22},{7,23},{8,24},{9,... | collective-permute-start | bytes 1572872 | tf_op jit(solution)/shard_map/ppermute | solution.py:256
  205.1 8.6 %collective-permute-start.24 = (bf16[256,512]{1,0:T(8,128)(2,1)}, bf16[256,512]{1,0:T(8,128)(2,1)S(1)}, u32[]{:S(2)}, u32[]{:S(2)}) collective-permute-start(bf16[256,512]{1,0:T(8,128)(2,1)} %get-tuple-element.46), channel_id=1, source_target_pairs={{0,2},{1,3},{2,0},{3,1},{4,6},{5,7},{6,4},{7,5},{8,10},{9,11},{10,... | collective-permute-start | bytes 786440 | tf_op jit(solution)/shard_map/ppermute | solution.py:256
  (35 other events, 167.1 us)

commit v3 on v2

--- a/solution.py
+++ b/solution.py
@@ -28,41 +28,9 @@
         out_specs=[pl.BlockSpec(memory_space=pl.ANY)] * len(values),
         out_shape=[jax.ShapeDtypeStruct(v.shape, v.dtype) for v in values],
         input_output_aliases={i: i for i in range(len(values))},
+        compiler_params=pltpu.CompilerParams(vmem_limit_bytes=60 << 20),
         cost_estimate=cost(weight),
     )(*values, *waits)
-
-
-def pick_kernel(count, which_ref, *refs):
-    outs = refs[count:]
-    part = outs[0].shape[1]
-    for n, ref in enumerate(refs[:count]):
-
-        @pl.when(which_ref[0] == n)
-        def _():
-            for i, out in enumerate(outs):
-                out[...] = ref[:, i * part : (i + 1) * part]
-
-
-def pick(choices, which, rows, parts=1):
-    width = choices[0].shape[1]
-    part = width // parts
-    tile = min(1024, rows)
-
-    def block_of(n):
-        return pl.BlockSpec((tile, width), lambda i, s: (jnp.where(s[0] == n, i, 0), 0))
-
-    return pl.pallas_call(
-        functools.partial(pick_kernel, len(choices)),
-        grid_spec=pltpu.PrefetchScalarGridSpec(
-            num_scalar_prefetch=1,
-            grid=(rows // tile,),
-            in_specs=[block_of(n) for n in range(len(choices))],
-            out_specs=[pl.BlockSpec((tile, part), lambda i, s: (i, 0))] * parts,
-        ),
-        out_shape=[jax.ShapeDtypeStruct((rows, part), choices[0].dtype)] * parts,
-        compiler_params=pltpu.CompilerParams(vmem_limit_bytes=16 << 20),
-        cost_estimate=cost(0.1),
-    )(jnp.reshape(which, (1,)).astype(jnp.int32), *choices)
 
 
 def product_of(key, value):
@@ -202,7 +170,7 @@
     far_ref[...] = (keep_ref[rows:, :] + arrived_ref[rows:, :].astype(F32)).astype(BF16)
 
 
-def settle(keep, arrived, waits):
+def settle(keep, arrived, waits=()):
     rows, width = keep.shape
     tile = min(512, width)
     whole = pl.BlockSpec((rows, tile), lambda i: (0, i))
@@ -212,7 +180,7 @@
         in_specs=[whole, whole] + [pl.BlockSpec(memory_space=pl.ANY)] * len(waits),
         out_specs=[pl.BlockSpec((rows // 2, tile), lambda i: (0, i))] * 2,
         out_shape=[jax.ShapeDtypeStruct((rows // 2, width), BF16)] * 2,
-        compiler_params=pltpu.CompilerParams(vmem_limit_bytes=16 << 20),
+        compiler_params=pltpu.CompilerParams(vmem_limit_bytes=60 << 20),
         cost_estimate=cost(0),
     )(keep, arrived, *waits)
 
@@ -222,19 +190,19 @@
     span = sum(widths)
     for h, width in enumerate(widths):
         for j in range(4):
-            start = place_ref[1 + j] * span + sum(widths[:h])
+            start = place_ref[j] * span + sum(widths[:h])
             lanes = pl.ds(pl.multiple_of(start, LANES), width)
             mine = refs[1 + 2 * h + j // 2][:, (j % 2) * width : (j % 2 + 1) * width]
             out_ref[:, lanes] = (total_ref[:, lanes].astype(F32) + mine.astype(F32)).astype(BF16)
 
 
-def add_slots(residual, total, parts, block, places, slots, order):
+def add_slots(residual, total, parts, block, place, first, slots, waits=()):
     widths = [cut[0].shape[1] // slots // 2 for cut in parts]
     rows = parts[0][0].shape[0]
     span = 4 * sum(widths)
     flat = [(piece, 2 * width) for cut, width in zip(parts, widths) for piece in cut]
-    whole = pl.BlockSpec((rows, span), lambda i, s: (block, s[5 + i]))
-    so_far = [] if total is None else [total]
+    whole = pl.BlockSpec((rows, span), lambda i, s: (block, s[4 + first + i]))
+    so_far = ([] if total is None else [total]) + list(waits)
     return pl.pallas_call(
         functools.partial(add_kernel, widths),
         grid_spec=pltpu.PrefetchScalarGridSpec(
@@ -246,32 +214,14 @@
             out_specs=whole,
         ),
         out_shape=jax.ShapeDtypeStruct(residual.shape, residual.dtype),
-        input_output_aliases={2 + len(flat): 0} if so_far else {},
-        compiler_params=pltpu.CompilerParams(vmem_limit_bytes=16 << 20),
+        input_output_aliases={} if total is None else {2 + len(flat): 0},
+        compiler_params=pltpu.CompilerParams(vmem_limit_bytes=60 << 20),
         cost_estimate=cost(1),
-    )(jnp.concatenate([jnp.zeros((1,), jnp.int32), order, places]), residual, *[p for p, _ in flat], *so_far)
+    )(place, residual, *[p for p, _ in flat], *so_far)
 
 
 def swapped(value, bit, devices):
     return lax.ppermute(value, EVERY, [(d, d ^ bit) for d in range(devices)])
-
-
-def along(value, planes, sources, steps, stride):
-    per_window = planes * stride
-    pairs = [
-        (w * per_window + z * stride + i, w * per_window + (z + steps) * stride + i)
-        for w in range(2)
-        for z in sources
-        for i in range(stride)
-    ]
-    return lax.ppermute(value, EVERY, pairs)
-
-
-def arrivals(planes):
-    return [
-        [(way, s) for s in range(1, planes) for way in (1, -1) if 0 <= z + way * s < planes]
-        for z in range(planes)
-    ]
 
 
 def paired(queries, key_proj, value_proj, filter_taps, skip_gain, out_weight, residual):
@@ -295,69 +245,48 @@
         )
         return jnp.pad(product, ((0, spare), (0, 0)))
 
-    before_own = lax.ppermute(outgoing(window * half, 32), EVERY, edge)
-    before_theirs = lax.ppermute(outgoing((1 - window) * half, 16), EVERY, edge)
-
-    mine = lax.dynamic_slice_in_dim(out_weight, window * half, half, 0)
-    (mine,) = after([mine], before_own)
-    got = {}
-
-    def forward(s, up, down):
-        got[-1, s] = along(up, planes, range(s - 1, planes - 1), 1, 4)
-        got[1, s] = along(down, planes, range(1, planes - s + 1), -1, 4)
-
-    def hold(s, *waits):
-        got[-1, s], got[1, s] = after([got[-1, s], got[1, s]], *waits)
-
-    def chosen(j, among, parts=1):
-        names = sorted({order[z][j] for z in among})
-        which = sum(jnp.where(plane == z, names.index(order[z][j]), 0) for z in among)
-        return pick([got[name] for name in names], which, half, parts)
-
-    def slot_place(j):
-        return sum(jnp.where(plane == z, z + order[z][j][0] * order[z][j][1], 0) for z in range(planes))
+    before_own = lax.ppermute(outgoing(window * half, 0), EVERY, edge)
+    before_theirs = lax.ppermute(outgoing((1 - window) * half, 16), EVERY, [(p, q ^ 1) for p, q in edge])
+
+    def step(value, *pairs):
+        return lax.ppermute(
+            value, EVERY, [(w * shards + p * 4 + i, w * shards + q * 4 + i) for w in range(2) for p, q in pairs for i in range(4)]
+        )
 
     def both(value):
         return [value, swapped(value, 1, devices)]
 
-    order = arrivals(planes)
-    everywhere, inner = list(range(planes)), list(range(1, planes - 1))
-    forward(1, mine, mine)
+    mine = lax.dynamic_slice_in_dim(out_weight, window * half, half, 0)
+    rings, skip = rings_of(filter_taps), skip_gain[None, :]
+    order = [side * 2 + section, side * 2 + 1 - section, 2 - side * 2 + section, 3 - side * 2 - section]
+    slots = [[0, 1, 2, 3], [1, 0, 3, 2], [2, 2, 1, 1], [3, 3, 0, 0]]
+    held = [sum(jnp.where(plane == z, p, 0) for z, p in enumerate(slot)) for slot in slots]
+    place = jnp.stack(order + held).astype(jnp.int32)
+    (mine,) = after([mine], before_own, rings, place)
+    partner = step(mine, (0, 1), (1, 0), (2, 3), (3, 2))
+    across = step(mine, (1, 2), (2, 1))
     early = both(mine)
 
-    rings, skip = rings_of(filter_taps), skip_gain[None, :]
     args = (rings, skip, queries, key_proj, value_proj)
     firsts = gate(*args, before_own, window, half)[::-1]
     crossed = [swapped(f, 2, devices) for f in firsts]
-    theirs = gate(*args, before_theirs, 1 - window, half, [*firsts, early[1]])[::-1]
-    hold(1, *theirs)
+    before_theirs = swapped(*after([before_theirs], *firsts), 1, devices)
+    theirs = gate(*args, before_theirs, 1 - window, half, [early[1]])[::-1]
+    partner, across = after([partner, across], *theirs, crossed[0])
+    handed = step(across, (1, 0), (2, 3))
+    kept = step(partner, (1, 2), (2, 1))
+    early += both(partner)
     seconds = [swapped(theirs[0], devices // 2, devices)]
     for t in theirs[1:]:
         seconds += [swapped(*after([t], crossed[0]), devices // 2, devices)]
-    far = [swapped(o, 2, devices) for o in seconds]
-    for s in range(2, planes - 1):
-        forward(s, got[-1, s - 1], got[1, s - 1])
-        early += both(*after(chosen(s - 2, everywhere), seconds[0], crossed[-1]))
-        hold(s, far[0], seconds[-1])
+    far = [swapped(*after([seconds[0]], crossed[-1]), 2, devices)]
+    far += [swapped(swapped(o, 3, devices), 1, devices) for o in seconds[1:]]
+    handed, kept = after([handed, kept], far[0], seconds[-1])
+    final = step(kept, (1, 0), (2, 3))
+    at_end = jnp.where((plane == 0) | (plane == planes - 1), 0, 1)
     gathered = list(zip(firsts, crossed, seconds, far))
-
-    (middle,) = after(chosen(planes - 2, inner), early[-1])
-    to_ends = [(w * shards + p * 4 + i, w * shards + q * 4 + i) for w in range(2) for i in range(4)
-               for p, q in ((1, 0), (planes - 2, planes - 1))]
-    last_arrived = lax.ppermute(middle, EVERY, to_ends)
-    at_end = jnp.where((plane == 0) | (plane == planes - 1), 0, 1)
-
     def sent_back(send):
         return swapped(send, devices // 2, devices)
-
-    def shared(keep, arrived, *waits):
-        near, far_rows = settle(keep, arrived, waits)
-        return [near, swapped(far_rows, 2, devices)]
-
-    place = jnp.stack([side * 2 + section, side * 2 + 1 - section, 2 - side * 2 + section, 3 - side * 2 - section])
-    place = place.astype(jnp.int32)
-    def places(slots):
-        return jnp.stack([slot_place(j) if j >= 0 else plane for j in slots]).astype(jnp.int32)
 
     sums = []
 
@@ -368,23 +297,22 @@
     single = [[w] for w in early]
     for pieces in gathered:
         summed(pieces, single)
-    halves = [both(cut) for cut in chosen(planes - 3, everywhere, 2)]
     everyone = [gathered[blocks - 1 - b][p] for p in range(4) for b in range(blocks)]
-    summed(everyone, [[pair[c]] for c in range(2) for pair in halves])
-    parts = [shared(keep, arrived) for keep, _, arrived in sums]
-
-    middle = both(middle)
-    last_arrived = both(*after([last_arrived], parts[0][1], sums[blocks - 1][2], sums[blocks][1], middle[1]))
-    ends = list(zip(last_arrived, middle))
-    (send,) = project(everyone[2 * blocks :], ends, [BF16], [], at_end)
-    (keep,) = project(everyone[: 2 * blocks], ends, [F32], [send], at_end)
-
+    keep, send = project(everyone, list(zip(both(handed), both(across))), [F32, BF16], [sums[-1][1]], at_end)
+    sums.append((keep, send, sent_back(send)))
+    settled = [settle(k, arrived, [send] if i < blocks else []) for i, (k, _, arrived) in enumerate(sums)]
+    parts = [[n, swapped(f, 2, devices)] for n, f in settled]
+
+    kept = both(kept)
+    final = both(*after([final], parts[0][1], settled[blocks - 1][0], send, kept[1]))
+    keep, send = project(everyone, list(zip(final, kept)), [F32, BF16], [], at_end)
     total = None
     for i, block in enumerate(reversed(range(blocks))):
-        total = add_slots(residual, total, [parts[i]], block, places(range(-1, planes - 3)), planes - 2, place)
-    total = add_slots(residual, total, [parts[blocks]], 0, places([planes - 3]), 1, place)
-    last_part = shared(keep, sent_back(send), total)
-    return add_slots(residual, total, [last_part], 0, places([planes - 2]), 1, place)
+        total = add_slots(residual, total, [parts[i]], block, place, 0, 2)
+    near, far_rows = settle(keep, sent_back(send), [total])
+    last_part = [near, swapped(far_rows, 2, devices)]
+    total = add_slots(residual, total, [parts[blocks]], 0, place, 2, 1, [near])
+    return add_slots(residual, total, [last_part], 0, place, 3, 1)
 
 
 def general(queries, key_proj, value_proj, filter_taps, skip_gain, out_weight, residual):
@@ -406,7 +334,7 @@
     sizes = mesh.shape
     fits = sizes["groups"] == 2 and sizes["chan"] == 1 and sizes["section"] == 2 and sizes["seq"] % 2 == 0
     return jax.shard_map(
-        paired if fits and sizes["seq"] >= 8 else general,
+        paired if fits and sizes["seq"] == 8 else general,
         mesh=mesh,
         in_specs=(
             P(("groups", "seq", "section"), "chan"),

time: 237 us -> 225 us (0.949)
  starting transfers between devices: 54.6 us -> 41.4 us
  waiting for transfers between devices: 63.5 us -> 73.5 us
  local copies, waits for them, and re-layouts: 22.7 us -> 18.8 us
  Pallas kernels: 89.6 us -> 86.3 us
    ppermute x20 -> x22, waiting for transfers between devices: 42.8 us -> 63.6 us  [swapped(): return lax.ppermute(value, EVERY, [(d, d ^ bit) for d in range(devices)])]
    ppermute x20 -> x22, starting transfers between devices: 37.6 us -> 19 us  [swapped(): return lax.ppermute(value, EVERY, [(d, d ^ bit) for d in range(devices)])]
    ppermute x7, waiting for transfers between devices: 20.7 us -> 9.92 us  [the longest x5 9.92 us: step(): lax.ppermute(value, EVERY, [(w * shards + p * 4 + i, w * shards + q * 4 +...]
    pallas_call x3 -> x0, Pallas kernels: 7.52 us -> none  [pick(): pl.pallas_call(functools.partial(pick_kernel, len(choices)), grid_spec=pl...]
    ppermute x7, starting transfers between devices: 17.1 us -> 22.3 us  [the longest x1 10.5 us: paired(): lax.ppermute(outgoing((1 - window) * half, 16), EVERY, [(p, q ^ 1) for p,...]
    pallas_call x4, Pallas kernels: 4.15 us -> 8.63 us  [settle(): pl.pallas_call(settle_kernel, grid=(width // tile,), in_specs=[whole, who...]
    unnamed x64 -> x43, local copies, waits for them, and re-layouts: 19.2 us -> 15.1 us
    pallas_call x5 -> x4, Pallas kernels: 42.2 us -> 38.1 us  [project(): pl.pallas_call(functools.partial(project_kernel, len(rows), choices, len(...]
  transfers between devices with their start and end apart: 27 -> 29, of which waited for: 11 -> 13; matrix products, arithmetic and copies ran while one was open for 2% -> 3% of each run, Pallas kernels for 37% -> 37%
where the time goes in v3:
time: 225 us; the launch traced here: 224 us
  Pallas kernels  86.3 us (38%)
  waiting for transfers between devices  73.5 us (33%)
  starting transfers between devices  41.4 us (18%)
  local copies, waits for them, and re-layouts  18.8 us (8%)
  other arithmetic  3.94 us (2%)
    ppermute x22, waiting for transfers between devices, swapped(): return lax.ppermute(value, EVERY, [(d, d ^ bit) for d in range(devices)])  63.6 us
    pallas_call x4, Pallas kernels, project(): pl.pallas_call(functools.partial(project_kernel, len(rows), choices, len(...  38.1 us
    pallas_call x2, Pallas kernels, gate(): pl.pallas_call(functools.partial(gate_kernel, per_group, blocks), grid_sp...  28.5 us
    ppermute x22, starting transfers between devices, swapped(): return lax.ppermute(value, EVERY, [(d, d ^ bit) for d in range(devices)])  19 us
    unnamed x43, local copies, waits for them, and re-layouts  15.1 us
    pallas_call x4, Pallas kernels, add_slots(): pl.pallas_call(functools.partial(add_kernel, widths), grid_spec=pltpu.Pre...  11 us
    ppermute x1, starting transfers between devices, paired(): lax.ppermute(outgoing((1 - window) * half, 16), EVERY, [(p, q ^ 1) for p,...  10.5 us
    ppermute x5, waiting for transfers between devices, step(): lax.ppermute(value, EVERY, [(w * shards + p * 4 + i, w * shards + q * 4 +...  9.92 us
  transfers between devices with their start and end apart: 29, of which 13 were waited for; matrix products, arithmetic and copies ran while one was open for 3% of the time, Pallas kernels for 37%

profile of v3, /device:TPU:0, one launch (start us, length us, event | category | flops | bytes accessed | tf_op | source)
XLA Modules:
  0.0 224.1 jit_solution(14191242421503897596)
XLA Ops:
  0.0 3.1 %multiply_convert_fusion = (bf16[128,4096]{1,0:T(8,128)(2,1)S(1)}, bf16[128,4096]{1,0:T(8,128)(2,1)S(1)}) fusion(bf16[256,8192]{1,0:T(8,128)(2,1)} %v_ref.3, s32[]{:T(128)S(6)} %select_n.80, bf16[256,8192]{1,0:T(8,128)(2,1)} %k_ref.3, s32[]{:T(128)S(6)} %select_n.79), kind=kLoop, calls=%fused_computation | loop fusion | flops 4194304 | bytes 6291464 | tf_op jit(solution)/shard_map/convert_element_type | solution.py:37
  3.1 2.4 %collective-permute-start = (bf16[128,4096]{1,0:T(8,128)(2,1)S(1)}, bf16[128,4096]{1,0:T(8,128)(2,1)S(1)}, u32[]{:S(2)}, u32[]{:S(2)}) collective-permute-start(bf16[128,4096]{1,0:T(8,128)(2,1)S(1)} %get-tuple-element.54), channel_id=1, source_target_pairs={{0,1},{1,2},{2,3},{3,4},{4,5},{5,6},{6,7},{7,8},{8,9},{9,10},{10,1... | collective-permute-start | bytes 3145736 | tf_op jit(solution)/shard_map/ppermute | solution.py:248
  6.7 10.5 %collective-permute-start.3 = (bf16[144,4096]{1,0:T(8,128)(2,1)}, bf16[144,4096]{1,0:T(8,128)(2,1)}, u32[]{:S(2)}, u32[]{:S(2)}) collective-permute-start(bf16[144,4096]{1,0:T(8,128)(2,1)} %pad.4), channel_id=1, source_target_pairs={{0,0},{1,3},{2,2},{3,5},{4,4},{5,7},{6,6},{7,9},{8,8},{9,11},{10,1... | collective-permute-start | bytes 3538952 | tf_op jit(solution)/shard_map/ppermute | solution.py:249
  21.7 2.5 %collective-permute-start.11 = (bf16[4096,256]{1,0:T(8,128)(2,1)}, bf16[4096,256]{1,0:T(8,128)(2,1)}, u32[]{:S(2)}, u32[]{:S(2)}) collective-permute-start(bf16[4096,256]{1,0:T(8,128)(2,1)} %shard_map.75.refs_4_), channel_id=1, source_target_pairs={{0,4},{1,5},{2,6},{3,7},{4,0},{5,1},{6,2},{7,3},{8,12},{9,13},{10,... | collective-permute-start | bytes 6291464 | tf_op jit(solution)/shard_map/ppermute | solution.py:252
  26.3 14.3 %shard_map.73 = (bf16[128,4096]{1,0:T(8,128)(2,1)}, bf16[128,4096]{1,0:T(8,128)(2,1)}) custom-call(s32[1]{0:T(128)} %bitcast.9.start_ref, f32[512,128]{1,0:T(8,128)} %maximum_convert_fusion.ring_ref.refs_2_, f32[1,8192]{1,0:T(1,128)} %bitcast.14, bf16[256,8192]{1,0:T(8,128)(2,1)} %q_ref.3, bf16[256,8192]{1,0:T(8,128)(2,1)} %k_ref.3, ...), custom_call_target="tpu_custom_call" | custom-call | flops 110000000 | bytes 1 | tf_op jit(solution)/shard_map/pallas_call | solution.py:86
  46.1 14.2 %shard_map.76 = (bf16[128,4096]{1,0:T(8,128)(2,1)}, bf16[128,4096]{1,0:T(8,128)(2,1)}) custom-call(s32[1]{0:T(128)} %bitcast.11.start_ref, f32[512,128]{1,0:T(8,128)} %maximum_convert_fusion.ring_ref.refs_2_, f32[1,8192]{1,0:T(1,128)} %bitcast.15, bf16[256,8192]{1,0:T(8,128)(2,1)} %q_ref.3, bf16[256,8192]{1,0:T(8,128)(2,1)} %k_ref.3, ...), custom_call_target="tpu_custom_call" | custom-call | flops 110000000 | bytes 1 | tf_op jit(solution)/shard_map/pallas_call | solution.py:86
  63.3 3.6 %collective-permute-done.2.refs_1_.refs_4_.refs_3_ = bf16[128,4096]{1,0:T(8,128)(2,1)S(1)} collective-permute-done((bf16[128,4096]{1,0:T(8,128)(2,1)}, bf16[128,4096]{1,0:T(8,128)(2,1)S(1)}, u32[]{:S(2)}, u32[]{:S(2)}) %collective-permute-start.2) | collective-permute-done | bytes 1048608 | tf_op jit(solution)/shard_map/ppermute | solution.py:224
  67.0 3.9 %collective-permute-done.11.refs_0_ = bf16[4096,256]{1,0:T(8,128)(2,1)} collective-permute-done((bf16[4096,256]{1,0:T(8,128)(2,1)}, bf16[4096,256]{1,0:T(8,128)(2,1)}, u32[]{:S(2)}, u32[]{:S(2)}) %collective-permute-start.11) | collective-permute-done | bytes 2097184 | tf_op jit(solution)/shard_map/ppermute | solution.py:252
  74.1 11.7 %collective-permute-done.7.refs_2_.refs_5_ = bf16[128,4096]{1,0:T(8,128)(2,1)} collective-permute-done((bf16[128,4096]{1,0:T(8,128)(2,1)}, bf16[128,4096]{1,0:T(8,128)(2,1)}, u32[]{:S(2)}, u32[]{:S(2)}) %collective-permute-start.7) | collective-permute-done | bytes 1048608 | tf_op jit(solution)/shard_map/ppermute | solution.py:224
  92.1 18.3 %collective-permute-done.6.refs_3_.refs_2_.refs_4_ = bf16[128,4096]{1,0:T(8,128)(2,1)S(1)} collective-permute-done((bf16[128,4096]{1,0:T(8,128)(2,1)}, bf16[128,4096]{1,0:T(8,128)(2,1)S(1)}, u32[]{:S(2)}, u32[]{:S(2)}) %collective-permute-start.6) | collective-permute-done | bytes 1048608 | tf_op jit(solution)/shard_map/ppermute | solution.py:224
  110.4 6.2 %collective-permute-done.10.refs_2_.refs_3_.refs_7_ = bf16[128,4096]{1,0:T(8,128)(2,1)S(1)} collective-permute-done((bf16[128,4096]{1,0:T(8,128)(2,1)}, bf16[128,4096]{1,0:T(8,128)(2,1)S(1)}, u32[]{:S(2)}, u32[]{:S(2)}) %collective-permute-start.10) | collective-permute-done | bytes 1048608 | tf_op jit(solution)/shard_map/ppermute | solution.py:224
  116.6 6.1 %collective-permute-done.13.refs_0_ = bf16[4096,256]{1,0:T(8,128)(2,1)} collective-permute-done((bf16[4096,256]{1,0:T(8,128)(2,1)}, bf16[4096,256]{1,0:T(8,128)(2,1)}, u32[]{:S(2)}, u32[]{:S(2)}) %collective-permute-start.13) | collective-permute-done | bytes 2097184 | tf_op jit(solution)/shard_map/ppermute | solution.py:252
  124.8 11.6 %collective-permute-done.8 = bf16[128,4096]{1,0:T(8,128)(2,1)S(1)} collective-permute-done((bf16[128,4096]{1,0:T(8,128)(2,1)S(1)}, bf16[128,4096]{1,0:T(8,128)(2,1)S(1)}, u32[]{:S(2)}, u32[]{:S(2)}) %collective-permute-start.8) | collective-permute-done | bytes 1048608 | tf_op jit(solution)/shard_map/ppermute | solution.py:224
  137.7 9.2 %shard_map.81 = (f32[256,1024]{1,0:T(8,128)}, bf16[256,1024]{1,0:T(8,128)(2,1)}) custom-call(s32[1]{0:T(128)} %constant.49.clone.1.which_ref, bf16[128,4096]{1,0:T(8,128)(2,1)} %get-tuple-element.30.refs_1_.refs_0_, bf16[128,4096]{1,0:T(8,128)(2,1)} %copy-done, bf16[128,4096]{1,0:T(8,128)(2,1)} %collective-permute-done.7.refs_2_.refs_5_, ...), custom_call_target="tpu_custom_call" | custom-call | flops 1100000000 | bytes 1 | tf_op jit(solution)/shard_map/pallas_call | solution.py:149
  148.2 9.2 %shard_map.82 = (f32[256,1024]{1,0:T(8,128)}, bf16[256,1024]{1,0:T(8,128)(2,1)}) custom-call(s32[1]{0:T(128)} %constant.49.clone.1.which_ref, bf16[128,4096]{1,0:T(8,128)(2,1)} %get-tuple-element.29.refs_2_.refs_0_, bf16[128,4096]{1,0:T(8,128)(2,1)} %copy-done.2, bf16[128,4096]{1,0:T(8,128)(2,1)} %copy-done.3, bf16[128,4096]{1,0:T(8,128)(2,1)} %copy-done.5, ...), custom_call_target="tpu_custom_call" | custom-call | flops 1100000000 | bytes 1 | tf_op jit(solution)/shard_map/pallas_call | solution.py:149
  158.5 9.9 %shard_map.83 = (f32[512,512]{1,0:T(8,128)}, bf16[512,512]{1,0:T(8,128)(2,1)}) custom-call(s32[1]{0:T(128)} %bitcast.8.which_ref, bf16[128,4096]{1,0:T(8,128)(2,1)} %get-tuple-element.29.refs_2_.refs_0_, bf16[128,4096]{1,0:T(8,128)(2,1)} %get-tuple-element.30.refs_1_.refs_0_, bf16[128,4096]{1,0:T(8,128)(2,1)} %copy-done.2, bf16[128,4096]{1,0:T(8,128)(2,1)} %copy-done, ...), custom_call_target="tpu_custom_call" | custom-call | flops 1100000000 | bytes 1 | tf_op jit(solution)/shard_map/pallas_call | solution.py:149
  175.7 3.7 %collective-permute-done.20.refs_1_.refs_2_ = bf16[128,1024]{1,0:T(8,128)(2,1)S(1)} collective-permute-done((bf16[128,1024]{1,0:T(8,128)(2,1)}, bf16[128,1024]{1,0:T(8,128)(2,1)S(1)}, u32[]{:S(2)}, u32[]{:S(2)}) %collective-permute-start.20) | collective-permute-done | bytes 262176 | tf_op jit(solution)/shard_map/ppermute | solution.py:224
  182.0 2.5 %collective-permute-done.23.refs_10_ = bf16[4096,256]{1,0:T(8,128)(2,1)S(1)} collective-permute-done((bf16[4096,256]{1,0:T(8,128)(2,1)}, bf16[4096,256]{1,0:T(8,128)(2,1)S(1)}, u32[]{:S(2)}, u32[]{:S(2)}) %collective-permute-start.23) | collective-permute-done | bytes 2097184 | tf_op jit(solution)/shard_map/ppermute | solution.py:224
  185.8 9.8 %shard_map.87 = (f32[512,512]{1,0:T(8,128)}, bf16[512,512]{1,0:T(8,128)(2,1)}) custom-call(s32[1]{0:T(128)} %bitcast.8.which_ref, bf16[128,4096]{1,0:T(8,128)(2,1)} %get-tuple-element.29.refs_2_.refs_0_, bf16[128,4096]{1,0:T(8,128)(2,1)} %get-tuple-element.30.refs_1_.refs_0_, bf16[128,4096]{1,0:T(8,128)(2,1)} %copy-done.2, bf16[128,4096]{1,0:T(8,128)(2,1)} %copy-done, ...), custom_call_target="tpu_custom_call" | custom-call | flops 1100000000 | bytes 1 | tf_op jit(solution)/shard_map/pallas_call | solution.py:149
  198.1 2.7 %shard_map.88.refs_3_ = bf16[256,4096]{1,0:T(8,128)(2,1)} custom-call(s32[8]{0:T(128)} %stack.35.refs_3_.place_ref, bf16[256,4096]{1,0:T(8,128)(2,1)} %refs_0_.7, bf16[128,1024]{1,0:T(8,128)(2,1)} %get-tuple-element.47.refs_1_, bf16[128,1024]{1,0:T(8,128)(2,1)} %copy-done.10), custom_call_target="tpu_custom_call" | custom-call | flops 1100000000 | bytes 1 | tf_op jit(solution)/shard_map/pallas_call | solution.py:206
  205.3 2.7 %shard_map.89.refs_0_.refs_3_ = bf16[256,4096]{1,0:T(8,128)(2,1)} custom-call(s32[8]{0:T(128)} %stack.35.refs_3_.place_ref, bf16[256,4096]{1,0:T(8,128)(2,1)} %refs_0_.7, bf16[128,1024]{1,0:T(8,128)(2,1)} %get-tuple-element.43.refs_2_.refs_1_, bf16[128,1024]{1,0:T(8,128)(2,1)} %copy-done.18, ...), custom_call_target="tpu_custom_call", output_to_operand_aliasing={{}: (4, {})} | custom-call | flops 1100000000 | bytes 1 | tf_op jit(solution)/shard_map/pallas_call | solution.py:206
  215.2 2.8 %shard_map.92.refs_3_ = bf16[256,4096]{1,0:T(8,128)(2,1)} custom-call(s32[8]{0:T(128)} %stack.35.refs_3_.place_ref, bf16[256,4096]{1,0:T(8,128)(2,1)} %refs_0_.7, bf16[256,512]{1,0:T(8,128)(2,1)} %get-tuple-element.51.refs_1_, bf16[256,512]{1,0:T(8,128)(2,1)} %copy-done.17, ...), custom_call_target="tpu_custom_call", output_to_operand_aliasing={{}: (4, {})} | custom-call | flops 1100000000 | bytes 1 | tf_op jit(solution)/shard_map/pallas_call | solution.py:206
  218.0 2.6 %collective-permute-done.26.refs_2_ = bf16[256,512]{1,0:T(8,128)(2,1)S(1)} collective-permute-done((bf16[256,512]{1,0:T(8,128)(2,1)}, bf16[256,512]{1,0:T(8,128)(2,1)S(1)}, u32[]{:S(2)}, u32[]{:S(2)}) %collective-permute-start.26) | collective-permute-done | bytes 262176 | tf_op jit(solution)/shard_map/ppermute | solution.py:224
  221.3 2.8 %shard_map.93 = bf16[256,4096]{1,0:T(8,128)(2,1)} custom-call(s32[8]{0:T(128)} %stack.35.refs_3_.place_ref, bf16[256,4096]{1,0:T(8,128)(2,1)} %refs_0_.7, bf16[256,512]{1,0:T(8,128)(2,1)} %get-tuple-element.48.refs_4_.refs_1_, bf16[256,512]{1,0:T(8,128)(2,1)} %copy-done.19, bf16[256,4096]{1,0:T(8,128)(2,1)} %shard_map.92.refs_3_), custom_call_target="tpu_custom_call", output_to_operand_aliasing={{}: (4, {})} | custom-call | flops 1100000000 | bytes 1 | tf_op jit(solution)/shard_map/pallas_call | solution.py:206
  (105 shorter events, 57.6 us)
Async XLA Ops:
  3.1 17.6 %collective-permute-start = (bf16[128,4096]{1,0:T(8,128)(2,1)S(1)}, bf16[128,4096]{1,0:T(8,128)(2,1)S(1)}, u32[]{:S(2)}, u32[]{:S(2)}) collective-permute-start(bf16[128,4096]{1,0:T(8,128)(2,1)S(1)} %get-tuple-element.54), channel_id=1, source_target_pairs={{0,1},{1,2},{2,3},{3,4},{4,5},{5,6},{6,7},{7,8},{8,9},{9,10},{10,1... | collective-permute-start | bytes 3145736 | tf_op jit(solution)/shard_map/ppermute | solution.py:248
  6.7 33.8 %collective-permute-start.3 = (bf16[144,4096]{1,0:T(8,128)(2,1)}, bf16[144,4096]{1,0:T(8,128)(2,1)}, u32[]{:S(2)}, u32[]{:S(2)}) collective-permute-start(bf16[144,4096]{1,0:T(8,128)(2,1)} %pad.4), channel_id=1, source_target_pairs={{0,0},{1,3},{2,2},{3,5},{4,4},{5,7},{6,6},{7,9},{8,8},{9,11},{10,1... | collective-permute-start | bytes 3538952 | tf_op jit(solution)/shard_map/ppermute | solution.py:249
  21.7 22.0 %collective-permute-start.5 = (bf16[4096,256]{1,0:T(8,128)(2,1)}, bf16[4096,256]{1,0:T(8,128)(2,1)S(1)}, u32[]{:S(2)}, u32[]{:S(2)}) collective-permute-start(bf16[4096,256]{1,0:T(8,128)(2,1)} %shard_map.75.refs_4_), channel_id=1, source_target_pairs={{0,1},{1,0},{2,3},{3,2},{4,5},{5,4},{6,7},{7,6},{8,9},{9,8},{10,11... | collective-permute-start | bytes 6291464 | tf_op jit(solution)/shard_map/ppermute | solution.py:224
  21.7 49.1 %collective-permute-start.11 = (bf16[4096,256]{1,0:T(8,128)(2,1)}, bf16[4096,256]{1,0:T(8,128)(2,1)}, u32[]{:S(2)}, u32[]{:S(2)}) collective-permute-start(bf16[4096,256]{1,0:T(8,128)(2,1)} %shard_map.75.refs_4_), channel_id=1, source_target_pairs={{0,4},{1,5},{2,6},{3,7},{4,0},{5,1},{6,2},{7,3},{8,12},{9,13},{10,... | collective-permute-start | bytes 6291464 | tf_op jit(solution)/shard_map/ppermute | solution.py:252
  24.2 46.6 %collective-permute-start.12 = (bf16[4096,256]{1,0:T(8,128)(2,1)}, bf16[4096,256]{1,0:T(8,128)(2,1)}, u32[]{:S(2)}, u32[]{:S(2)}) collective-permute-start(bf16[4096,256]{1,0:T(8,128)(2,1)} %shard_map.75.refs_4_), channel_id=1, source_target_pairs={{4,8},{5,9},{6,10},{7,11},{8,4},{9,5},{10,6},{11,7},{20,24},{21,25... | collective-permute-start | bytes 6291464 | tf_op jit(solution)/shard_map/ppermute | solution.py:252
  40.8 26.2 %collective-permute-start.2 = (bf16[128,4096]{1,0:T(8,128)(2,1)}, bf16[128,4096]{1,0:T(8,128)(2,1)S(1)}, u32[]{:S(2)}, u32[]{:S(2)}) collective-permute-start(bf16[128,4096]{1,0:T(8,128)(2,1)} %get-tuple-element.30.refs_1_.refs_0_), channel_id=1, source_target_pairs={{0,2},{1,3},{2,0},{3,1},{4,6},{5,7},{6,4},{7,5},{8,10},{9,11},{10,... | collective-permute-start | bytes 3145736 | tf_op jit(solution)/shard_map/ppermute | solution.py:224
  60.3 25.5 %collective-permute-start.7 = (bf16[128,4096]{1,0:T(8,128)(2,1)}, bf16[128,4096]{1,0:T(8,128)(2,1)}, u32[]{:S(2)}, u32[]{:S(2)}) collective-permute-start(bf16[128,4096]{1,0:T(8,128)(2,1)} %get-tuple-element.32.refs_2_), channel_id=1, source_target_pairs={{0,16},{1,17},{2,18},{3,19},{4,20},{5,21},{6,22},{7,23},{8,24},{9,... | collective-permute-start | bytes 3145736 | tf_op jit(solution)/shard_map/ppermute | solution.py:224
  61.7 27.9 %collective-permute-start.1 = (bf16[128,4096]{1,0:T(8,128)(2,1)}, bf16[128,4096]{1,0:T(8,128)(2,1)S(1)}, u32[]{:S(2)}, u32[]{:S(2)}) collective-permute-start(bf16[128,4096]{1,0:T(8,128)(2,1)} %get-tuple-element.29.refs_2_.refs_0_), channel_id=1, source_target_pairs={{0,2},{1,3},{2,0},{3,1},{4,6},{5,7},{6,4},{7,5},{8,10},{9,11},{10,... | collective-permute-start | bytes 3145736 | tf_op jit(solution)/shard_map/ppermute | solution.py:224
  70.8 51.9 %collective-permute-start.13 = (bf16[4096,256]{1,0:T(8,128)(2,1)}, bf16[4096,256]{1,0:T(8,128)(2,1)}, u32[]{:S(2)}, u32[]{:S(2)}) collective-permute-start(bf16[4096,256]{1,0:T(8,128)(2,1)} %get-tuple-element.33.refs_9_), channel_id=1, source_target_pairs={{4,0},{5,1},{6,2},{7,3},{8,12},{9,13},{10,14},{11,15},{20,16},{21,... | collective-permute-start | bytes 6291464 | tf_op jit(solution)/shard_map/ppermute | solution.py:252
  72.1 50.6 %collective-permute-start.14 = (bf16[4096,256]{1,0:T(8,128)(2,1)}, bf16[4096,256]{1,0:T(8,128)(2,1)}, u32[]{:S(2)}, u32[]{:S(2)}) collective-permute-start(bf16[4096,256]{1,0:T(8,128)(2,1)} %get-tuple-element.34.refs_6_), channel_id=1, source_target_pairs={{4,8},{5,9},{6,10},{7,11},{8,4},{9,5},{10,6},{11,7},{20,24},{21,25... | collective-permute-start | bytes 6291464 | tf_op jit(solution)/shard_map/ppermute | solution.py:252
  74.1 50.1 %collective-permute-start.16 = (bf16[4096,256]{1,0:T(8,128)(2,1)}, bf16[4096,256]{1,0:T(8,128)(2,1)}, u32[]{:S(2)}, u32[]{:S(2)}) collective-permute-start(bf16[4096,256]{1,0:T(8,128)(2,1)} %get-tuple-element.34.refs_6_), channel_id=1, source_target_pairs={{0,1},{1,0},{2,3},{3,2},{4,5},{5,4},{6,7},{7,6},{8,9},{9,8},{10,11... | collective-permute-start | bytes 6291464 | tf_op jit(solution)/shard_map/ppermute | solution.py:224
  85.8 24.6 %collective-permute-start.6 = (bf16[128,4096]{1,0:T(8,128)(2,1)}, bf16[128,4096]{1,0:T(8,128)(2,1)S(1)}, u32[]{:S(2)}, u32[]{:S(2)}) collective-permute-start(bf16[128,4096]{1,0:T(8,128)(2,1)} %shard_map.77), channel_id=1, source_target_pairs={{0,16},{1,17},{2,18},{3,19},{4,20},{5,21},{6,22},{7,23},{8,24},{9,... | collective-permute-start | bytes 3145736 | tf_op jit(solution)/shard_map/ppermute | solution.py:224
  90.6 26.0 %collective-permute-start.10 = (bf16[128,4096]{1,0:T(8,128)(2,1)}, bf16[128,4096]{1,0:T(8,128)(2,1)S(1)}, u32[]{:S(2)}, u32[]{:S(2)}) collective-permute-start(bf16[128,4096]{1,0:T(8,128)(2,1)} %shard_map.78), channel_id=1, source_target_pairs={{0,2},{1,3},{2,0},{3,1},{4,6},{5,7},{6,4},{7,5},{8,10},{9,11},{10,... | collective-permute-start | bytes 3145736 | tf_op jit(solution)/shard_map/ppermute | solution.py:224
  110.4 26.0 %collective-permute-start.8 = (bf16[128,4096]{1,0:T(8,128)(2,1)S(1)}, bf16[128,4096]{1,0:T(8,128)(2,1)S(1)}, u32[]{:S(2)}, u32[]{:S(2)}) collective-permute-start(bf16[128,4096]{1,0:T(8,128)(2,1)S(1)} %collective-permute-done.6.refs_3_.refs_2_.refs_4_), channel_id=1, source_target_pairs={{0,3},{1,2},{2,1},{3,0},{4,7},{5,6},{6,5},{7,4},{8,11},{9,10},{10,... | collective-permute-start | bytes 3145736 | tf_op jit(solution)/shard_map/ppermute | solution.py:224
  116.6 40.8 %collective-permute-start.19 = (bf16[4096,256]{1,0:T(8,128)(2,1)}, bf16[4096,256]{1,0:T(8,128)(2,1)}, u32[]{:S(2)}, u32[]{:S(2)}) collective-permute-start(bf16[4096,256]{1,0:T(8,128)(2,1)} %get-tuple-element.33.refs_9_), channel_id=1, source_target_pairs={{0,1},{1,0},{2,3},{3,2},{4,5},{5,4},{6,7},{7,6},{8,9},{9,8},{10,11... | collective-permute-start | bytes 6291464 | tf_op jit(solution)/shard_map/ppermute | solution.py:224
  122.7 35.8 %collective-permute-start.18 = (bf16[4096,256]{1,0:T(8,128)(2,1)}, bf16[4096,256]{1,0:T(8,128)(2,1)}, u32[]{:S(2)}, u32[]{:S(2)}) collective-permute-start(bf16[4096,256]{1,0:T(8,128)(2,1)} %get-tuple-element.38.refs_8_), channel_id=1, source_target_pairs={{0,1},{1,0},{2,3},{3,2},{4,5},{5,4},{6,7},{7,6},{8,9},{9,8},{10,11... | collective-permute-start | bytes 6291464 | tf_op jit(solution)/shard_map/ppermute | solution.py:224
  122.8 52.9 %collective-permute-start.15 = (bf16[4096,256]{1,0:T(8,128)(2,1)}, bf16[4096,256]{1,0:T(8,128)(2,1)}, u32[]{:S(2)}, u32[]{:S(2)}) collective-permute-start(bf16[4096,256]{1,0:T(8,128)(2,1)} %get-tuple-element.35.refs_9_), channel_id=1, source_target_pairs={{4,0},{5,1},{6,2},{7,3},{8,12},{9,13},{10,14},{11,15},{20,16},{21,... | collective-permute-start | bytes 6291464 | tf_op jit(solution)/shard_map/ppermute | solution.py:252
  124.3 51.5 %collective-permute-start.22 = (bf16[4096,256]{1,0:T(8,128)(2,1)}, bf16[4096,256]{1,0:T(8,128)(2,1)}, u32[]{:S(2)}, u32[]{:S(2)}) collective-permute-start(bf16[4096,256]{1,0:T(8,128)(2,1)} %get-tuple-element.35.refs_9_), channel_id=1, source_target_pairs={{0,1},{1,0},{2,3},{3,2},{4,5},{5,4},{6,7},{7,6},{8,9},{9,8},{10,11... | collective-permute-start | bytes 6291464 | tf_op jit(solution)/shard_map/ppermute | solution.py:224
  136.4 10.6 %collective-permute-start.9 = (bf16[128,4096]{1,0:T(8,128)(2,1)S(1)}, bf16[128,4096]{1,0:T(8,128)(2,1)S(1)}, u32[]{:S(2)}, u32[]{:S(2)}) collective-permute-start(bf16[128,4096]{1,0:T(8,128)(2,1)S(1)} %collective-permute-done.8), channel_id=1, source_target_pairs={{0,1},{1,0},{2,3},{3,2},{4,5},{5,4},{6,7},{7,6},{8,9},{9,8},{10,11... | collective-permute-start | bytes 3145736 | tf_op jit(solution)/shard_map/ppermute | solution.py:224
  147.0 21.3 %collective-permute-start.17 = (bf16[256,1024]{1,0:T(8,128)(2,1)}, bf16[256,1024]{1,0:T(8,128)(2,1)S(1)}, u32[]{:S(2)}, u32[]{:S(2)}) collective-permute-start(bf16[256,1024]{1,0:T(8,128)(2,1)} %get-tuple-element.37.refs_8_), channel_id=1, source_target_pairs={{0,16},{1,17},{2,18},{3,19},{4,20},{5,21},{6,22},{7,23},{8,24},{9,... | collective-permute-start | bytes 1572872 | tf_op jit(solution)/shard_map/ppermute | solution.py:224
  157.4 15.4 %collective-permute-start.21 = (bf16[256,1024]{1,0:T(8,128)(2,1)}, bf16[256,1024]{1,0:T(8,128)(2,1)S(1)}, u32[]{:S(2)}, u32[]{:S(2)}) collective-permute-start(bf16[256,1024]{1,0:T(8,128)(2,1)} %get-tuple-element.39.refs_12_), channel_id=1, source_target_pairs={{0,16},{1,17},{2,18},{3,19},{4,20},{5,21},{6,22},{7,23},{8,24},{9,... | collective-permute-start | bytes 1572872 | tf_op jit(solution)/shard_map/ppermute | solution.py:224
  181.1 19.6 %collective-permute-start.27 = (bf16[512,512]{1,0:T(8,128)(2,1)S(1)}, bf16[512,512]{1,0:T(8,128)(2,1)S(1)}, u32[]{:S(2)}, u32[]{:S(2)}) collective-permute-start(bf16[512,512]{1,0:T(8,128)(2,1)S(1)} %copy-done.6), channel_id=1, source_target_pairs={{0,16},{1,17},{2,18},{3,19},{4,20},{5,21},{6,22},{7,23},{8,24},{9,... | collective-permute-start | bytes 1572872 | tf_op jit(solution)/shard_map/ppermute | solution.py:224
  195.6 14.2 %collective-permute-start.24 = (bf16[512,512]{1,0:T(8,128)(2,1)}, bf16[512,512]{1,0:T(8,128)(2,1)S(1)}, u32[]{:S(2)}, u32[]{:S(2)}) collective-permute-start(bf16[512,512]{1,0:T(8,128)(2,1)} %get-tuple-element.45), channel_id=1, source_target_pairs={{0,16},{1,17},{2,18},{3,19},{4,20},{5,21},{6,22},{7,23},{8,24},{9,... | collective-permute-start | bytes 1572872 | tf_op jit(solution)/shard_map/ppermute | solution.py:224
  203.8 10.7 %collective-permute-start.28 = (bf16[256,512]{1,0:T(8,128)(2,1)}, bf16[256,512]{1,0:T(8,128)(2,1)S(1)}, u32[]{:S(2)}, u32[]{:S(2)}) collective-permute-start(bf16[256,512]{1,0:T(8,128)(2,1)} %get-tuple-element.52), channel_id=1, source_target_pairs={{0,2},{1,3},{2,0},{3,1},{4,6},{5,7},{6,4},{7,5},{8,10},{9,11},{10,... | collective-permute-start | bytes 786440 | tf_op jit(solution)/shard_map/ppermute | solution.py:224
  (26 other events, 113.3 us)

commit v4 on v3

--- a/solution.py
+++ b/solution.py
@@ -28,7 +28,7 @@
         out_specs=[pl.BlockSpec(memory_space=pl.ANY)] * len(values),
         out_shape=[jax.ShapeDtypeStruct(v.shape, v.dtype) for v in values],
         input_output_aliases={i: i for i in range(len(values))},
-        compiler_params=pltpu.CompilerParams(vmem_limit_bytes=60 << 20),
+        compiler_params=pltpu.CompilerParams(vmem_limit_bytes=16 << 20),
         cost_estimate=cost(weight),
     )(*values, *waits)
 
@@ -158,7 +158,7 @@
             scratch_shapes=[pltpu.VMEM((height, sum(widths)), F32)],
         ),
         out_shape=[jax.ShapeDtypeStruct(part, dtype) for dtype in dtypes],
-        compiler_params=pltpu.CompilerParams(vmem_limit_bytes=60 << 20),
+        compiler_params=pltpu.CompilerParams(vmem_limit_bytes=24 << 20),
         cost_estimate=cost(1),
     )(jnp.full((1,), which, jnp.int32), *rows, *[w for group in weights for w in group], *waits)
 
@@ -180,44 +180,88 @@
         in_specs=[whole, whole] + [pl.BlockSpec(memory_space=pl.ANY)] * len(waits),
         out_specs=[pl.BlockSpec((rows // 2, tile), lambda i: (0, i))] * 2,
         out_shape=[jax.ShapeDtypeStruct((rows // 2, width), BF16)] * 2,
-        compiler_params=pltpu.CompilerParams(vmem_limit_bytes=60 << 20),
+        compiler_params=pltpu.CompilerParams(vmem_limit_bytes=16 << 20),
         cost_estimate=cost(0),
     )(keep, arrived, *waits)
 
 
-def add_kernel(widths, place_ref, *refs):
-    total_ref, out_ref = refs[0], refs[-1]
-    span = sum(widths)
-    for h, width in enumerate(widths):
-        for j in range(4):
-            start = place_ref[j] * span + sum(widths[:h])
-            lanes = pl.ds(pl.multiple_of(start, LANES), width)
-            mine = refs[1 + 2 * h + j // 2][:, (j % 2) * width : (j % 2 + 1) * width]
-            out_ref[:, lanes] = (total_ref[:, lanes].astype(F32) + mine.astype(F32)).astype(BF16)
-
-
-def add_slots(residual, total, parts, block, place, first, slots, waits=()):
-    widths = [cut[0].shape[1] // slots // 2 for cut in parts]
-    rows = parts[0][0].shape[0]
-    span = 4 * sum(widths)
-    flat = [(piece, 2 * width) for cut, width in zip(parts, widths) for piece in cut]
-    whole = pl.BlockSpec((rows, span), lambda i, s: (block, s[4 + first + i]))
+def add_kernel(counts, place_ref, *refs):
+    residual_ref, out_ref = refs[0], refs[-1]
+    step, at, first = pl.program_id(0), 1, 0
+    for slots, heights in counts:
+        near, far = refs[at : at + len(heights)], refs[at + len(heights) : at + 2 * len(heights)]
+
+        @pl.when((step >= first) & (step < first + slots))
+        def _():
+            top = 0
+            for height, pair in zip(heights, zip(near, far)):
+                rows, top = slice(top, top + height), top + height
+                for j in range(4):
+                    width = pair[0].shape[1] // 2
+                    lanes = pl.ds(pl.multiple_of(place_ref[j] * width, LANES), width)
+                    mine = pair[j // 2][:, (j % 2) * width : (j % 2 + 1) * width]
+                    out_ref[rows, lanes] = (residual_ref[rows, lanes].astype(F32) + mine.astype(F32)).astype(BF16)
+
+        at, first = at + 2 * len(heights), first + slots
+
+
+def add_slots(residual, groups, place, start=0, total=None, waits=()):
+    rows = residual.shape[0]
+    span = groups[0][1][0].shape[1] // groups[0][0] * 2
+    whole = pl.BlockSpec((rows, span), lambda i, s: (0, s[4 + start + i]))
     so_far = ([] if total is None else [total]) + list(waits)
-    return pl.pallas_call(
-        functools.partial(add_kernel, widths),
+    specs, operands, counts, first = [], [], [], 0
+    for slots, near, far in groups:
+        for piece in [*near, *far]:
+
+            def at(i, s, first=first, slots=slots):
+                return (0, jnp.clip(i - first, 0, slots - 1))
+
+            specs.append(pl.BlockSpec((piece.shape[0], span // 2), at))
+            operands.append(piece)
+        counts.append((slots, [n.shape[0] for n in near]))
+        first += slots
+    return pl.pallas_call(
+        functools.partial(add_kernel, counts),
         grid_spec=pltpu.PrefetchScalarGridSpec(
             num_scalar_prefetch=1,
-            grid=(slots,),
-            in_specs=[whole]
-            + [pl.BlockSpec((rows, w), lambda i, s: (0, i)) for _, w in flat]
-            + [pl.BlockSpec(memory_space=pl.ANY)] * len(so_far),
+            grid=(first,),
+            in_specs=[whole] + specs + [pl.BlockSpec(memory_space=pl.ANY)] * len(so_far),
             out_specs=whole,
         ),
         out_shape=jax.ShapeDtypeStruct(residual.shape, residual.dtype),
-        input_output_aliases={} if total is None else {2 + len(flat): 0},
-        compiler_params=pltpu.CompilerParams(vmem_limit_bytes=60 << 20),
+        input_output_aliases={} if total is None else {2 + len(operands): 0},
+        compiler_params=pltpu.CompilerParams(vmem_limit_bytes=16 << 20),
         cost_estimate=cost(1),
-    )(place, residual, *[p for p, _ in flat], *so_far)
+    )(place, residual, *operands, *so_far)
+
+
+def finish_kernel(place_ref, *refs):
+    residual_ref, out_ref = refs[0], refs[-1]
+    width = refs[1].shape[1]
+    for j in range(4):
+        lanes = pl.ds(pl.multiple_of(place_ref[j] * width, LANES), width)
+        out_ref[:, lanes] = (residual_ref[:, lanes].astype(F32) + refs[1 + j][...].astype(F32)).astype(BF16)
+
+
+def finish(residual, total, terms, place, slot):
+    rows, width = terms[0].shape
+    whole = pl.BlockSpec((rows, 4 * width), lambda i, s: (0, s[4 + slot]))
+    return pl.pallas_call(
+        finish_kernel,
+        grid_spec=pltpu.PrefetchScalarGridSpec(
+            num_scalar_prefetch=1,
+            grid=(1,),
+            in_specs=[whole]
+            + [pl.BlockSpec((rows, width), lambda i, s: (0, 0))] * len(terms)
+            + [pl.BlockSpec(memory_space=pl.ANY)],
+            out_specs=whole,
+        ),
+        out_shape=jax.ShapeDtypeStruct(residual.shape, residual.dtype),
+        input_output_aliases={2 + len(terms): 0},
+        compiler_params=pltpu.CompilerParams(vmem_limit_bytes=16 << 20),
+        cost_estimate=cost(1),
+    )(place, residual, *terms, total)
 
 
 def swapped(value, bit, devices):
@@ -280,11 +324,10 @@
     for t in theirs[1:]:
         seconds += [swapped(*after([t], crossed[0]), devices // 2, devices)]
     far = [swapped(*after([seconds[0]], crossed[-1]), 2, devices)]
-    far += [swapped(swapped(o, 3, devices), 1, devices) for o in seconds[1:]]
+    far += [swapped(o, 3, devices) for o in seconds[1:]]
     handed, kept = after([handed, kept], far[0], seconds[-1])
     final = step(kept, (1, 0), (2, 3))
     at_end = jnp.where((plane == 0) | (plane == planes - 1), 0, 1)
-    gathered = list(zip(firsts, crossed, seconds, far))
     def sent_back(send):
         return swapped(send, devices // 2, devices)
 
@@ -295,24 +338,34 @@
         sums.append((keep, send, sent_back(send)))
 
     single = [[w] for w in early]
-    for pieces in gathered:
+    gathered = []
+    for n, pieces in enumerate(zip(firsts, crossed, seconds, far)):
+        if n:
+            pieces = [*pieces[:3], swapped(*after([pieces[3]], sums[-1][1]), 1, devices)]
+        gathered.append(pieces)
         summed(pieces, single)
     everyone = [gathered[blocks - 1 - b][p] for p in range(4) for b in range(blocks)]
     keep, send = project(everyone, list(zip(both(handed), both(across))), [F32, BF16], [sums[-1][1]], at_end)
     sums.append((keep, send, sent_back(send)))
-    settled = [settle(k, arrived, [send] if i < blocks else []) for i, (k, _, arrived) in enumerate(sums)]
+    settled = [settle(k, arrived, [sums[i + 1][1]] if i < blocks else []) for i, (k, _, arrived) in enumerate(sums)]
     parts = [[n, swapped(f, 2, devices)] for n, f in settled]
 
     kept = both(kept)
-    final = both(*after([final], parts[0][1], settled[blocks - 1][0], send, kept[1]))
-    keep, send = project(everyone, list(zip(final, kept)), [F32, BF16], [], at_end)
-    total = None
-    for i, block in enumerate(reversed(range(blocks))):
-        total = add_slots(residual, total, [parts[i]], block, place, 0, 2)
-    near, far_rows = settle(keep, sent_back(send), [total])
-    last_part = [near, swapped(far_rows, 2, devices)]
-    total = add_slots(residual, total, [parts[blocks]], 0, place, 2, 1, [near])
-    return add_slots(residual, total, [last_part], 0, place, 3, 1)
+    (final,) = after([final], *[p[1] for p in parts[: blocks - 1]], settled[blocks - 1][0], sums[blocks][2], kept[1])
+    final = both(final)
+    waits, last = [], []
+    for n in range(2):
+        keep, send = project(everyone, [(final[n], kept[n])], [F32, BF16], waits, at_end)
+        waits = [send, parts[blocks - 1][1]]
+        last.append((keep, sent_back(send)))
+    near, far_rows = settle(*last[0])
+    terms = [[near, swapped(far_rows, 2, devices)]]
+    near, far_rows = settle(*last[1], [terms[0][1], parts[blocks][1]])
+    terms.append([near, swapped(far_rows, 2, devices)])
+    rows_up = parts[:blocks][::-1]
+    groups = [(2, [p[0] for p in rows_up], [p[1] for p in rows_up]), (1, [parts[blocks][0]], [parts[blocks][1]])]
+    total = add_slots(residual, groups, place, waits=[near])
+    return finish(residual, total, [terms[dc][dx] for dx in range(2) for dc in range(2)], place, 3)
 
 
 def general(queries, key_proj, value_proj, filter_taps, skip_gain, out_weight, residual):

time: 225 us -> 215 us (0.956); the launches traced: 224 us -> 211 us
  Pallas kernels: 86.3 us -> 68.6 us
  starting transfers between devices: 41.4 us -> 45.7 us
  local copies, waits for them, and re-layouts: 18.8 us -> 15.8 us
  waiting for transfers between devices: 73.5 us -> 76.1 us
    pallas_call x4 -> x5, Pallas kernels: 8.63 us -> 1.7 us  [settle(): pl.pallas_call(settle_kernel, grid=(width // tile,), in_specs=[whole, who...]
    pallas_call x4 -> x2, Pallas kernels: 11 us -> 4.22 us  [the longest x1 2.62 us: add_slots(): pl.pallas_call(functools.partial(add_kernel, counts), grid_spec=pltpu.Pre...]
    ppermute x5, waiting for transfers between devices: 9.92 us -> 14.1 us  [step(): lax.ppermute(value, EVERY, [(w * shards + p * 4 + i, w * shards + q * 4 +...]
    pallas_call x4 -> x5, Pallas kernels: 38.1 us -> 34.1 us  [project(): pl.pallas_call(functools.partial(project_kernel, len(rows), choices, len(...]
    ppermute x22 -> x24, starting transfers between devices: 19 us -> 22.9 us  [swapped(): return lax.ppermute(value, EVERY, [(d, d ^ bit) for d in range(devices)])]
    ppermute x22 -> x24, waiting for transfers between devices: 63.6 us -> 62 us  [swapped(): return lax.ppermute(value, EVERY, [(d, d ^ bit) for d in range(devices)])]
    unnamed x43 -> x57, local copies, waits for them, and re-layouts: 15.1 us -> 13.9 us
  transfers between devices with their start and end apart: 29 -> 31, of which waited for: 13 -> 17; matrix products, arithmetic and copies ran while one was open for 3% -> 1% of each run, Pallas kernels for 37% -> 32%
where the time goes in v4:
time: 215 us; the launch traced here: 211 us
  waiting for transfers between devices  76.1 us (35%)
  Pallas kernels  68.6 us (32%)
  starting transfers between devices  45.7 us (21%)
  local copies, waits for them, and re-layouts  15.8 us (7%)
  other arithmetic  4.16 us (2%)
    ppermute x24, waiting for transfers between devices, swapped(): return lax.ppermute(value, EVERY, [(d, d ^ bit) for d in range(devices)])  62 us
    pallas_call x5, Pallas kernels, project(): pl.pallas_call(functools.partial(project_kernel, len(rows), choices, len(...  34.1 us
    pallas_call x2, Pallas kernels, gate(): pl.pallas_call(functools.partial(gate_kernel, per_group, blocks), grid_sp...  28.6 us
    ppermute x24, starting transfers between devices, swapped(): return lax.ppermute(value, EVERY, [(d, d ^ bit) for d in range(devices)])  22.9 us
    ppermute x5, waiting for transfers between devices, step(): lax.ppermute(value, EVERY, [(w * shards + p * 4 + i, w * shards + q * 4 +...  14.1 us
    unnamed x57, local copies, waits for them, and re-layouts  13.9 us
    ppermute x1, starting transfers between devices, paired(): lax.ppermute(outgoing((1 - window) * half, 16), EVERY, [(p, q ^ 1) for p,...  10.5 us
    ppermute x5, starting transfers between devices, step(): lax.ppermute(value, EVERY, [(w * shards + p * 4 + i, w * shards + q * 4 +...  9.94 us
  transfers between devices with their start and end apart: 31, of which 17 were waited for; matrix products, arithmetic and copies ran while one was open for 1% of the time, Pallas kernels for 32%

profile of v4, /device:TPU:0, one launch (start us, length us, event | category | flops | bytes accessed | tf_op | source)
XLA Modules:
  0.0 210.8 jit_solution(6460402048675413880)
XLA Ops:
  0.0 4.0 %multiply_convert_fusion = (bf16[128,4096]{1,0:T(8,128)(2,1)S(1)}, bf16[128,4096]{1,0:T(8,128)(2,1)}) fusion(bf16[256,8192]{1,0:T(8,128)(2,1)} %v_ref.3, s32[]{:T(128)S(6)} %select_n.80, bf16[256,8192]{1,0:T(8,128)(2,1)} %k_ref.3, s32[]{:T(128)S(6)} %select_n.79), kind=kLoop, calls=%fused_computation | loop fusion | flops 4194304 | bytes 6291464 | tf_op jit(solution)/shard_map/convert_element_type | solution.py:37
  4.1 2.4 %collective-permute-start = (bf16[128,4096]{1,0:T(8,128)(2,1)}, bf16[128,4096]{1,0:T(8,128)(2,1)S(1)}, u32[]{:S(2)}, u32[]{:S(2)}) collective-permute-start(bf16[128,4096]{1,0:T(8,128)(2,1)} %get-tuple-element.62), channel_id=1, source_target_pairs={{0,1},{1,2},{2,3},{3,4},{4,5},{5,6},{6,7},{7,8},{8,9},{9,10},{10,1... | collective-permute-start | bytes 3145736 | tf_op jit(solution)/shard_map/ppermute | solution.py:292
  7.6 10.5 %collective-permute-start.3 = (bf16[144,4096]{1,0:T(8,128)(2,1)}, bf16[144,4096]{1,0:T(8,128)(2,1)}, u32[]{:S(2)}, u32[]{:S(2)}) collective-permute-start(bf16[144,4096]{1,0:T(8,128)(2,1)} %pad.4), channel_id=1, source_target_pairs={{0,0},{1,3},{2,2},{3,5},{4,4},{5,7},{6,6},{7,9},{8,8},{9,11},{10,1... | collective-permute-start | bytes 3538952 | tf_op jit(solution)/shard_map/ppermute | solution.py:293
  22.0 3.2 %collective-permute-start.10 = (bf16[4096,256]{1,0:T(8,128)(2,1)S(1)}, bf16[4096,256]{1,0:T(8,128)(2,1)}, u32[]{:S(2)}, u32[]{:S(2)}) collective-permute-start(bf16[4096,256]{1,0:T(8,128)(2,1)S(1)} %shard_map.75.refs_4_), channel_id=1, source_target_pairs={{0,4},{1,5},{2,6},{3,7},{4,0},{5,1},{6,2},{7,3},{8,12},{9,13},{10,... | collective-permute-start | bytes 6291464 | tf_op jit(solution)/shard_map/ppermute | solution.py:296
  27.2 14.3 %shard_map.73 = (bf16[128,4096]{1,0:T(8,128)(2,1)}, bf16[128,4096]{1,0:T(8,128)(2,1)}) custom-call(s32[1]{0:T(128)} %bitcast.9.start_ref, f32[512,128]{1,0:T(8,128)} %copy-done.19, f32[1,8192]{1,0:T(1,128)} %bitcast.14, bf16[256,8192]{1,0:T(8,128)(2,1)} %q_ref.3, bf16[256,8192]{1,0:T(8,128)(2,1)} %k_ref.3, bf16[256,8192]{1,0:T(8,128)(2,1)} %v_ref.3, ...), custom_call_target="tpu_custom_call" | custom-call | flops 110000000 | bytes 1 | tf_op jit(solution)/shard_map/pallas_call | solution.py:86
  46.8 14.3 %shard_map.76 = (bf16[128,4096]{1,0:T(8,128)(2,1)}, bf16[128,4096]{1,0:T(8,128)(2,1)}) custom-call(s32[1]{0:T(128)} %bitcast.11.start_ref, f32[512,128]{1,0:T(8,128)} %copy-done.19, f32[1,8192]{1,0:T(1,128)} %bitcast.15, bf16[256,8192]{1,0:T(8,128)(2,1)} %q_ref.3, bf16[256,8192]{1,0:T(8,128)(2,1)} %k_ref.3, bf16[256,8192]{1,0:T(8,128)(2,1)} %v_ref.3, ...), custom_call_target="tpu_custom_call" | custom-call | flops 110000000 | bytes 1 | tf_op jit(solution)/shard_map/pallas_call | solution.py:86
  64.0 5.1 %collective-permute-done.2.refs_1_.refs_4_.refs_3_ = bf16[128,4096]{1,0:T(8,128)(2,1)S(1)} collective-permute-done((bf16[128,4096]{1,0:T(8,128)(2,1)}, bf16[128,4096]{1,0:T(8,128)(2,1)S(1)}, u32[]{:S(2)}, u32[]{:S(2)}) %collective-permute-start.2) | collective-permute-done | bytes 1048608 | tf_op jit(solution)/shard_map/ppermute | solution.py:268
  69.1 2.6 %collective-permute-done.10.refs_0_ = bf16[4096,256]{1,0:T(8,128)(2,1)} collective-permute-done((bf16[4096,256]{1,0:T(8,128)(2,1)S(1)}, bf16[4096,256]{1,0:T(8,128)(2,1)}, u32[]{:S(2)}, u32[]{:S(2)}) %collective-permute-start.10) | collective-permute-done | bytes 2097184 | tf_op jit(solution)/shard_map/ppermute | solution.py:296
  77.4 9.1 %collective-permute-done.7.refs_2_.refs_5_ = bf16[128,4096]{1,0:T(8,128)(2,1)S(1)} collective-permute-done((bf16[128,4096]{1,0:T(8,128)(2,1)}, bf16[128,4096]{1,0:T(8,128)(2,1)S(1)}, u32[]{:S(2)}, u32[]{:S(2)}) %collective-permute-start.7) | collective-permute-done | bytes 1048608 | tf_op jit(solution)/shard_map/ppermute | solution.py:268
  88.2 2.8 %collective-permute-done.1.refs_1_.refs_2_ = bf16[128,4096]{1,0:T(8,128)(2,1)S(1)} collective-permute-done((bf16[128,4096]{1,0:T(8,128)(2,1)}, bf16[128,4096]{1,0:T(8,128)(2,1)S(1)}, u32[]{:S(2)}, u32[]{:S(2)}) %collective-permute-start.1) | collective-permute-done | bytes 1048608 | tf_op jit(solution)/shard_map/ppermute | solution.py:268
  92.2 18.8 %collective-permute-done.6.refs_3_.refs_2_.refs_4_ = bf16[128,4096]{1,0:T(8,128)(2,1)S(1)} collective-permute-done((bf16[128,4096]{1,0:T(8,128)(2,1)S(1)}, bf16[128,4096]{1,0:T(8,128)(2,1)S(1)}, u32[]{:S(2)}, u32[]{:S(2)}) %collective-permute-start.6) | collective-permute-done | bytes 1048608 | tf_op jit(solution)/shard_map/ppermute | solution.py:268
  111.6 5.5 %collective-permute-done.9.refs_3_.refs_2_.refs_7_ = bf16[128,4096]{1,0:T(8,128)(2,1)S(1)} collective-permute-done((bf16[128,4096]{1,0:T(8,128)(2,1)S(1)}, bf16[128,4096]{1,0:T(8,128)(2,1)S(1)}, u32[]{:S(2)}, u32[]{:S(2)}) %collective-permute-start.9) | collective-permute-done | bytes 1048608 | tf_op jit(solution)/shard_map/ppermute | solution.py:268
  117.1 8.9 %collective-permute-done.14.refs_0_ = bf16[4096,256]{1,0:T(8,128)(2,1)} collective-permute-done((bf16[4096,256]{1,0:T(8,128)(2,1)}, bf16[4096,256]{1,0:T(8,128)(2,1)}, u32[]{:S(2)}, u32[]{:S(2)}) %collective-permute-start.14) | collective-permute-done | bytes 2097184 | tf_op jit(solution)/shard_map/ppermute | solution.py:296
  128.1 8.0 %shard_map.80 = (f32[256,1024]{1,0:T(8,128)S(1)}, bf16[256,1024]{1,0:T(8,128)(2,1)}) custom-call(s32[1]{0:T(128)} %constant.49.clone.1.which_ref, bf16[128,4096]{1,0:T(8,128)(2,1)} %get-tuple-element.34.refs_1_.refs_0_, bf16[128,4096]{1,0:T(8,128)(2,1)S(1)} %collective-permute-done.2.refs_1_.refs_4_.refs_3_, ...), custom_call_target="tpu_custom_call" | custom-call | flops 1100000000 | bytes 1 | tf_op jit(solution)/shard_map/pallas_call | solution.py:149
  149.7 7.3 %shard_map.83 = (f32[256,1024]{1,0:T(8,128)S(1)}, bf16[256,1024]{1,0:T(8,128)(2,1)S(1)}) custom-call(s32[1]{0:T(128)} %constant.49.clone.1.which_ref, bf16[128,4096]{1,0:T(8,128)(2,1)S(1)} %copy-done.1, bf16[128,4096]{1,0:T(8,128)(2,1)S(1)} %copy-done.6, bf16[128,4096]{1,0:T(8,128)(2,1)S(1)} %copy-done.9, bf16[128,4096]{1,0:T(8,128)(2,1)S(1)} %copy-done.14, ...), custom_call_target="tpu_custom_call" | custom-call | flops 1100000000 | bytes 1 | tf_op jit(solution)/shard_map/pallas_call | solution.py:149
  157.7 8.1 %shard_map.85 = (f32[512,512]{1,0:T(8,128)S(1)}, bf16[512,512]{1,0:T(8,128)(2,1)S(1)}) custom-call(s32[1]{0:T(128)} %bitcast.8.which_ref, bf16[128,4096]{1,0:T(8,128)(2,1)S(1)} %copy-done.2, bf16[128,4096]{1,0:T(8,128)(2,1)} %get-tuple-element.34.refs_1_.refs_0_, bf16[128,4096]{1,0:T(8,128)(2,1)S(1)} %copy-done.7, ...), custom_call_target="tpu_custom_call" | custom-call | flops 1100000000 | bytes 1 | tf_op jit(solution)/shard_map/pallas_call | solution.py:149
  169.4 2.4 %collective-permute-done.19.arrived_ref = bf16[256,1024]{1,0:T(8,128)(2,1)S(1)} collective-permute-done((bf16[256,1024]{1,0:T(8,128)(2,1)S(1)}, bf16[256,1024]{1,0:T(8,128)(2,1)S(1)}, u32[]{:S(2)}, u32[]{:S(2)}) %collective-permute-start.19) | collective-permute-done | bytes 524320 | tf_op jit(solution)/shard_map/ppermute | solution.py:268
  172.1 4.2 %collective-permute-done.18.refs_1_.refs_4_ = bf16[128,1024]{1,0:T(8,128)(2,1)S(1)} collective-permute-done((bf16[128,1024]{1,0:T(8,128)(2,1)S(1)}, bf16[128,1024]{1,0:T(8,128)(2,1)S(1)}, u32[]{:S(2)}, u32[]{:S(2)}) %collective-permute-start.18) | collective-permute-done | bytes 262176 | tf_op jit(solution)/shard_map/ppermute | solution.py:268
  176.3 2.6 %collective-permute-done.16.refs_0_ = bf16[4096,256]{1,0:T(8,128)(2,1)} collective-permute-done((bf16[4096,256]{1,0:T(8,128)(2,1)}, bf16[4096,256]{1,0:T(8,128)(2,1)}, u32[]{:S(2)}, u32[]{:S(2)}) %collective-permute-start.16) | collective-permute-done | bytes 2097184 | tf_op jit(solution)/shard_map/ppermute | solution.py:296
  178.8 3.4 %collective-permute-done.22.refs_3_.arrived_ref = bf16[512,512]{1,0:T(8,128)(2,1)S(1)} collective-permute-done((bf16[512,512]{1,0:T(8,128)(2,1)S(1)}, bf16[512,512]{1,0:T(8,128)(2,1)S(1)}, u32[]{:S(2)}, u32[]{:S(2)}) %collective-permute-start.22) | collective-permute-done | bytes 524320 | tf_op jit(solution)/shard_map/ppermute | solution.py:268
  183.7 5.5 %shard_map.88 = (f32[512,256]{1,0:T(8,128)S(1)}, bf16[512,256]{1,0:T(8,128)(2,1)S(1)}) custom-call(s32[1]{0:T(128)} %bitcast.8.which_ref, bf16[128,4096]{1,0:T(8,128)(2,1)S(1)} %copy-done.2, bf16[128,4096]{1,0:T(8,128)(2,1)} %get-tuple-element.34.refs_1_.refs_0_, bf16[128,4096]{1,0:T(8,128)(2,1)S(1)} %copy-done.7, ...), custom_call_target="tpu_custom_call" | custom-call | flops 1100000000 | bytes 1 | tf_op jit(solution)/shard_map/pallas_call | solution.py:149
  190.9 5.3 %shard_map.90 = (f32[512,256]{1,0:T(8,128)S(1)}, bf16[512,256]{1,0:T(8,128)(2,1)S(1)}) custom-call(s32[1]{0:T(128)} %bitcast.8.which_ref, bf16[128,4096]{1,0:T(8,128)(2,1)S(1)} %copy-done.2, bf16[128,4096]{1,0:T(8,128)(2,1)} %get-tuple-element.34.refs_1_.refs_0_, bf16[128,4096]{1,0:T(8,128)(2,1)S(1)} %copy-done.7, ...), custom_call_target="tpu_custom_call" | custom-call | flops 1100000000 | bytes 1 | tf_op jit(solution)/shard_map/pallas_call | solution.py:149
  199.0 3.9 %collective-permute-done.28.refs_0_.refs_3_ = bf16[256,256]{1,0:T(8,128)(2,1)S(1)} collective-permute-done((bf16[256,256]{1,0:T(8,128)(2,1)S(1)}, bf16[256,256]{1,0:T(8,128)(2,1)S(1)}, u32[]{:S(2)}, u32[]{:S(2)}) %collective-permute-start.28) | collective-permute-done | bytes 131104 | tf_op jit(solution)/shard_map/ppermute | solution.py:268
  205.2 2.6 %shard_map.93.refs_5_ = bf16[256,4096]{1,0:T(8,128)(2,1)} custom-call(s32[8]{0:T(128)S(1)} %stack.35.refs_3_.place_ref, bf16[256,4096]{1,0:T(8,128)(2,1)S(1)} %copy-done.18, bf16[128,1024]{1,0:T(8,128)(2,1)S(1)} %get-tuple-element.47.refs_2_.refs_1_, bf16[128,1024]{1,0:T(8,128)(2,1)S(1)} %get-tuple-element.59.refs_2_, ...), custom_call_target="tpu_custom_call" | custom-call | flops 1100000000 | bytes 1 | tf_op jit(solution)/shard_map/pallas_call | solution.py:224
  (124 shorter events, 55.9 us)
Async XLA Ops:
  4.1 15.0 %collective-permute-start = (bf16[128,4096]{1,0:T(8,128)(2,1)}, bf16[128,4096]{1,0:T(8,128)(2,1)S(1)}, u32[]{:S(2)}, u32[]{:S(2)}) collective-permute-start(bf16[128,4096]{1,0:T(8,128)(2,1)} %get-tuple-element.62), channel_id=1, source_target_pairs={{0,1},{1,2},{2,3},{3,4},{4,5},{5,6},{6,7},{7,8},{8,9},{9,10},{10,1... | collective-permute-start | bytes 3145736 | tf_op jit(solution)/shard_map/ppermute | solution.py:292
  7.6 33.9 %collective-permute-start.3 = (bf16[144,4096]{1,0:T(8,128)(2,1)}, bf16[144,4096]{1,0:T(8,128)(2,1)}, u32[]{:S(2)}, u32[]{:S(2)}) collective-permute-start(bf16[144,4096]{1,0:T(8,128)(2,1)} %pad.4), channel_id=1, source_target_pairs={{0,0},{1,3},{2,2},{3,5},{4,4},{5,7},{6,6},{7,9},{8,8},{9,11},{10,1... | collective-permute-start | bytes 3538952 | tf_op jit(solution)/shard_map/ppermute | solution.py:293
  20.1 25.7 %collective-permute-start.5 = (bf16[4096,256]{1,0:T(8,128)(2,1)S(1)}, bf16[4096,256]{1,0:T(8,128)(2,1)}, u32[]{:S(2)}, u32[]{:S(2)}) collective-permute-start(bf16[4096,256]{1,0:T(8,128)(2,1)S(1)} %shard_map.75.refs_4_), channel_id=1, source_target_pairs={{0,1},{1,0},{2,3},{3,2},{4,5},{5,4},{6,7},{7,6},{8,9},{9,8},{10,11... | collective-permute-start | bytes 6291464 | tf_op jit(solution)/shard_map/ppermute | solution.py:268
  22.0 49.7 %collective-permute-start.10 = (bf16[4096,256]{1,0:T(8,128)(2,1)S(1)}, bf16[4096,256]{1,0:T(8,128)(2,1)}, u32[]{:S(2)}, u32[]{:S(2)}) collective-permute-start(bf16[4096,256]{1,0:T(8,128)(2,1)S(1)} %shard_map.75.refs_4_), channel_id=1, source_target_pairs={{0,4},{1,5},{2,6},{3,7},{4,0},{5,1},{6,2},{7,3},{8,12},{9,13},{10,... | collective-permute-start | bytes 6291464 | tf_op jit(solution)/shard_map/ppermute | solution.py:296
  25.3 46.4 %collective-permute-start.11 = (bf16[4096,256]{1,0:T(8,128)(2,1)S(1)}, bf16[4096,256]{1,0:T(8,128)(2,1)}, u32[]{:S(2)}, u32[]{:S(2)}) collective-permute-start(bf16[4096,256]{1,0:T(8,128)(2,1)S(1)} %shard_map.75.refs_4_), channel_id=1, source_target_pairs={{4,8},{5,9},{6,10},{7,11},{8,4},{9,5},{10,6},{11,7},{20,24},{21,25... | collective-permute-start | bytes 6291464 | tf_op jit(solution)/shard_map/ppermute | solution.py:296
  42.9 26.2 %collective-permute-start.2 = (bf16[128,4096]{1,0:T(8,128)(2,1)}, bf16[128,4096]{1,0:T(8,128)(2,1)S(1)}, u32[]{:S(2)}, u32[]{:S(2)}) collective-permute-start(bf16[128,4096]{1,0:T(8,128)(2,1)} %get-tuple-element.34.refs_1_.refs_0_), channel_id=1, source_target_pairs={{0,2},{1,3},{2,0},{3,1},{4,6},{5,7},{6,4},{7,5},{8,10},{9,11},{10,... | collective-permute-start | bytes 3145736 | tf_op jit(solution)/shard_map/ppermute | solution.py:268
  61.1 25.4 %collective-permute-start.7 = (bf16[128,4096]{1,0:T(8,128)(2,1)}, bf16[128,4096]{1,0:T(8,128)(2,1)S(1)}, u32[]{:S(2)}, u32[]{:S(2)}) collective-permute-start(bf16[128,4096]{1,0:T(8,128)(2,1)} %get-tuple-element.36.refs_2_), channel_id=1, source_target_pairs={{0,16},{1,17},{2,18},{3,19},{4,20},{5,21},{6,22},{7,23},{8,24},{9,... | collective-permute-start | bytes 3145736 | tf_op jit(solution)/shard_map/ppermute | solution.py:268
  62.6 28.4 %collective-permute-start.1 = (bf16[128,4096]{1,0:T(8,128)(2,1)}, bf16[128,4096]{1,0:T(8,128)(2,1)S(1)}, u32[]{:S(2)}, u32[]{:S(2)}) collective-permute-start(bf16[128,4096]{1,0:T(8,128)(2,1)} %get-tuple-element.33.refs_2_.refs_0_), channel_id=1, source_target_pairs={{0,2},{1,3},{2,0},{3,1},{4,6},{5,7},{6,4},{7,5},{8,10},{9,11},{10,... | collective-permute-start | bytes 3145736 | tf_op jit(solution)/shard_map/ppermute | solution.py:268
  74.1 51.9 %collective-permute-start.14 = (bf16[4096,256]{1,0:T(8,128)(2,1)}, bf16[4096,256]{1,0:T(8,128)(2,1)}, u32[]{:S(2)}, u32[]{:S(2)}) collective-permute-start(bf16[4096,256]{1,0:T(8,128)(2,1)} %get-tuple-element.39.refs_9_), channel_id=1, source_target_pairs={{4,0},{5,1},{6,2},{7,3},{8,12},{9,13},{10,14},{11,15},{20,16},{21,... | collective-permute-start | bytes 6291464 | tf_op jit(solution)/shard_map/ppermute | solution.py:296
  75.4 50.6 %collective-permute-start.15 = (bf16[4096,256]{1,0:T(8,128)(2,1)}, bf16[4096,256]{1,0:T(8,128)(2,1)}, u32[]{:S(2)}, u32[]{:S(2)}) collective-permute-start(bf16[4096,256]{1,0:T(8,128)(2,1)} %get-tuple-element.37.refs_6_), channel_id=1, source_target_pairs={{4,8},{5,9},{6,10},{7,11},{8,4},{9,5},{10,6},{11,7},{20,24},{21,25... | collective-permute-start | bytes 6291464 | tf_op jit(solution)/shard_map/ppermute | solution.py:296
  77.4 50.2 %collective-permute-start.12 = (bf16[4096,256]{1,0:T(8,128)(2,1)}, bf16[4096,256]{1,0:T(8,128)(2,1)S(1)}, u32[]{:S(2)}, u32[]{:S(2)}) collective-permute-start(bf16[4096,256]{1,0:T(8,128)(2,1)} %get-tuple-element.37.refs_6_), channel_id=1, source_target_pairs={{0,1},{1,0},{2,3},{3,2},{4,5},{5,4},{6,7},{7,6},{8,9},{9,8},{10,11... | collective-permute-start | bytes 6291464 | tf_op jit(solution)/shard_map/ppermute | solution.py:268
  86.5 24.5 %collective-permute-start.6 = (bf16[128,4096]{1,0:T(8,128)(2,1)S(1)}, bf16[128,4096]{1,0:T(8,128)(2,1)S(1)}, u32[]{:S(2)}, u32[]{:S(2)}) collective-permute-start(bf16[128,4096]{1,0:T(8,128)(2,1)S(1)} %shard_map.77), channel_id=1, source_target_pairs={{0,16},{1,17},{2,18},{3,19},{4,20},{5,21},{6,22},{7,23},{8,24},{9,... | collective-permute-start | bytes 3145736 | tf_op jit(solution)/shard_map/ppermute | solution.py:268
  91.0 26.1 %collective-permute-start.9 = (bf16[128,4096]{1,0:T(8,128)(2,1)S(1)}, bf16[128,4096]{1,0:T(8,128)(2,1)S(1)}, u32[]{:S(2)}, u32[]{:S(2)}) collective-permute-start(bf16[128,4096]{1,0:T(8,128)(2,1)S(1)} %shard_map.78), channel_id=1, source_target_pairs={{0,2},{1,3},{2,0},{3,1},{4,6},{5,7},{6,4},{7,5},{8,10},{9,11},{10,... | collective-permute-start | bytes 3145736 | tf_op jit(solution)/shard_map/ppermute | solution.py:268
  111.0 25.9 %collective-permute-start.8 = (bf16[128,4096]{1,0:T(8,128)(2,1)S(1)}, bf16[128,4096]{1,0:T(8,128)(2,1)S(1)}, u32[]{:S(2)}, u32[]{:S(2)}) collective-permute-start(bf16[128,4096]{1,0:T(8,128)(2,1)S(1)} %collective-permute-done.6.refs_3_.refs_2_.refs_4_), channel_id=1, source_target_pairs={{0,3},{1,2},{2,1},{3,0},{4,7},{5,6},{6,5},{7,4},{8,11},{9,10},{10,... | collective-permute-start | bytes 3145736 | tf_op jit(solution)/shard_map/ppermute | solution.py:268
  117.1 39.9 %collective-permute-start.21 = (bf16[4096,256]{1,0:T(8,128)(2,1)}, bf16[4096,256]{1,0:T(8,128)(2,1)}, u32[]{:S(2)}, u32[]{:S(2)}) collective-permute-start(bf16[4096,256]{1,0:T(8,128)(2,1)} %get-tuple-element.39.refs_9_), channel_id=1, source_target_pairs={{0,1},{1,0},{2,3},{3,2},{4,5},{5,4},{6,7},{7,6},{8,9},{9,8},{10,11... | collective-permute-start | bytes 6291464 | tf_op jit(solution)/shard_map/ppermute | solution.py:268
  126.0 31.7 %collective-permute-start.20 = (bf16[4096,256]{1,0:T(8,128)(2,1)}, bf16[4096,256]{1,0:T(8,128)(2,1)}, u32[]{:S(2)}, u32[]{:S(2)}) collective-permute-start(bf16[4096,256]{1,0:T(8,128)(2,1)} %get-tuple-element.45.refs_8_), channel_id=1, source_target_pairs={{0,1},{1,0},{2,3},{3,2},{4,5},{5,4},{6,7},{7,6},{8,9},{9,8},{10,11... | collective-permute-start | bytes 6291464 | tf_op jit(solution)/shard_map/ppermute | solution.py:268
  126.1 52.7 %collective-permute-start.16 = (bf16[4096,256]{1,0:T(8,128)(2,1)}, bf16[4096,256]{1,0:T(8,128)(2,1)}, u32[]{:S(2)}, u32[]{:S(2)}) collective-permute-start(bf16[4096,256]{1,0:T(8,128)(2,1)} %get-tuple-element.40.refs_9_), channel_id=1, source_target_pairs={{4,0},{5,1},{6,2},{7,3},{8,12},{9,13},{10,14},{11,15},{20,16},{21,... | collective-permute-start | bytes 6291464 | tf_op jit(solution)/shard_map/ppermute | solution.py:296
  127.6 51.2 %collective-permute-start.23 = (bf16[4096,256]{1,0:T(8,128)(2,1)}, bf16[4096,256]{1,0:T(8,128)(2,1)}, u32[]{:S(2)}, u32[]{:S(2)}) collective-permute-start(bf16[4096,256]{1,0:T(8,128)(2,1)} %get-tuple-element.40.refs_9_), channel_id=1, source_target_pairs={{0,1},{1,0},{2,3},{3,2},{4,5},{5,4},{6,7},{7,6},{8,9},{9,8},{10,11... | collective-permute-start | bytes 6291464 | tf_op jit(solution)/shard_map/ppermute | solution.py:268
  141.8 25.5 %collective-permute-start.17 = (bf16[256,1024]{1,0:T(8,128)(2,1)}, bf16[256,1024]{1,0:T(8,128)(2,1)}, u32[]{:S(2)}, u32[]{:S(2)}) collective-permute-start(bf16[256,1024]{1,0:T(8,128)(2,1)} %get-tuple-element.38.refs_1_.refs_8_), channel_id=1, source_target_pairs={{0,16},{1,17},{2,18},{3,19},{4,20},{5,21},{6,22},{7,23},{8,24},{9,... | collective-permute-start | bytes 1572872 | tf_op jit(solution)/shard_map/ppermute | solution.py:268
  157.0 14.8 %collective-permute-start.19 = (bf16[256,1024]{1,0:T(8,128)(2,1)S(1)}, bf16[256,1024]{1,0:T(8,128)(2,1)S(1)}, u32[]{:S(2)}, u32[]{:S(2)}) collective-permute-start(bf16[256,1024]{1,0:T(8,128)(2,1)S(1)} %get-tuple-element.42.refs_0_.refs_12_), channel_id=1, source_target_pairs={{0,16},{1,17},{2,18},{3,19},{4,20},{5,21},{6,22},{7,23},{8,24},{9,... | collective-permute-start | bytes 1572872 | tf_op jit(solution)/shard_map/ppermute | solution.py:268
  165.8 16.4 %collective-permute-start.22 = (bf16[512,512]{1,0:T(8,128)(2,1)S(1)}, bf16[512,512]{1,0:T(8,128)(2,1)S(1)}, u32[]{:S(2)}, u32[]{:S(2)}) collective-permute-start(bf16[512,512]{1,0:T(8,128)(2,1)S(1)} %get-tuple-element.46.refs_0_), channel_id=1, source_target_pairs={{0,16},{1,17},{2,18},{3,19},{4,20},{5,21},{6,22},{7,23},{8,24},{9,... | collective-permute-start | bytes 1572872 | tf_op jit(solution)/shard_map/ppermute | solution.py:268
  182.2 8.7 %collective-permute-start.25 = (bf16[4096,256]{1,0:T(8,128)(2,1)}, bf16[4096,256]{1,0:T(8,128)(2,1)S(1)}, u32[]{:S(2)}, u32[]{:S(2)}) collective-permute-start(bf16[4096,256]{1,0:T(8,128)(2,1)} %shard_map.87.refs_8_), channel_id=1, source_target_pairs={{0,1},{1,0},{2,3},{3,2},{4,5},{5,4},{6,7},{7,6},{8,9},{9,8},{10,11... | collective-permute-start | bytes 6291464 | tf_op jit(solution)/shard_map/ppermute | solution.py:268
  182.2 8.7 %collective-permute-start.26 = (bf16[128,1024]{1,0:T(8,128)(2,1)S(1)}, bf16[128,1024]{1,0:T(8,128)(2,1)S(1)}, u32[]{:S(2)}, u32[]{:S(2)}) collective-permute-start(bf16[128,1024]{1,0:T(8,128)(2,1)S(1)} %get-tuple-element.51), channel_id=1, source_target_pairs={{0,2},{1,3},{2,0},{3,1},{4,6},{5,7},{6,4},{7,5},{8,10},{9,11},{10,... | collective-permute-start | bytes 786440 | tf_op jit(solution)/shard_map/ppermute | solution.py:268
  190.1 9.0 %collective-permute-start.29 = (bf16[256,512]{1,0:T(8,128)(2,1)S(1)}, bf16[256,512]{1,0:T(8,128)(2,1)S(1)}, u32[]{:S(2)}, u32[]{:S(2)}) collective-permute-start(bf16[256,512]{1,0:T(8,128)(2,1)S(1)} %get-tuple-element.56), channel_id=1, source_target_pairs={{0,2},{1,3},{2,0},{3,1},{4,6},{5,7},{6,4},{7,5},{8,10},{9,11},{10,... | collective-permute-start | bytes 786440 | tf_op jit(solution)/shard_map/ppermute | solution.py:268
  (35 other events, 258.3 us)

commit v5 on v4

--- a/solution.py
+++ b/solution.py
@@ -21,14 +21,14 @@
     pass
 
 
-def after(values, *waits, weight=0):
+def after(values, *waits, weight=0, room=60):
     return pl.pallas_call(
         pass_kernel,
         in_specs=[pl.BlockSpec(memory_space=pl.ANY)] * (len(values) + len(waits)),
         out_specs=[pl.BlockSpec(memory_space=pl.ANY)] * len(values),
         out_shape=[jax.ShapeDtypeStruct(v.shape, v.dtype) for v in values],
         input_output_aliases={i: i for i in range(len(values))},
-        compiler_params=pltpu.CompilerParams(vmem_limit_bytes=16 << 20),
+        compiler_params=pltpu.CompilerParams(vmem_limit_bytes=room << 20),
         cost_estimate=cost(weight),
     )(*values, *waits)
 
@@ -133,7 +133,7 @@
             out_ref[...] = total[i * part : (i + 1) * part, :].astype(out_ref.dtype)
 
 
-def project(rows, weights, dtypes, waits=(), which=0):
+def project(rows, weights, dtypes, waits=(), which=0, room=60):
     depth = rows[0].shape[1]
     height = sum(r.shape[0] for r in rows)
     widths = [w[0].shape[1] for w in weights]
@@ -158,7 +158,7 @@
             scratch_shapes=[pltpu.VMEM((height, sum(widths)), F32)],
         ),
         out_shape=[jax.ShapeDtypeStruct(part, dtype) for dtype in dtypes],
-        compiler_params=pltpu.CompilerParams(vmem_limit_bytes=24 << 20),
+        compiler_params=pltpu.CompilerParams(vmem_limit_bytes=room << 20),
         cost_estimate=cost(1),
     )(jnp.full((1,), which, jnp.int32), *rows, *[w for group in weights for w in group], *waits)
 
@@ -351,11 +351,11 @@
     parts = [[n, swapped(f, 2, devices)] for n, f in settled]
 
     kept = both(kept)
-    (final,) = after([final], *[p[1] for p in parts[: blocks - 1]], settled[blocks - 1][0], sums[blocks][2], kept[1])
+    (final,) = after([final], *[p[1] for p in parts[: blocks - 1]], settled[blocks - 1][0], sums[blocks][2], kept[1], room=16)
     final = both(final)
     waits, last = [], []
     for n in range(2):
-        keep, send = project(everyone, [(final[n], kept[n])], [F32, BF16], waits, at_end)
+        keep, send = project(everyone, [(final[n], kept[n])], [F32, BF16], waits, at_end, 24)
         waits = [send, parts[blocks - 1][1]]
         last.append((keep, sent_back(send)))
     near, far_rows = settle(*last[0])

time: 215 us -> 210 us (0.977); the launches traced: 211 us -> 209 us
  Pallas kernels: 68.6 us -> 74.5 us
  starting transfers between devices: 45.7 us -> 40.1 us
  local copies, waits for them, and re-layouts: 15.8 us -> 12.2 us
    ppermute x1, starting transfers between devices: 10.5 us -> 0.74 us  [paired(): lax.ppermute(outgoing((1 - window) * half, 16), EVERY, [(p, q ^ 1) for p,...]
    unnamed x57 -> x47, local copies, waits for them, and re-layouts: 13.9 us -> 7.42 us
    pallas_call x5, Pallas kernels: 34.1 us -> 39.2 us  [project(): pl.pallas_call(functools.partial(project_kernel, len(rows), choices, len(...]
    ppermute x24, starting transfers between devices: 22.9 us -> 26.8 us  [swapped(): return lax.ppermute(value, EVERY, [(d, d ^ bit) for d in range(devices)])]
    ppermute x24, waiting for transfers between devices: 62 us -> 65.8 us  [swapped(): return lax.ppermute(value, EVERY, [(d, d ^ bit) for d in range(devices)])]
    ppermute x5, waiting for transfers between devices: 14.1 us -> 10.7 us  [step(): lax.ppermute(value, EVERY, [(w * shards + p * 4 + i, w * shards + q * 4 +...]
  transfers between devices with their start and end apart: 31 -> 31, of which waited for: 17 -> 17; matrix products, arithmetic and copies ran while one was open for 1% -> 4% of each run, Pallas kernels for 32% -> 35%
where the time goes in v5:
time: 210 us; the launch traced here: 209 us
  waiting for transfers between devices  76.5 us (36%)
  Pallas kernels  74.5 us (35%)
  starting transfers between devices  40.1 us (19%)
  local copies, waits for them, and re-layouts  12.2 us (6%)
  other arithmetic  5.91 us (3%)
    ppermute x24, waiting for transfers between devices, swapped(): return lax.ppermute(value, EVERY, [(d, d ^ bit) for d in range(devices)])  65.8 us
    pallas_call x5, Pallas kernels, project(): pl.pallas_call(functools.partial(project_kernel, len(rows), choices, len(...  39.2 us
    pallas_call x2, Pallas kernels, gate(): pl.pallas_call(functools.partial(gate_kernel, per_group, blocks), grid_sp...  28.6 us
    ppermute x24, starting transfers between devices, swapped(): return lax.ppermute(value, EVERY, [(d, d ^ bit) for d in range(devices)])  26.8 us
    ppermute x5, waiting for transfers between devices, step(): lax.ppermute(value, EVERY, [(w * shards + p * 4 + i, w * shards + q * 4 +...  10.7 us
    ppermute x5, starting transfers between devices, step(): lax.ppermute(value, EVERY, [(w * shards + p * 4 + i, w * shards + q * 4 +...  10.1 us
    unnamed x47, local copies, waits for them, and re-layouts  7.42 us
  transfers between devices with their start and end apart: 31, of which 17 were waited for; matrix products, arithmetic and copies ran while one was open for 4% of the time, Pallas kernels for 35%

profile of v5, /device:TPU:0, one launch (start us, length us, event | category | flops | bytes accessed | tf_op | source)
XLA Modules:
  0.0 209.4 jit_solution(14430709738564571476)
XLA Ops:
  0.0 4.1 %multiply_convert_fusion = (bf16[128,4096]{1,0:T(8,128)(2,1)S(1)}, bf16[128,4096]{1,0:T(8,128)(2,1)}) fusion(bf16[256,8192]{1,0:T(8,128)(2,1)} %v_ref.3, s32[]{:T(128)S(6)} %select_n.80, bf16[256,8192]{1,0:T(8,128)(2,1)} %k_ref.3, s32[]{:T(128)S(6)} %select_n.79), kind=kLoop, calls=%fused_computation | loop fusion | flops 4194304 | bytes 6291464 | tf_op jit(solution)/shard_map/convert_element_type | solution.py:37
  4.1 2.4 %collective-permute-start = (bf16[128,4096]{1,0:T(8,128)(2,1)}, bf16[128,4096]{1,0:T(8,128)(2,1)S(1)}, u32[]{:S(2)}, u32[]{:S(2)}) collective-permute-start(bf16[128,4096]{1,0:T(8,128)(2,1)} %get-tuple-element.62), channel_id=1, source_target_pairs={{0,1},{1,2},{2,3},{3,4},{4,5},{5,6},{6,7},{7,8},{8,9},{9,10},{10,1... | collective-permute-start | bytes 3145736 | tf_op jit(solution)/shard_map/ppermute | solution.py:292
  14.8 7.3 %collective-permute-start.5 = (bf16[4096,256]{1,0:T(8,128)(2,1)}, bf16[4096,256]{1,0:T(8,128)(2,1)}, u32[]{:S(2)}, u32[]{:S(2)}) collective-permute-start(bf16[4096,256]{1,0:T(8,128)(2,1)} %shard_map.75.refs_4_), channel_id=1, source_target_pairs={{0,1},{1,0},{2,3},{3,2},{4,5},{5,4},{6,7},{7,6},{8,9},{9,8},{10,11... | collective-permute-start | bytes 6291464 | tf_op jit(solution)/shard_map/ppermute | solution.py:268
  22.1 3.2 %collective-permute-start.10 = (bf16[4096,256]{1,0:T(8,128)(2,1)}, bf16[4096,256]{1,0:T(8,128)(2,1)}, u32[]{:S(2)}, u32[]{:S(2)}) collective-permute-start(bf16[4096,256]{1,0:T(8,128)(2,1)} %shard_map.75.refs_4_), channel_id=1, source_target_pairs={{0,4},{1,5},{2,6},{3,7},{4,0},{5,1},{6,2},{7,3},{8,12},{9,13},{10,... | collective-permute-start | bytes 6291464 | tf_op jit(solution)/shard_map/ppermute | solution.py:296
  25.4 2.1 collective-permute-start.11
  27.4 14.3 %shard_map.73 = (bf16[128,4096]{1,0:T(8,128)(2,1)}, bf16[128,4096]{1,0:T(8,128)(2,1)}) custom-call(s32[1]{0:T(128)} %bitcast.9.start_ref, f32[512,128]{1,0:T(8,128)} %maximum_convert_fusion.ring_ref.refs_2_, f32[1,8192]{1,0:T(1,128)} %bitcast.14, bf16[256,8192]{1,0:T(8,128)(2,1)} %q_ref.3, bf16[256,8192]{1,0:T(8,128)(2,1)} %k_ref.3, ...), custom_call_target="tpu_custom_call" | custom-call | flops 110000000 | bytes 1 | tf_op jit(solution)/shard_map/pallas_call | solution.py:86
  46.8 14.4 %shard_map.76 = (bf16[128,4096]{1,0:T(8,128)(2,1)}, bf16[128,4096]{1,0:T(8,128)(2,1)}) custom-call(s32[1]{0:T(128)} %bitcast.11.start_ref, f32[512,128]{1,0:T(8,128)} %maximum_convert_fusion.ring_ref.refs_2_, f32[1,8192]{1,0:T(1,128)} %bitcast.15, bf16[256,8192]{1,0:T(8,128)(2,1)} %q_ref.3, bf16[256,8192]{1,0:T(8,128)(2,1)} %k_ref.3, ...), custom_call_target="tpu_custom_call" | custom-call | flops 110000000 | bytes 1 | tf_op jit(solution)/shard_map/pallas_call | solution.py:86
  63.7 6.3 %collective-permute-done.2.refs_1_.refs_4_.refs_3_ = bf16[128,4096]{1,0:T(8,128)(2,1)S(1)} collective-permute-done((bf16[128,4096]{1,0:T(8,128)(2,1)S(1)}, bf16[128,4096]{1,0:T(8,128)(2,1)S(1)}, u32[]{:S(2)}, u32[]{:S(2)}) %collective-permute-start.2) | collective-permute-done | bytes 1048608 | tf_op jit(solution)/shard_map/ppermute | solution.py:268
  75.3 11.4 %collective-permute-done.7.refs_2_.refs_5_ = bf16[128,4096]{1,0:T(8,128)(2,1)} collective-permute-done((bf16[128,4096]{1,0:T(8,128)(2,1)}, bf16[128,4096]{1,0:T(8,128)(2,1)}, u32[]{:S(2)}, u32[]{:S(2)}) %collective-permute-start.7) | collective-permute-done | bytes 1048608 | tf_op jit(solution)/shard_map/ppermute | solution.py:268
  88.3 2.3 %copy.22.refs_0_ = bf16[128,4096]{1,0:T(8,128)(2,1)} copy(bf16[128,4096]{1,0:T(8,128)(2,1)} %collective-permute-done.7.refs_2_.refs_5_) | data formatting | bytes 2097152
  92.9 18.5 %collective-permute-done.6.refs_3_.refs_2_.refs_4_ = bf16[128,4096]{1,0:T(8,128)(2,1)S(1)} collective-permute-done((bf16[128,4096]{1,0:T(8,128)(2,1)}, bf16[128,4096]{1,0:T(8,128)(2,1)S(1)}, u32[]{:S(2)}, u32[]{:S(2)}) %collective-permute-start.6) | collective-permute-done | bytes 1048608 | tf_op jit(solution)/shard_map/ppermute | solution.py:268
  111.4 6.8 %collective-permute-done.9.refs_3_.refs_2_.refs_7_ = bf16[128,4096]{1,0:T(8,128)(2,1)S(1)} collective-permute-done((bf16[128,4096]{1,0:T(8,128)(2,1)}, bf16[128,4096]{1,0:T(8,128)(2,1)S(1)}, u32[]{:S(2)}, u32[]{:S(2)}) %collective-permute-start.9) | collective-permute-done | bytes 1048608 | tf_op jit(solution)/shard_map/ppermute | solution.py:268
  118.2 5.7 %collective-permute-done.14.refs_0_ = bf16[4096,256]{1,0:T(8,128)(2,1)} collective-permute-done((bf16[4096,256]{1,0:T(8,128)(2,1)}, bf16[4096,256]{1,0:T(8,128)(2,1)}, u32[]{:S(2)}, u32[]{:S(2)}) %collective-permute-start.14) | collective-permute-done | bytes 2097184 | tf_op jit(solution)/shard_map/ppermute | solution.py:296
  126.0 9.2 %shard_map.80 = (f32[256,1024]{1,0:T(8,128)}, bf16[256,1024]{1,0:T(8,128)(2,1)}) custom-call(s32[1]{0:T(128)} %constant.49.clone.1.which_ref, bf16[128,4096]{1,0:T(8,128)(2,1)} %get-tuple-element.34.refs_1_.refs_0_, bf16[128,4096]{1,0:T(8,128)(2,1)} %copy-done, bf16[128,4096]{1,0:T(8,128)(2,1)} %collective-permute-done.7.refs_2_.refs_5_, ...), custom_call_target="tpu_custom_call" | custom-call | flops 1100000000 | bytes 1 | tf_op jit(solution)/shard_map/pallas_call | solution.py:149
  135.2 2.9 %collective-permute-done.8.refs_0_ = bf16[128,4096]{1,0:T(8,128)(2,1)} collective-permute-done((bf16[128,4096]{1,0:T(8,128)(2,1)S(1)}, bf16[128,4096]{1,0:T(8,128)(2,1)}, u32[]{:S(2)}, u32[]{:S(2)}) %collective-permute-start.8) | collective-permute-done | bytes 1048608 | tf_op jit(solution)/shard_map/ppermute | solution.py:268
  139.2 2.5 %collective-permute-done.13.refs_3_.refs_6_ = bf16[128,4096]{1,0:T(8,128)(2,1)S(1)} collective-permute-done((bf16[128,4096]{1,0:T(8,128)(2,1)}, bf16[128,4096]{1,0:T(8,128)(2,1)S(1)}, u32[]{:S(2)}, u32[]{:S(2)}) %collective-permute-start.13) | collective-permute-done | bytes 1048608 | tf_op jit(solution)/shard_map/ppermute | solution.py:268
  143.4 9.2 %shard_map.83 = (f32[256,1024]{1,0:T(8,128)}, bf16[256,1024]{1,0:T(8,128)(2,1)}) custom-call(s32[1]{0:T(128)} %constant.49.clone.1.which_ref, bf16[128,4096]{1,0:T(8,128)(2,1)} %get-tuple-element.33.refs_2_.refs_0_, bf16[128,4096]{1,0:T(8,128)(2,1)} %collective-permute-done.1.refs_1_.refs_2_, bf16[128,4096]{1,0:T(8,128)(2,1)} %copy-done.6, ...), custom_call_target="tpu_custom_call" | custom-call | flops 1100000000 | bytes 1 | tf_op jit(solution)/shard_map/pallas_call | solution.py:149
  153.6 9.9 %shard_map.85 = (f32[512,512]{1,0:T(8,128)}, bf16[512,512]{1,0:T(8,128)(2,1)}) custom-call(s32[1]{0:T(128)} %bitcast.8.which_ref, bf16[128,4096]{1,0:T(8,128)(2,1)} %get-tuple-element.33.refs_2_.refs_0_, bf16[128,4096]{1,0:T(8,128)(2,1)} %get-tuple-element.34.refs_1_.refs_0_, bf16[128,4096]{1,0:T(8,128)(2,1)} %collective-permute-done.1.refs_1_.refs_2_, ...), custom_call_target="tpu_custom_call" | custom-call | flops 1100000000 | bytes 1 | tf_op jit(solution)/shard_map/pallas_call | solution.py:149
  169.2 4.5 %collective-permute-done.18.refs_1_.refs_4_ = bf16[128,1024]{1,0:T(8,128)(2,1)S(1)} collective-permute-done((bf16[128,1024]{1,0:T(8,128)(2,1)S(1)}, bf16[128,1024]{1,0:T(8,128)(2,1)S(1)}, u32[]{:S(2)}, u32[]{:S(2)}) %collective-permute-start.18) | collective-permute-done | bytes 262176 | tf_op jit(solution)/shard_map/ppermute | solution.py:268
  173.7 3.0 %collective-permute-done.16.refs_0_ = bf16[4096,256]{1,0:T(8,128)(2,1)} collective-permute-done((bf16[4096,256]{1,0:T(8,128)(2,1)}, bf16[4096,256]{1,0:T(8,128)(2,1)}, u32[]{:S(2)}, u32[]{:S(2)}) %collective-permute-start.16) | collective-permute-done | bytes 2097184 | tf_op jit(solution)/shard_map/ppermute | solution.py:296
  181.4 5.6 %shard_map.88 = (f32[512,256]{1,0:T(8,128)S(1)}, bf16[512,256]{1,0:T(8,128)(2,1)S(1)}) custom-call(s32[1]{0:T(128)} %bitcast.8.which_ref, bf16[128,4096]{1,0:T(8,128)(2,1)S(1)} %copy-done.3, bf16[128,4096]{1,0:T(8,128)(2,1)S(1)} %copy-done.5, bf16[128,4096]{1,0:T(8,128)(2,1)} %collective-permute-done.1.refs_1_.refs_2_, bf16[128,4096]{1,0:T(8,128)(2,1)S(1)} %copy-done.1, ...), custom_call_target="tpu_custom_call" | custom-call | flops 1100000000 | bytes 1 | tf_op jit(solution)/shard_map/pallas_call | solution.py:149
  190.3 5.2 %shard_map.90 = (f32[512,256]{1,0:T(8,128)S(1)}, bf16[512,256]{1,0:T(8,128)(2,1)S(1)}) custom-call(s32[1]{0:T(128)} %bitcast.8.which_ref, bf16[128,4096]{1,0:T(8,128)(2,1)S(1)} %copy-done.3, bf16[128,4096]{1,0:T(8,128)(2,1)S(1)} %copy-done.5, bf16[128,4096]{1,0:T(8,128)(2,1)} %collective-permute-done.1.refs_1_.refs_2_, bf16[128,4096]{1,0:T(8,128)(2,1)S(1)} %copy-done.1, ...), custom_call_target="tpu_custom_call" | custom-call | flops 1100000000 | bytes 1 | tf_op jit(solution)/shard_map/pallas_call | solution.py:149
  196.7 4.5 %collective-permute-done.28.refs_0_.refs_3_ = bf16[256,256]{1,0:T(8,128)(2,1)S(1)} collective-permute-done((bf16[256,256]{1,0:T(8,128)(2,1)S(1)}, bf16[256,256]{1,0:T(8,128)(2,1)S(1)}, u32[]{:S(2)}, u32[]{:S(2)}) %collective-permute-start.28) | collective-permute-done | bytes 131104 | tf_op jit(solution)/shard_map/ppermute | solution.py:268
  203.5 2.6 %shard_map.93.refs_5_ = bf16[256,4096]{1,0:T(8,128)(2,1)} custom-call(s32[8]{0:T(128)S(1)} %copy-done.18, bf16[256,4096]{1,0:T(8,128)(2,1)S(1)} %copy-done.12, bf16[128,1024]{1,0:T(8,128)(2,1)S(1)} %get-tuple-element.47.refs_2_.refs_1_, bf16[128,1024]{1,0:T(8,128)(2,1)S(1)} %get-tuple-element.59.refs_2_, ...), custom_call_target="tpu_custom_call" | custom-call | flops 1100000000 | bytes 1 | tf_op jit(solution)/shard_map/pallas_call | solution.py:224
  (114 shorter events, 51.2 us)
Async XLA Ops:
  4.1 9.7 %collective-permute-start = (bf16[128,4096]{1,0:T(8,128)(2,1)}, bf16[128,4096]{1,0:T(8,128)(2,1)S(1)}, u32[]{:S(2)}, u32[]{:S(2)}) collective-permute-start(bf16[128,4096]{1,0:T(8,128)(2,1)} %get-tuple-element.62), channel_id=1, source_target_pairs={{0,1},{1,2},{2,3},{3,4},{4,5},{5,6},{6,7},{7,8},{8,9},{9,10},{10,1... | collective-permute-start | bytes 3145736 | tf_op jit(solution)/shard_map/ppermute | solution.py:292
  6.7 35.0 %collective-permute-start.3 = (bf16[144,4096]{1,0:T(8,128)(2,1)S(1)}, bf16[144,4096]{1,0:T(8,128)(2,1)S(1)}, u32[]{:S(2)}, u32[]{:S(2)}) collective-permute-start(bf16[144,4096]{1,0:T(8,128)(2,1)S(1)} %pad.4), channel_id=1, source_target_pairs={{0,0},{1,3},{2,2},{3,5},{4,4},{5,7},{6,6},{7,9},{8,8},{9,11},{10,1... | collective-permute-start | bytes 3538952 | tf_op jit(solution)/shard_map/ppermute | solution.py:293
  14.8 31.0 %collective-permute-start.5 = (bf16[4096,256]{1,0:T(8,128)(2,1)}, bf16[4096,256]{1,0:T(8,128)(2,1)}, u32[]{:S(2)}, u32[]{:S(2)}) collective-permute-start(bf16[4096,256]{1,0:T(8,128)(2,1)} %shard_map.75.refs_4_), channel_id=1, source_target_pairs={{0,1},{1,0},{2,3},{3,2},{4,5},{5,4},{6,7},{7,6},{8,9},{9,8},{10,11... | collective-permute-start | bytes 6291464 | tf_op jit(solution)/shard_map/ppermute | solution.py:268
  22.1 49.9 %collective-permute-start.10 = (bf16[4096,256]{1,0:T(8,128)(2,1)}, bf16[4096,256]{1,0:T(8,128)(2,1)}, u32[]{:S(2)}, u32[]{:S(2)}) collective-permute-start(bf16[4096,256]{1,0:T(8,128)(2,1)} %shard_map.75.refs_4_), channel_id=1, source_target_pairs={{0,4},{1,5},{2,6},{3,7},{4,0},{5,1},{6,2},{7,3},{8,12},{9,13},{10,... | collective-permute-start | bytes 6291464 | tf_op jit(solution)/shard_map/ppermute | solution.py:296
  25.4 46.6 %collective-permute-start.11 = (bf16[4096,256]{1,0:T(8,128)(2,1)}, bf16[4096,256]{1,0:T(8,128)(2,1)}, u32[]{:S(2)}, u32[]{:S(2)}) collective-permute-start(bf16[4096,256]{1,0:T(8,128)(2,1)} %shard_map.75.refs_4_), channel_id=1, source_target_pairs={{4,8},{5,9},{6,10},{7,11},{8,4},{9,5},{10,6},{11,7},{20,24},{21,25... | collective-permute-start | bytes 6291464 | tf_op jit(solution)/shard_map/ppermute | solution.py:296
  44.0 26.0 %collective-permute-start.2 = (bf16[128,4096]{1,0:T(8,128)(2,1)S(1)}, bf16[128,4096]{1,0:T(8,128)(2,1)S(1)}, u32[]{:S(2)}, u32[]{:S(2)}) collective-permute-start(bf16[128,4096]{1,0:T(8,128)(2,1)S(1)} %copy-done.4), channel_id=1, source_target_pairs={{0,2},{1,3},{2,0},{3,1},{4,6},{5,7},{6,4},{7,5},{8,10},{9,11},{10,... | collective-permute-start | bytes 3145736 | tf_op jit(solution)/shard_map/ppermute | solution.py:268
  61.2 25.5 %collective-permute-start.7 = (bf16[128,4096]{1,0:T(8,128)(2,1)}, bf16[128,4096]{1,0:T(8,128)(2,1)}, u32[]{:S(2)}, u32[]{:S(2)}) collective-permute-start(bf16[128,4096]{1,0:T(8,128)(2,1)} %get-tuple-element.36.refs_2_), channel_id=1, source_target_pairs={{0,16},{1,17},{2,18},{3,19},{4,20},{5,21},{6,22},{7,23},{8,24},{9,... | collective-permute-start | bytes 3145736 | tf_op jit(solution)/shard_map/ppermute | solution.py:268
  62.6 29.2 %collective-permute-start.1 = (bf16[128,4096]{1,0:T(8,128)(2,1)S(1)}, bf16[128,4096]{1,0:T(8,128)(2,1)}, u32[]{:S(2)}, u32[]{:S(2)}) collective-permute-start(bf16[128,4096]{1,0:T(8,128)(2,1)S(1)} %copy-done.2), channel_id=1, source_target_pairs={{0,2},{1,3},{2,0},{3,1},{4,6},{5,7},{6,4},{7,5},{8,10},{9,11},{10,... | collective-permute-start | bytes 3145736 | tf_op jit(solution)/shard_map/ppermute | solution.py:268
  72.0 51.9 %collective-permute-start.14 = (bf16[4096,256]{1,0:T(8,128)(2,1)}, bf16[4096,256]{1,0:T(8,128)(2,1)}, u32[]{:S(2)}, u32[]{:S(2)}) collective-permute-start(bf16[4096,256]{1,0:T(8,128)(2,1)} %get-tuple-element.39.refs_9_), channel_id=1, source_target_pairs={{4,0},{5,1},{6,2},{7,3},{8,12},{9,13},{10,14},{11,15},{20,16},{21,... | collective-permute-start | bytes 6291464 | tf_op jit(solution)/shard_map/ppermute | solution.py:296
  73.3 50.6 %collective-permute-start.15 = (bf16[4096,256]{1,0:T(8,128)(2,1)}, bf16[4096,256]{1,0:T(8,128)(2,1)}, u32[]{:S(2)}, u32[]{:S(2)}) collective-permute-start(bf16[4096,256]{1,0:T(8,128)(2,1)} %get-tuple-element.37.refs_6_), channel_id=1, source_target_pairs={{4,8},{5,9},{6,10},{7,11},{8,4},{9,5},{10,6},{11,7},{20,24},{21,25... | collective-permute-start | bytes 6291464 | tf_op jit(solution)/shard_map/ppermute | solution.py:296
  75.3 50.2 %collective-permute-start.12 = (bf16[4096,256]{1,0:T(8,128)(2,1)}, bf16[4096,256]{1,0:T(8,128)(2,1)}, u32[]{:S(2)}, u32[]{:S(2)}) collective-permute-start(bf16[4096,256]{1,0:T(8,128)(2,1)} %get-tuple-element.37.refs_6_), channel_id=1, source_target_pairs={{0,1},{1,0},{2,3},{3,2},{4,5},{5,4},{6,7},{7,6},{8,9},{9,8},{10,11... | collective-permute-start | bytes 6291464 | tf_op jit(solution)/shard_map/ppermute | solution.py:268
  86.7 24.6 %collective-permute-start.6 = (bf16[128,4096]{1,0:T(8,128)(2,1)}, bf16[128,4096]{1,0:T(8,128)(2,1)S(1)}, u32[]{:S(2)}, u32[]{:S(2)}) collective-permute-start(bf16[128,4096]{1,0:T(8,128)(2,1)} %shard_map.77), channel_id=1, source_target_pairs={{0,16},{1,17},{2,18},{3,19},{4,20},{5,21},{6,22},{7,23},{8,24},{9,... | collective-permute-start | bytes 3145736 | tf_op jit(solution)/shard_map/ppermute | solution.py:268
  91.8 26.3 %collective-permute-start.9 = (bf16[128,4096]{1,0:T(8,128)(2,1)}, bf16[128,4096]{1,0:T(8,128)(2,1)S(1)}, u32[]{:S(2)}, u32[]{:S(2)}) collective-permute-start(bf16[128,4096]{1,0:T(8,128)(2,1)} %shard_map.78), channel_id=1, source_target_pairs={{0,2},{1,3},{2,0},{3,1},{4,6},{5,7},{6,4},{7,5},{8,10},{9,11},{10,... | collective-permute-start | bytes 3145736 | tf_op jit(solution)/shard_map/ppermute | solution.py:268
  111.4 26.7 %collective-permute-start.8 = (bf16[128,4096]{1,0:T(8,128)(2,1)S(1)}, bf16[128,4096]{1,0:T(8,128)(2,1)}, u32[]{:S(2)}, u32[]{:S(2)}) collective-permute-start(bf16[128,4096]{1,0:T(8,128)(2,1)S(1)} %collective-permute-done.6.refs_3_.refs_2_.refs_4_), channel_id=1, source_target_pairs={{0,3},{1,2},{2,1},{3,0},{4,7},{5,6},{6,5},{7,4},{8,11},{9,10},{10,... | collective-permute-start | bytes 3145736 | tf_op jit(solution)/shard_map/ppermute | solution.py:268
  118.1 34.5 %collective-permute-start.21 = (bf16[4096,256]{1,0:T(8,128)(2,1)}, bf16[4096,256]{1,0:T(8,128)(2,1)}, u32[]{:S(2)}, u32[]{:S(2)}) collective-permute-start(bf16[4096,256]{1,0:T(8,128)(2,1)} %get-tuple-element.39.refs_9_), channel_id=1, source_target_pairs={{0,1},{1,0},{2,3},{3,2},{4,5},{5,4},{6,7},{7,6},{8,9},{9,8},{10,11... | collective-permute-start | bytes 6291464 | tf_op jit(solution)/shard_map/ppermute | solution.py:268
  123.9 29.8 %collective-permute-start.20 = (bf16[4096,256]{1,0:T(8,128)(2,1)}, bf16[4096,256]{1,0:T(8,128)(2,1)}, u32[]{:S(2)}, u32[]{:S(2)}) collective-permute-start(bf16[4096,256]{1,0:T(8,128)(2,1)} %get-tuple-element.45.refs_8_), channel_id=1, source_target_pairs={{0,1},{1,0},{2,3},{3,2},{4,5},{5,4},{6,7},{7,6},{8,9},{9,8},{10,11... | collective-permute-start | bytes 6291464 | tf_op jit(solution)/shard_map/ppermute | solution.py:268
  124.0 52.7 %collective-permute-start.16 = (bf16[4096,256]{1,0:T(8,128)(2,1)}, bf16[4096,256]{1,0:T(8,128)(2,1)}, u32[]{:S(2)}, u32[]{:S(2)}) collective-permute-start(bf16[4096,256]{1,0:T(8,128)(2,1)} %get-tuple-element.40.refs_9_), channel_id=1, source_target_pairs={{4,0},{5,1},{6,2},{7,3},{8,12},{9,13},{10,14},{11,15},{20,16},{21,... | collective-permute-start | bytes 6291464 | tf_op jit(solution)/shard_map/ppermute | solution.py:296
  125.4 51.2 %collective-permute-start.23 = (bf16[4096,256]{1,0:T(8,128)(2,1)}, bf16[4096,256]{1,0:T(8,128)(2,1)S(1)}, u32[]{:S(2)}, u32[]{:S(2)}) collective-permute-start(bf16[4096,256]{1,0:T(8,128)(2,1)} %get-tuple-element.40.refs_9_), channel_id=1, source_target_pairs={{0,1},{1,0},{2,3},{3,2},{4,5},{5,4},{6,7},{7,6},{8,9},{9,8},{10,11... | collective-permute-start | bytes 6291464 | tf_op jit(solution)/shard_map/ppermute | solution.py:268
  141.7 23.0 %collective-permute-start.17 = (bf16[256,1024]{1,0:T(8,128)(2,1)}, bf16[256,1024]{1,0:T(8,128)(2,1)}, u32[]{:S(2)}, u32[]{:S(2)}) collective-permute-start(bf16[256,1024]{1,0:T(8,128)(2,1)} %get-tuple-element.38.refs_1_.refs_8_), channel_id=1, source_target_pairs={{0,16},{1,17},{2,18},{3,19},{4,20},{5,21},{6,22},{7,23},{8,24},{9,... | collective-permute-start | bytes 1572872 | tf_op jit(solution)/shard_map/ppermute | solution.py:268
  152.6 15.4 %collective-permute-start.19 = (bf16[256,1024]{1,0:T(8,128)(2,1)}, bf16[256,1024]{1,0:T(8,128)(2,1)}, u32[]{:S(2)}, u32[]{:S(2)}) collective-permute-start(bf16[256,1024]{1,0:T(8,128)(2,1)} %get-tuple-element.42.refs_0_.refs_12_), channel_id=1, source_target_pairs={{0,16},{1,17},{2,18},{3,19},{4,20},{5,21},{6,22},{7,23},{8,24},{9,... | collective-permute-start | bytes 1572872 | tf_op jit(solution)/shard_map/ppermute | solution.py:268
  163.6 15.0 %collective-permute-start.22 = (bf16[512,512]{1,0:T(8,128)(2,1)}, bf16[512,512]{1,0:T(8,128)(2,1)S(1)}, u32[]{:S(2)}, u32[]{:S(2)}) collective-permute-start(bf16[512,512]{1,0:T(8,128)(2,1)} %get-tuple-element.46.refs_0_), channel_id=1, source_target_pairs={{0,16},{1,17},{2,18},{3,19},{4,20},{5,21},{6,22},{7,23},{8,24},{9,... | collective-permute-start | bytes 1572872 | tf_op jit(solution)/shard_map/ppermute | solution.py:268
  178.6 11.7 %collective-permute-start.25 = (bf16[4096,256]{1,0:T(8,128)(2,1)}, bf16[4096,256]{1,0:T(8,128)(2,1)S(1)}, u32[]{:S(2)}, u32[]{:S(2)}) collective-permute-start(bf16[4096,256]{1,0:T(8,128)(2,1)} %shard_map.87.refs_8_), channel_id=1, source_target_pairs={{0,1},{1,0},{2,3},{3,2},{4,5},{5,4},{6,7},{7,6},{8,9},{9,8},{10,11... | collective-permute-start | bytes 6291464 | tf_op jit(solution)/shard_map/ppermute | solution.py:268
  178.7 11.6 %collective-permute-start.26 = (bf16[128,1024]{1,0:T(8,128)(2,1)S(1)}, bf16[128,1024]{1,0:T(8,128)(2,1)S(1)}, u32[]{:S(2)}, u32[]{:S(2)}) collective-permute-start(bf16[128,1024]{1,0:T(8,128)(2,1)S(1)} %get-tuple-element.51), channel_id=1, source_target_pairs={{0,2},{1,3},{2,0},{3,1},{4,6},{5,7},{6,4},{7,5},{8,10},{9,11},{10,... | collective-permute-start | bytes 786440 | tf_op jit(solution)/shard_map/ppermute | solution.py:268
  187.0 9.1 %collective-permute-start.24 = (bf16[512,256]{1,0:T(8,128)(2,1)S(1)}, bf16[512,256]{1,0:T(8,128)(2,1)S(1)}, u32[]{:S(2)}, u32[]{:S(2)}) collective-permute-start(bf16[512,256]{1,0:T(8,128)(2,1)S(1)} %get-tuple-element.49.refs_10_), channel_id=1, source_target_pairs={{0,16},{1,17},{2,18},{3,19},{4,20},{5,21},{6,22},{7,23},{8,24},{9,... | collective-permute-start | bytes 786440 | tf_op jit(solution)/shard_map/ppermute | solution.py:268
  (30 other events, 170.9 us)
